TPU v7x, 32 devices: a whole 2x2x4 slice. The times are simulated.
32 devices in a mesh: tor: 2 (over x), pol: 16 (over z, y, core).
Axes of the slice: x: 2, y: 2, z: 4, core: 2. Of those that a mesh axis runs over, the one named last changes fastest.
Arguments:
- plasma_state: float32 [6, 2, 128, 256], P(None, 'tor', 'pol'), may hold values from -3 to 3
- right_side: float32 [6, 2, 128, 256], P(None, 'tor', 'pol'), may hold values from -12 to 12
- resistivity: float32 [2, 128, 256], P('tor', 'pol'), may hold values from 0.05 to 0.6
- jacobi_blocks: float32 [6, 6, 2, 128, 256], P(None, None, 'tor', 'pol'), may hold values from -0.6 to 1.6, as said below
Outputs:
- update: float32 [6, 2, 128, 256], P(None, 'tor', 'pol')
- estimates: float32 [3], replicated
Inputs may be any that keep to these rules, and one draw needn't show every extreme that they name: `jacobi_blocks`: each block's diagonal entries lie in 0.4 to 1.6.
All inputs are finite; a program needn't handle non-finite values.
Results may differ from a plain program's by a relative error of at most 0.006.
Values may be sent and summed in bfloat16 or wider, within the bound.
No kernel may reach another device: no remote copies, remote signals or barrier semaphores. Data moves between devices by JAX's collectives and lax.ppermute only.
A program may use at most 64 MiB of HBM per device.

v0:
```python
import jax
import jax.numpy as jnp
from jax import lax
from jax.sharding import PartitionSpec as P

ITERS = 3


inverse_step = 1.0
viscosity = 0.2
epsilon = 1e-06


def padded_2(cells, sides, width, closed):
    for axis, dim in sides:
        count = lax.axis_size(axis)
        ends = count if closed else count - 1
        head = lax.slice_in_dim(cells, 0, width, axis=dim)
        tail = lax.slice_in_dim(cells, cells.shape[dim] - width, cells.shape[dim], axis=dim)
        cells = jnp.concatenate(
            [
                lax.ppermute(tail, axis, [(i, (i + 1) % count) for i in range(ends)]),
                cells,
                lax.ppermute(head, axis, [((i + 1) % count, i) for i in range(ends)]),
            ],
            axis=dim,
        )
    return cells


def neighbour(values, array_axis, offset):
    length = values.shape[array_axis]
    widths = [(0, 0)] * values.ndim
    widths[array_axis] = (1, 1)
    padded = jnp.pad(values, widths)
    return lax.slice_in_dim(padded, 1 + offset, 1 + offset + length, axis=array_axis)


def linear_flux(plasma, tangent, direction):
    magnetic = plasma[0:3]
    velocity = plasma[3:6]
    tang_mag = tangent[0:3]
    tang_vel = tangent[3:6]
    pressure = jnp.sum(magnetic * tang_mag, axis=0)
    components = []
    for inner_index in range(3):
        components.append(
            tang_vel[direction] * magnetic[inner_index]
            + velocity[direction] * tang_mag[inner_index]
            - tang_mag[direction] * velocity[inner_index]
            - magnetic[direction] * tang_vel[inner_index]
        )
    for inner_index in range(3):
        moment = (
            tang_vel[direction] * velocity[inner_index]
            + velocity[direction] * tang_vel[inner_index]
            - tang_mag[direction] * magnetic[inner_index]
            - magnetic[direction] * tang_mag[inner_index]
        )
        if inner_index == direction:
            moment = moment + pressure
        components.append(moment)
    return jnp.stack(components)


def diffusion_field(resistivity):
    shape = (3,) + resistivity.shape
    return jnp.concatenate(
        [jnp.broadcast_to(resistivity[None], shape), jnp.full(shape, viscosity, jnp.float32)]
    )


def jacobian_product(
    plasma, tangent, plasma_planes, tangent_planes, plasma_rows, tangent_rows, diffusion
):
    result_sum = inverse_step * tangent
    flux_planes = linear_flux(plasma_planes, tangent_planes, 0)
    result_sum = result_sum + 0.5 * (flux_planes[:, 2:] - flux_planes[:, :-2])
    laplace_sum = tangent_planes[:, 2:] + tangent_planes[:, :-2] - 2.0 * tangent
    flux_rows = linear_flux(plasma_rows, tangent_rows, 1)
    result_sum = result_sum + 0.5 * (flux_rows[:, :, 2:] - flux_rows[:, :, :-2])
    laplace_sum = laplace_sum + tangent_rows[:, :, 2:] + tangent_rows[:, :, :-2] - 2.0 * tangent
    flux_depth = linear_flux(plasma, tangent, 2)
    result_sum = result_sum + 0.5 * (neighbour(flux_depth, 3, 1) - neighbour(flux_depth, 3, -1))
    laplace_sum = laplace_sum + neighbour(tangent, 3, 1) + neighbour(tangent, 3, -1) - 2.0 * tangent
    return result_sum - diffusion * laplace_sum


def precondition(blocks, vector):
    widened = vector.astype(jnp.float32)
    total = blocks[:, 0] * widened[0]
    for column in range(1, 6):
        total = total + blocks[:, column] * widened[column]
    return total


def least_squares(columns, initial_norm):
    count = len(columns)
    rhs_list = [initial_norm] + [jnp.float32(0.0)] * count
    cosines = []
    sines = []
    triangle = []
    estimate_list = []
    for column in range(count):
        entries = list(columns[column])
        for inner_index in range(column):
            first_value = entries[inner_index]
            second_value = entries[inner_index + 1]
            entries[inner_index] = (
                cosines[inner_index] * first_value + sines[inner_index] * second_value
            )
            entries[inner_index + 1] = (
                -sines[inner_index] * first_value + cosines[inner_index] * second_value
            )
        first_value = entries[column]
        second_value = entries[column + 1]
        radius = jnp.sqrt(first_value * first_value + second_value * second_value)
        cosine = first_value / radius
        sine_value = second_value / radius
        cosines.append(cosine)
        sines.append(sine_value)
        entries[column] = radius
        triangle.append(entries[: column + 1])
        previous = rhs_list[column]
        rhs_list[column] = cosine * previous
        rhs_list[column + 1] = -sine_value * previous
        estimate_list.append(jnp.abs(rhs_list[column + 1]))
    weights = [jnp.float32(0.0)] * count
    for column in reversed(range(count)):
        partial_value = rhs_list[column]
        for later in range(column + 1, count):
            partial_value = partial_value - triangle[later][column] * weights[later]
        weights[column] = partial_value / triangle[column][column]
    return (weights, estimate_list)


def shards(plasma_state, right_side, resistivity, jacobi_blocks):
    cell_count = (
        6
        * plasma_state.shape[1]
        * plasma_state.shape[2]
        * plasma_state.shape[3]
        * lax.axis_size("tor")
        * lax.axis_size("pol")
    )
    diffusion = diffusion_field(resistivity)
    plasma_planes = padded_2(plasma_state.astype(jnp.bfloat16), (("tor", 1),), 1, True).astype(
        plasma_state.dtype
    )
    plasma_rows = padded_2(plasma_state, (("pol", 2),), 1, False)
    square_sum = lax.psum(jnp.sum(right_side * right_side), ("tor", "pol"))
    initial_norm = jnp.sqrt(square_sum + epsilon)
    krylov_basis = [(right_side / initial_norm).astype(jnp.bfloat16)]
    directions = []
    columns = []
    for column in range(ITERS):
        vector = krylov_basis[column]
        tangent = precondition(jacobi_blocks, vector)
        tangent_planes = padded_2(tangent.astype(jnp.bfloat16), (("tor", 1),), 1, True).astype(
            tangent.dtype
        )
        tangent_rows = padded_2(tangent, (("pol", 2),), 1, False)
        image = jacobian_product(
            plasma_state,
            tangent,
            plasma_planes,
            tangent_planes,
            plasma_rows,
            tangent_rows,
            diffusion,
        )
        directions.append(tangent)
        local_products = jnp.stack(
            [jnp.sum(image * earlier.astype(jnp.float32)) for earlier in krylov_basis]
        )
        products = lax.psum(local_products, ("tor", "pol"))
        coefficients = [products[inner_index] for inner_index in range(column + 1)]
        remainder = image
        for inner_index in range(column + 1):
            remainder = remainder - coefficients[inner_index] * krylov_basis[inner_index].astype(
                jnp.float32
            )
        remainder_square = lax.psum(jnp.sum(remainder * remainder), ("tor", "pol"))
        new_norm = jnp.sqrt(remainder_square + epsilon)
        columns.append(coefficients + [new_norm])
        if column + 1 < ITERS:
            krylov_basis.append((remainder / new_norm).astype(jnp.bfloat16))
    weights, estimate_list = least_squares(columns, initial_norm)
    update = weights[0] * directions[0]
    for column in range(1, ITERS):
        update = update + weights[column] * directions[column]
    estimates = jnp.stack(estimate_list) / jnp.sqrt(jnp.float32(cell_count))
    return (update, estimates)


def solution(mesh):
    return jax.shard_map(
        shards,
        mesh=mesh,
        in_specs=(
            P(None, "tor", "pol", None),
            P(None, "tor", "pol", None),
            P("tor", "pol", None),
            P(None, None, "tor", "pol", None),
        ),
        out_specs=(P(None, "tor", "pol", None), P()),
        check_vma=False,
    )
```

profile of v0, /device:TPU:0, one launch (start us, length us, event | category | flops | bytes accessed | tf_op | source)
XLA Modules:
  0.0 352.0 jit_solution(11250309698395564013)
XLA Ops:
  0.6 1.5 multiply_reduce_fusion.5
  2.1 42.2 %psum.49 = f32[]{:T(128)} all-reduce(f32[]{:T(128)} %multiply_reduce_fusion.5), channel_id=1, replica_groups=mesh['tor'=2,'pol'=16] {'tor','pol'}, use_global_device_ids=true, to_apply=%region_1.0 | all-reduce | flops 1 | bytes 8 | tf_op jit(solution)/shard_map/psum | solution.py:151
  45.1 1.0 fusion.104
  46.0 2.3 collective-permute-start
  48.4 2.0 collective-permute-start.2
  50.5 1.3 collective-permute-start.4
  51.8 1.3 collective-permute-start.5
  53.2 4.0 %collective-permute-start.6 = (f32[6,1,1,256]{3,2,1,0:T(1,128)S(1)}, f32[6,1,1,256]{3,2,1,0:T(1,128)S(1)}, u32[]{:S(2)}, u32[]{:S(2)}) collective-permute-start(f32[6,1,1,256]{3,2,1,0:T(1,128)S(1)} %get-tuple-element.37), channel_id=1, source_target_pairs={{0,1},{1,2},{2,3},{3,4},{4,5},{5,6},{6,7},{7,8},{8,9},{9,10},{10,1... | collective-permute-start | bytes 18440 | tf_op jit(solution)/shard_map/ppermute | solution.py:22
  57.2 1.3 collective-permute-start.7
  58.6 1.6 collective-permute-start.3
  60.1 1.4 collective-permute-done.7
  64.0 44.5 %psum.50 = f32[]{:T(128)} all-reduce(f32[]{:T(128)} %get-tuple-element.15), channel_id=1, replica_groups=mesh['tor'=2,'pol'=16] {'tor','pol'}, use_global_device_ids=true, to_apply=%region_6.7 | all-reduce | flops 1 | bytes 8 | tf_op jit(solution)/shard_map/psum | solution.py:176
  108.5 1.3 multiply_reduce_fusion.4
  109.7 39.0 %psum.51 = f32[]{:T(128)} all-reduce(f32[]{:T(128)} %multiply_reduce_fusion.4), channel_id=1, replica_groups=mesh['tor'=2,'pol'=16] {'tor','pol'}, use_global_device_ids=true, to_apply=%region_8.9 | all-reduce | flops 1 | bytes 8 | tf_op jit(solution)/shard_map/psum | solution.py:183
  150.2 2.3 collective-permute-start.8
  152.7 1.3 collective-permute-start.10
  154.0 1.3 collective-permute-start.11
  157.4 2.0 collective-permute-done.11
  160.5 1.4 pad_maximum_fusion.10
  161.9 42.2 %psum.52 = f32[2]{0:T(128)S(1)} all-reduce(f32[2]{0:T(128)S(1)} %pad_maximum_fusion.10), channel_id=1, replica_groups=mesh['tor'=2,'pol'=16] {'tor','pol'}, use_global_device_ids=true, to_apply=%region_14.15 | all-reduce | flops 2 | bytes 16 | tf_op jit(solution)/shard_map/psum | solution.py:176
  204.6 1.9 multiply_reduce_fusion.2
  206.5 39.7 %psum.53 = f32[]{:T(128)} all-reduce(f32[]{:T(128)} %multiply_reduce_fusion.2), channel_id=1, replica_groups=mesh['tor'=2,'pol'=16] {'tor','pol'}, use_global_device_ids=true, to_apply=%region_16.17 | all-reduce | flops 1 | bytes 8 | tf_op jit(solution)/shard_map/psum | solution.py:183
  246.8 1.3 fusion.80
  248.2 2.3 collective-permute-start.12
  250.6 1.3 collective-permute-start.14
  251.9 1.3 collective-permute-start.15
  256.0 1.3 collective-permute-done.15
  257.7 0.8 fusion.8
  258.5 2.0 pad_maximum_fusion.11
  260.5 42.0 %psum.54 = f32[3]{0:T(128)S(1)} all-reduce(f32[3]{0:T(128)S(1)} %pad_maximum_fusion.11), channel_id=1, replica_groups=mesh['tor'=2,'pol'=16] {'tor','pol'}, use_global_device_ids=true, to_apply=%region_23.24 | all-reduce | flops 3 | bytes 24 | tf_op jit(solution)/shard_map/psum | solution.py:176
  305.6 2.6 fusion.13
  308.9 40.3 %psum.55 = f32[]{:T(128)} all-reduce(f32[]{:T(128)} %fusion.13), channel_id=1, replica_groups=mesh['tor'=2,'pol'=16] {'tor','pol'}, use_global_device_ids=true, to_apply=%region_25.26 | all-reduce | flops 1 | bytes 8 | tf_op jit(solution)/shard_map/psum | solution.py:183
  (114 shorter events, 7.3 us)
Async XLA Ops:
  0.6 44.4 %copy-start.2 = (f32[6,1,8,256]{3,2,1,0:T(8,128)S(1)}, f32[6,1,8,256]{3,2,1,0:T(8,128)}, u32[]{:S(2)}) copy-start(f32[6,1,8,256]{3,2,1,0:T(8,128)} %param.5) | copy-start | bytes 147460
  45.0 3.4 copy-start
  46.0 15.7 %collective-permute-start = (bf16[6,1,8,256]{3,2,1,0:T(8,128)(2,1)S(1)}, bf16[6,1,8,256]{3,2,1,0:T(8,128)(2,1)S(1)}, u32[]{:S(2)}, u32[]{:S(2)}) collective-permute-start(bf16[6,1,8,256]{3,2,1,0:T(8,128)(2,1)S(1)} %get-tuple-element.17), channel_id=1, source_target_pairs={{0,16},{16,0},{1,17},{17,1},{2,18},{18,2},{3,19},{19,3},{4,20},{20... | collective-permute-start | bytes 73736 | tf_op jit(solution)/shard_map/ppermute | solution.py:22
  48.4 13.3 %collective-permute-start.1 = (bf16[6,1,8,256]{3,2,1,0:T(8,128)(2,1)S(1)}, bf16[6,1,8,256]{3,2,1,0:T(8,128)(2,1)S(1)}, u32[]{:S(2)}, u32[]{:S(2)}) collective-permute-start(bf16[6,1,8,256]{3,2,1,0:T(8,128)(2,1)S(1)} %get-tuple-element.17), channel_id=1, source_target_pairs={{16,0},{0,16},{17,1},{1,17},{18,2},{2,18},{19,3},{3,19},{20,4},{4,... | collective-permute-start | bytes 73736 | tf_op jit(solution)/shard_map/ppermute | solution.py:24
  48.4 13.3 %collective-permute-start.2 = (bf16[6,1,8,256]{3,2,1,0:T(8,128)(2,1)S(1)}, bf16[6,1,8,256]{3,2,1,0:T(8,128)(2,1)S(1)}, u32[]{:S(2)}, u32[]{:S(2)}) collective-permute-start(bf16[6,1,8,256]{3,2,1,0:T(8,128)(2,1)S(1)} %convert_element_type.95), channel_id=1, source_target_pairs={{0,16},{16,0},{1,17},{17,1},{2,18},{18,2},{3,19},{19,3},{4,20},{20... | collective-permute-start | bytes 73736 | tf_op jit(solution)/shard_map/ppermute | solution.py:22
  50.5 2.7 collective-permute-start.4
  51.8 5.4 %collective-permute-start.5 = (f32[6,1,1,256]{3,2,1,0:T(1,128)S(1)}, f32[6,1,1,256]{3,2,1,0:T(1,128)S(1)}, u32[]{:S(2)}, u32[]{:S(2)}) collective-permute-start(f32[6,1,1,256]{3,2,1,0:T(1,128)S(1)} %get-tuple-element.39), channel_id=1, source_target_pairs={{1,0},{2,1},{3,2},{4,3},{5,4},{6,5},{7,6},{8,7},{9,8},{10,9},{11,1... | collective-permute-start | bytes 18440 | tf_op jit(solution)/shard_map/ppermute | solution.py:24
  53.2 5.3 %collective-permute-start.6 = (f32[6,1,1,256]{3,2,1,0:T(1,128)S(1)}, f32[6,1,1,256]{3,2,1,0:T(1,128)S(1)}, u32[]{:S(2)}, u32[]{:S(2)}) collective-permute-start(f32[6,1,1,256]{3,2,1,0:T(1,128)S(1)} %get-tuple-element.37), channel_id=1, source_target_pairs={{0,1},{1,2},{2,3},{3,4},{4,5},{5,6},{6,7},{7,8},{8,9},{9,10},{10,1... | collective-permute-start | bytes 18440 | tf_op jit(solution)/shard_map/ppermute | solution.py:22
  57.2 4.3 %collective-permute-start.7 = (f32[6,1,1,256]{3,2,1,0:T(1,128)S(1)}, f32[6,1,1,256]{3,2,1,0:T(1,128)S(1)}, u32[]{:S(2)}, u32[]{:S(2)}) collective-permute-start(f32[6,1,1,256]{3,2,1,0:T(1,128)S(1)} %get-tuple-element.38), channel_id=1, source_target_pairs={{1,0},{2,1},{3,2},{4,3},{5,4},{6,5},{7,6},{8,7},{9,8},{10,9},{11,1... | collective-permute-start | bytes 18440 | tf_op jit(solution)/shard_map/ppermute | solution.py:24
  58.6 3.9 %collective-permute-start.3 = (bf16[6,1,8,256]{3,2,1,0:T(8,128)(2,1)S(1)}, bf16[6,1,8,256]{3,2,1,0:T(8,128)(2,1)S(1)}, u32[]{:S(2)}, u32[]{:S(2)}) collective-permute-start(bf16[6,1,8,256]{3,2,1,0:T(8,128)(2,1)S(1)} %convert_element_type.95), channel_id=1, source_target_pairs={{16,0},{0,16},{17,1},{1,17},{18,2},{2,18},{19,3},{3,19},{20,4},{4,... | collective-permute-start | bytes 73736 | tf_op jit(solution)/shard_map/ppermute | solution.py:24
  62.6 0.7 copy-start.3
  64.0 86.1 %copy-start.1 = (f32[6,6,1,8,256]{4,3,2,1,0:T(8,128)S(1)}, f32[6,6,1,8,256]{4,3,2,1,0:T(8,128)}, u32[]{:S(2)}) copy-start(f32[6,6,1,8,256]{4,3,2,1,0:T(8,128)} %param.7) | copy-start | bytes 884740
  150.2 9.4 %collective-permute-start.8 = (bf16[6,1,8,256]{3,2,1,0:T(8,128)(2,1)S(1)}, bf16[6,1,8,256]{3,2,1,0:T(8,128)(2,1)S(1)}, u32[]{:S(2)}, u32[]{:S(2)}) collective-permute-start(bf16[6,1,8,256]{3,2,1,0:T(8,128)(2,1)S(1)} %get-tuple-element.11), channel_id=1, source_target_pairs={{0,16},{16,0},{1,17},{17,1},{2,18},{18,2},{3,19},{19,3},{4,20},{20... | collective-permute-start | bytes 73736 | tf_op jit(solution)/shard_map/ppermute | solution.py:22
  152.6 7.0 %collective-permute-start.9 = (bf16[6,1,8,256]{3,2,1,0:T(8,128)(2,1)S(1)}, bf16[6,1,8,256]{3,2,1,0:T(8,128)(2,1)S(1)}, u32[]{:S(2)}, u32[]{:S(2)}) collective-permute-start(bf16[6,1,8,256]{3,2,1,0:T(8,128)(2,1)S(1)} %get-tuple-element.11), channel_id=1, source_target_pairs={{16,0},{0,16},{17,1},{1,17},{18,2},{2,18},{19,3},{3,19},{20,4},{4,... | collective-permute-start | bytes 73736 | tf_op jit(solution)/shard_map/ppermute | solution.py:24
  152.7 4.7 %collective-permute-start.10 = (f32[6,1,1,256]{3,2,1,0:T(1,128)S(1)}, f32[6,1,1,256]{3,2,1,0:T(1,128)S(1)}, u32[]{:S(2)}, u32[]{:S(2)}) collective-permute-start(f32[6,1,1,256]{3,2,1,0:T(1,128)S(1)} %get-tuple-element.30), channel_id=1, source_target_pairs={{0,1},{1,2},{2,3},{3,4},{4,5},{5,6},{6,7},{7,8},{8,9},{9,10},{10,1... | collective-permute-start | bytes 18440 | tf_op jit(solution)/shard_map/ppermute | solution.py:22
  154.0 5.4 %collective-permute-start.11 = (f32[6,1,1,256]{3,2,1,0:T(1,128)S(1)}, f32[6,1,1,256]{3,2,1,0:T(1,128)S(1)}, u32[]{:S(2)}, u32[]{:S(2)}) collective-permute-start(f32[6,1,1,256]{3,2,1,0:T(1,128)S(1)} %get-tuple-element.29), channel_id=1, source_target_pairs={{1,0},{2,1},{3,2},{4,3},{5,4},{6,5},{7,6},{8,7},{9,8},{10,9},{11,1... | collective-permute-start | bytes 18440 | tf_op jit(solution)/shard_map/ppermute | solution.py:24
  248.2 9.4 %collective-permute-start.12 = (bf16[6,1,8,256]{3,2,1,0:T(8,128)(2,1)S(1)}, bf16[6,1,8,256]{3,2,1,0:T(8,128)(2,1)S(1)}, u32[]{:S(2)}, u32[]{:S(2)}) collective-permute-start(bf16[6,1,8,256]{3,2,1,0:T(8,128)(2,1)S(1)} %get-tuple-element.8), channel_id=1, source_target_pairs={{0,16},{16,0},{1,17},{17,1},{2,18},{18,2},{3,19},{19,3},{4,20},{20... | collective-permute-start | bytes 73736 | tf_op jit(solution)/shard_map/ppermute | solution.py:22
  250.5 7.0 %collective-permute-start.13 = (bf16[6,1,8,256]{3,2,1,0:T(8,128)(2,1)S(1)}, bf16[6,1,8,256]{3,2,1,0:T(8,128)(2,1)S(1)}, u32[]{:S(2)}, u32[]{:S(2)}) collective-permute-start(bf16[6,1,8,256]{3,2,1,0:T(8,128)(2,1)S(1)} %get-tuple-element.8), channel_id=1, source_target_pairs={{16,0},{0,16},{17,1},{1,17},{18,2},{2,18},{19,3},{3,19},{20,4},{4,... | collective-permute-start | bytes 73736 | tf_op jit(solution)/shard_map/ppermute | solution.py:24
  250.6 5.4 %collective-permute-start.14 = (f32[6,1,1,256]{3,2,1,0:T(1,128)S(1)}, f32[6,1,1,256]{3,2,1,0:T(1,128)S(1)}, u32[]{:S(2)}, u32[]{:S(2)}) collective-permute-start(f32[6,1,1,256]{3,2,1,0:T(1,128)S(1)} %get-tuple-element.22), channel_id=1, source_target_pairs={{0,1},{1,2},{2,3},{3,4},{4,5},{5,6},{6,7},{7,8},{8,9},{9,10},{10,1... | collective-permute-start | bytes 18440 | tf_op jit(solution)/shard_map/ppermute | solution.py:22
  251.9 5.4 %collective-permute-start.15 = (f32[6,1,1,256]{3,2,1,0:T(1,128)S(1)}, f32[6,1,1,256]{3,2,1,0:T(1,128)S(1)}, u32[]{:S(2)}, u32[]{:S(2)}) collective-permute-start(f32[6,1,1,256]{3,2,1,0:T(1,128)S(1)} %get-tuple-element.21), channel_id=1, source_target_pairs={{1,0},{2,1},{3,2},{4,3},{5,4},{6,5},{7,6},{8,7},{9,8},{10,9},{11,1... | collective-permute-start | bytes 18440 | tf_op jit(solution)/shard_map/ppermute | solution.py:24
where the time goes:
time: 354 us; the launch traced here: 352 us
  blocking collectives  290 us (82%)
  starting transfers between devices  23.9 us (7%)
  other arithmetic  18 us (5%)
  between operations  13 us (4%)
  waiting for transfers between devices  5.48 us (2%)
    psum x3, blocking collectives, shards(): products = lax.psum(local_products, ('tor', 'pol'))  129 us
    psum x3, blocking collectives, shards(): remainder_square = lax.psum(jnp.sum(remainder * remainder), ('tor', 'pol'))  119 us
    psum x1, blocking collectives, shards(): square_sum = lax.psum(jnp.sum(right_side * right_side), ('tor', 'pol'))  42.2 us
    ppermute x8, starting transfers between devices, padded_2(): lax.ppermute(tail, axis, [(i, (i + 1) % count) for i in range(ends)])  16.9 us
  transfers between devices with their start and end apart: 16, of which 4 were waited for; matrix products, arithmetic and copies ran while one was open for 0% of the time, Pallas kernels for 0%

commit v1 on v0

v1 whole, which is shorter than its diff:
```python
import functools

import jax
import jax.numpy as jnp
from jax import lax
from jax.experimental import pallas as pl
from jax.experimental.pallas import tpu as pltpu
from jax.sharding import PartitionSpec as P

ITERS = 3
SHIFTS = (1.0, 2.0, 3.0)
inverse_step = 1.0
viscosity = 0.2
epsilon = 1e-06
AXES = ("tor", "pol")
PAIRS = [(i, j) for i in range(ITERS + 1) for j in range(i, ITERS + 1)]
BF16 = jnp.bfloat16
F32 = jnp.float32


def linear_flux(plasma, tangent, direction):
    magnetic, velocity = plasma[0:3], plasma[3:6]
    tang_mag, tang_vel = tangent[0:3], tangent[3:6]
    pressure = magnetic[0] * tang_mag[0] + magnetic[1] * tang_mag[1] + magnetic[2] * tang_mag[2]
    components = []
    for i in range(3):
        components.append(
            tang_vel[direction] * magnetic[i]
            + velocity[direction] * tang_mag[i]
            - tang_mag[direction] * velocity[i]
            - magnetic[direction] * tang_vel[i]
        )
    for i in range(3):
        moment = (
            tang_vel[direction] * velocity[i]
            + velocity[direction] * tang_vel[i]
            - tang_mag[direction] * magnetic[i]
            - magnetic[direction] * tang_mag[i]
        )
        if i == direction:
            moment = moment + pressure
        components.append(moment)
    return components


def least_squares(columns, initial_norm):
    count = len(columns)
    rhs_list = [initial_norm] + [None] * count
    cosines = []
    sines = []
    triangle = []
    estimate_list = []
    for column in range(count):
        entries = list(columns[column])
        for i in range(column):
            first_value, second_value = entries[i], entries[i + 1]
            entries[i] = cosines[i] * first_value + sines[i] * second_value
            entries[i + 1] = -sines[i] * first_value + cosines[i] * second_value
        first_value, second_value = entries[column], entries[column + 1]
        radius = jnp.sqrt(first_value * first_value + second_value * second_value)
        cosine = first_value / radius
        sine_value = second_value / radius
        cosines.append(cosine)
        sines.append(sine_value)
        entries[column] = radius
        triangle.append(entries[: column + 1])
        previous = rhs_list[column]
        rhs_list[column] = cosine * previous
        rhs_list[column + 1] = -sine_value * previous
        estimate_list.append(jnp.abs(rhs_list[column + 1]))
    weights = [None] * count
    for column in reversed(range(count)):
        partial_value = rhs_list[column]
        for later in range(column + 1, count):
            partial_value = partial_value - triangle[later][column] * weights[later]
        weights[column] = partial_value / triangle[column][column]
    return weights, estimate_list


def solve_from_gram(gram):
    count = ITERS + 1

    def inner(left, right):
        total = None
        for i in range(count):
            row = None
            for j in range(count):
                if right[j] is None:
                    continue
                term = gram[(min(i, j), max(i, j))] * right[j]
                row = term if row is None else row + term
            if left[i] is None or row is None:
                continue
            term = left[i] * row
            total = term if total is None else total + term
        return total

    def minus(left, factor, right):
        out = []
        for a, b in zip(left, right):
            if b is None:
                out.append(a)
            else:
                out.append(a - factor * b)
        return out

    initial_norm = jnp.sqrt(gram[(0, 0)] + epsilon)
    basis = [[1.0 / initial_norm] + [None] * ITERS]
    columns = []
    for column in range(ITERS):
        vector = basis[column]
        image = []
        for i in range(count):
            entry = None
            if vector[i] is not None:
                entry = SHIFTS[i] * vector[i]
            if i > 0 and vector[i - 1] is not None:
                entry = vector[i - 1] if entry is None else entry + vector[i - 1]
            image.append(entry)
        coefficients = [inner(earlier, image) for earlier in basis]
        remainder = image
        for coefficient, earlier in zip(coefficients, basis):
            remainder = minus(remainder, coefficient, earlier)
        square = jnp.maximum(inner(remainder, remainder), 0.0)
        new_norm = jnp.sqrt(square + epsilon)
        columns.append(coefficients + [new_norm])
        if column + 1 < ITERS:
            scale = 1.0 / new_norm
            basis.append([None if r is None else r * scale for r in remainder])
    weights, estimate_list = least_squares(columns, initial_norm)
    factors = []
    for k in range(ITERS):
        total = None
        for weight, vector in zip(weights, basis):
            if vector[k] is not None:
                term = weight * vector[k]
                total = term if total is None else total + term
        factors.append(total)
    return factors, estimate_list


P_ROWS, Q_ROWS = 128, 64


def pack_kernel(plasma_ref, rhs_ref, blocks_ref, res_ref, t0_ref, bulk_ref, edge_ref, side_ref, scr_p, scr_q):
    vector = [rhs_ref[b] for b in range(6)]
    t0 = []
    for a in range(6):
        total = blocks_ref[a, 0] * vector[0]
        for b in range(1, 6):
            total = total + blocks_ref[a, b] * vector[b]
        t0_ref[a] = total
        t0.append(total)
    state = [plasma_ref[a] for a in range(6)]
    deep = t0 + state
    wide = [blocks_ref[i // 6, i % 6] for i in range(36)] + [res_ref[...]]
    fields = wide[:36] + deep + [wide[36], wide[36]]
    for g in range(25):
        pair = jnp.concatenate([fields[2 * g], fields[2 * g + 1]], axis=0)
        bulk_ref[pl.ds(16 * g, 16), :] = pair.astype(BF16)
    zeros = jnp.zeros((8, deep[0].shape[1]), F32)
    for side in range(2):
        scr_p[pl.ds(P_ROWS - 8, 8), :] = zeros
        scr_q[pl.ds(Q_ROWS - 8, 8), :] = zeros
        for f, value in enumerate(deep):
            scr_p[pl.ds(4 * f, 4), :] = value[0:4] if side == 0 else value[4:8]
            scr_q[pl.ds(2 * f, 2), :] = value[0:2] if side == 0 else value[6:8]
        for f, value in enumerate(wide):
            scr_p[pl.ds(48 + 2 * f, 2), :] = value[0:2] if side == 0 else value[6:8]
            scr_q[pl.ds(24 + f, 1), :] = value[0:1] if side == 0 else value[7:8]
        side_ref[side] = scr_p[...].astype(BF16)
        edge_ref[side] = scr_q[...].astype(BF16)


def krylov_kernel(
    plasma_ref, rhs_ref, blocks_ref, res_ref, t0_ref, bulk_ref, above_ref, below_ref,
    gram_ref, t_ref, up, down, blk_p, blk_q, st_p, st_q, res_s,
):
    width = rhs_ref.shape[-1]
    up[...] = above_ref[...].astype(F32)
    down[...] = below_ref[...].astype(F32)
    zeros = jnp.zeros((8, width), F32)

    def halo(ref, at, offset, rows):
        if rows < 4:
            ref[at, 8:16] = zeros
        ref[at, 8 : 8 + rows] = down[pl.ds(offset, rows), :]
        ref[at, 16 - rows : 16] = up[pl.ds(offset, rows), :]

    def other(field):
        pair = bulk_ref[pl.ds(16 * (field // 2), 16), :].astype(F32)
        return pair[0:8] if field % 2 == 0 else pair[8:16]

    for i in range(36):
        blk_p[i, 0:8] = blocks_ref[i // 6, i % 6]
        halo(blk_p, i, 48 + 2 * i, 2)
        blk_q[i, 0:8] = other(i)
        halo(blk_q, i, P_ROWS + 24 + i, 1)
    for i in range(12):
        st_p[i, 0:8] = t0_ref[i] if i < 6 else plasma_ref[i - 6]
        halo(st_p, i, 4 * i, 4)
        st_q[i, 0:8] = other(36 + i)
        halo(st_q, i, P_ROWS + 2 * i, 2)
    res_s[0, 0:8] = res_ref[...]
    halo(res_s, 0, 120, 2)
    res_s[1, 0:8] = other(48)
    halo(res_s, 1, P_ROWS + 60, 1)

    def lane(shape):
        return lax.broadcasted_iota(jnp.int32, shape, 1)

    def depth_next(x):
        return jnp.where(lane(x.shape) == width - 1, 0.0, pltpu.roll(x, width - 1, 1))

    def depth_prev(x):
        return jnp.where(lane(x.shape) == 0, 0.0, pltpu.roll(x, 1, 1))

    def jacobian(plasma, tangent, plasma_next, tangent_next, plasma_prev, tangent_prev, res, rows):
        flux_next = linear_flux(plasma_next, tangent_next, 0)
        flux_prev = linear_flux(plasma_prev, tangent_prev, 0)
        flux_rows = linear_flux(plasma, tangent, 1)
        own = [x[0:rows] for x in tangent]
        flux_depth = linear_flux([x[0:rows] for x in plasma], own, 2)
        out = []
        for i in range(6):
            total = inverse_step * own[i] + 0.5 * (flux_next[i][0:rows] - flux_prev[i][0:rows])
            laplace = tangent_next[i][0:rows] + tangent_prev[i][0:rows] - 2.0 * own[i]
            total = total + 0.5 * (
                pltpu.roll(flux_rows[i], 15, 0)[0:rows] - pltpu.roll(flux_rows[i], 1, 0)[0:rows]
            )
            laplace = laplace + (
                pltpu.roll(tangent[i], 15, 0)[0:rows] + pltpu.roll(tangent[i], 1, 0)[0:rows] - 2.0 * own[i]
            )
            total = total + 0.5 * (depth_next(flux_depth[i]) - depth_prev(flux_depth[i]))
            laplace = laplace + (depth_next(own[i]) + depth_prev(own[i]) - 2.0 * own[i])
            out.append(total - (res[0:rows] if i < 3 else viscosity) * laplace)
        return out

    def precondition(ref, vector, rows):
        out = []
        for a in range(6):
            total = ref[6 * a, 0:rows] * vector[0]
            for b in range(1, 6):
                total = total + ref[6 * a + b, 0:rows] * vector[b]
            out.append(total)
        return out

    plasma_p = [st_p[6 + i] for i in range(6)]
    plasma_q = [st_q[6 + i] for i in range(6)]
    half_p = [x[0:8] for x in plasma_p]
    half_q = [x[0:8] for x in plasma_q]
    krylov = [[rhs_ref[i] for i in range(6)]]
    tang_p = [st_p[i] for i in range(6)]
    tang_q = [st_q[i] for i in range(6)]
    for i in range(6):
        t_ref[i] = t0_ref[i]

    image_p = jacobian(plasma_p, tang_p, plasma_q, tang_q, plasma_q, tang_q, res_s[0], 16)
    image_q = jacobian(plasma_q, tang_q, plasma_p, tang_p, plasma_p, tang_p, res_s[1], 16)
    krylov.append([image_p[i][0:8] - SHIFTS[0] * krylov[0][i] for i in range(6)])
    next_p = [x - SHIFTS[0] * t for x, t in zip(precondition(blk_p, image_p, 16), tang_p)]
    next_q = [x - SHIFTS[0] * t for x, t in zip(precondition(blk_q, image_q, 16), tang_q)]
    for i in range(6):
        t_ref[6 + i] = next_p[i][0:8]

    image_p = jacobian(plasma_p, next_p, plasma_q, next_q, plasma_q, next_q, res_s[0], 16)
    image_q = jacobian(plasma_q, next_q, half_p, [x[0:8] for x in next_p], half_p, [x[0:8] for x in next_p], res_s[1], 8)
    krylov.append([image_p[i][0:8] - SHIFTS[1] * krylov[1][i] for i in range(6)])
    last_p = [x - SHIFTS[1] * t for x, t in zip(precondition(blk_p, image_p, 16), next_p)]
    last_q = [x - SHIFTS[1] * t[0:8] for x, t in zip(precondition(blk_q, image_q, 8), next_q)]
    for i in range(6):
        t_ref[12 + i] = last_p[i][0:8]

    image_p = jacobian(plasma_p, last_p, half_q, last_q, half_q, last_q, res_s[0], 8)
    krylov.append([image_p[i] - SHIFTS[2] * krylov[2][i] for i in range(6)])

    out = jnp.zeros((1, 128), F32)
    lanes = lax.broadcasted_iota(jnp.int32, (1, 128), 1)
    for k, (i, j) in enumerate(PAIRS):
        total = krylov[i][0] * krylov[j][0]
        for f in range(1, 6):
            total = total + krylov[i][f] * krylov[j][f]
        total = jnp.sum(jnp.sum(total, axis=0, keepdims=True), axis=1, keepdims=True)
        out = jnp.where(lanes == k, total, out)
    gram_ref[...] = jnp.broadcast_to(out[None], gram_ref.shape)


def finish_kernel(inverse_root, gram_ref, t_ref, update_ref, estimates_ref):
    gathered = gram_ref[...]
    sums = jnp.sum(gathered, axis=0)
    lanes = lax.broadcasted_iota(jnp.int32, sums.shape, 1)
    gram = {}
    for k, pair in enumerate(PAIRS):
        gram[pair] = jnp.sum(jnp.where(lanes == k, sums, 0.0), axis=1, keepdims=True)
    factors, estimate_list = solve_from_gram(gram)
    width = update_ref.shape[-1]
    wide = [jnp.broadcast_to(f, (8, width)) for f in factors]
    for i in range(6):
        update_ref[i] = wide[0] * t_ref[i] + wide[1] * t_ref[6 + i] + wide[2] * t_ref[12 + i]
    out = jnp.zeros((1, 128), F32)
    for k, value in enumerate(estimate_list):
        out = jnp.where(lanes == k, value * inverse_root, out)
    estimates_ref[...] = out


def two_planes(pol, plasma_state, right_side, resistivity, jacobi_blocks):
    rows, width = plasma_state.shape[2], plasma_state.shape[3]
    count = 2 * pol

    def pairs(partner):
        out = []
        for t in range(2):
            for p in range(pol):
                other = partner(t, p)
                if 0 <= other[1] < pol:
                    out.append((t * pol + p, other[0] * pol + other[1]))
        return out

    across = pairs(lambda t, p: (1 - t, p))
    core = pairs(lambda t, p: (t, p ^ 1))
    outer = pairs(lambda t, p: (t, p - 1 if p % 2 == 0 else p + 1))

    plasma = plasma_state.reshape(6, rows, width)
    rhs = right_side.reshape(6, rows, width)
    res = resistivity.reshape(rows, width)
    blocks = jacobi_blocks.reshape(6, 6, rows, width)
    vmem = pl.BlockSpec(memory_space=pltpu.VMEM)
    shape = jax.ShapeDtypeStruct
    t0, bulk, edge, side = pl.pallas_call(
        pack_kernel,
        out_shape=(
            shape((6, rows, width), F32),
            shape((400, width), BF16),
            shape((2, Q_ROWS, width), BF16),
            shape((2, P_ROWS, width), BF16),
        ),
        in_specs=[vmem] * 4,
        out_specs=(vmem,) * 4,
        scratch_shapes=[pltpu.VMEM((P_ROWS, width), F32), pltpu.VMEM((Q_ROWS, width), F32)],
    )(plasma, rhs, blocks, res)
    edge = lax.ppermute(edge, AXES, across)
    bulk = lax.ppermute(bulk, AXES, across)
    even = lax.axis_index("pol") % 2 == 0
    both = jnp.concatenate([side, edge], axis=1)
    from_core = lax.ppermute(jnp.where(even, both[1], both[0]), AXES, core)
    from_outer = lax.ppermute(jnp.where(even, both[0], both[1]), AXES, outer)
    above = jnp.where(even, from_outer, from_core)
    below = jnp.where(even, from_core, from_outer)
    slab = P_ROWS + Q_ROWS
    gram, tangents = pl.pallas_call(
        krylov_kernel,
        out_shape=(shape((count, 1, 128), F32), shape((18, rows, width), F32)),
        in_specs=[vmem] * 8,
        out_specs=(vmem,) * 2,
        scratch_shapes=[
            pltpu.VMEM((slab, width), F32),
            pltpu.VMEM((slab, width), F32),
            pltpu.VMEM((36, 16, width), F32),
            pltpu.VMEM((36, 16, width), F32),
            pltpu.VMEM((12, 16, width), F32),
            pltpu.VMEM((12, 16, width), F32),
            pltpu.VMEM((2, 16, width), F32),
        ],
    )(plasma, rhs, blocks, res, t0, bulk, above, below)
    gram = lax.all_to_all(gram, AXES, 0, 0, tiled=True)
    inverse_root = float((6.0 * count * rows * width) ** -0.5)
    update, estimates = pl.pallas_call(
        functools.partial(finish_kernel, inverse_root),
        out_shape=(shape((6, rows, width), F32), shape((1, 128), F32)),
        in_specs=[vmem] * 2,
        out_specs=(vmem,) * 2,
    )(gram, tangents)
    return update.reshape(plasma_state.shape), estimates[0, :ITERS]


def padded(cells, axis, dim, closed):
    count = lax.axis_size(axis)
    ends = count if closed else count - 1
    size = cells.shape[dim]
    head = lax.slice_in_dim(cells, 0, 1, axis=dim)
    tail = lax.slice_in_dim(cells, size - 1, size, axis=dim)
    before = lax.ppermute(tail, axis, [(i, (i + 1) % count) for i in range(ends)])
    after = lax.ppermute(head, axis, [((i + 1) % count, i) for i in range(ends)])
    return jnp.concatenate([before, cells, after], axis=dim)


def any_planes(plasma_state, right_side, resistivity, jacobi_blocks):
    cell_count = right_side.size * lax.axis_size("tor") * lax.axis_size("pol")
    fixed = jnp.full((3,) + resistivity.shape, viscosity, F32)
    diffusion = jnp.concatenate([jnp.broadcast_to(resistivity[None], fixed.shape), fixed])

    def around(cells):
        planes = padded(cells.astype(BF16), "tor", 1, True).astype(F32)
        planes = jnp.concatenate([planes[:, :1], cells, planes[:, -1:]], axis=1)
        deep = jnp.pad(cells, ((0, 0), (0, 0), (0, 0), (1, 1)))
        return planes, padded(cells, "pol", 2, False), deep

    plasma_around = around(plasma_state)
    vectors, tangents = [right_side], []
    for shift in SHIFTS:
        vector = vectors[-1]
        tangent = jnp.sum(jacobi_blocks * vector[None], axis=1)
        tangents.append(tangent)
        image = inverse_step * tangent
        laplace = jnp.zeros_like(tangent)
        for direction, (plasma, cells) in enumerate(zip(plasma_around, around(tangent))):
            dim = direction + 1
            flux = jnp.stack(linear_flux(plasma, cells, direction))
            size = cells.shape[dim]
            part = functools.partial(lax.slice_in_dim, axis=dim)
            image = image + 0.5 * (part(flux, 2, size) - part(flux, 0, size - 2))
            laplace = laplace + part(cells, 2, size) + part(cells, 0, size - 2) - 2.0 * tangent
        vectors.append(image - diffusion * laplace - shift * vector)
    local = jnp.stack([jnp.sum(vectors[i] * vectors[j]) for i, j in PAIRS])
    gram = lax.psum(local, AXES)
    factors, estimate_list = solve_from_gram({pair: gram[k] for k, pair in enumerate(PAIRS)})
    update = sum(factor * tangent for factor, tangent in zip(factors, tangents))
    return update, jnp.stack(estimate_list) / jnp.sqrt(F32(cell_count))


def solution(mesh):
    tor, pol = mesh.shape["tor"], mesh.shape["pol"]

    def shards(plasma_state, right_side, resistivity, jacobi_blocks):
        _, planes, rows, width = plasma_state.shape
        fast = tor == 2 and planes == 1 and pol % 2 == 0 and rows == 8 and width % 128 == 0
        if fast:
            return two_planes(pol, plasma_state, right_side, resistivity, jacobi_blocks)
        return any_planes(plasma_state, right_side, resistivity, jacobi_blocks)

    return jax.shard_map(
        shards,
        mesh=mesh,
        in_specs=(
            P(None, "tor", "pol", None),
            P(None, "tor", "pol", None),
            P("tor", "pol", None),
            P(None, None, "tor", "pol", None),
        ),
        out_specs=(P(None, "tor", "pol", None), P()),
        check_vma=False,
    )
```

time: 354 us -> 38.2 us (0.11)
  blocking collectives: 290 us -> 16.7 us
  starting transfers between devices: 23.9 us -> 5.7 us
  other arithmetic: 18 us -> 0.71 us
  between operations: 13 us -> 0.67 us
  Pallas kernels: 0 us -> 6.66 us
    psum x7 -> x0, blocking collectives: 290 us -> none  [the longest x3 129 us: shards(): products = lax.psum(local_products, ('tor', 'pol'))]
    ppermute x16 -> x4, starting transfers between devices: 23.9 us -> 5.7 us  [the longest x1 2.94 us: two_planes(): edge = lax.ppermute(edge, AXES, across)]
    all_to_all x0 -> x1, blocking collectives: none -> 16.7 us  [two_planes(): gram = lax.all_to_all(gram, AXES, 0, 0, tiled=True)]
    reduce_sum x16 -> x0, other arithmetic: 9.56 us -> none  [the longest x3 5.77 us: shards(): remainder_square = lax.psum(jnp.sum(remainder * remainder), ('tor', 'pol'))]
    pallas_call x0 -> x3, Pallas kernels: none -> 6.66 us  [the longest x1 2.99 us: two_planes(): pl.pallas_call(krylov_kernel, out_shape=(shape((count, 1, 128), F32), sha...]
  transfers between devices with their start and end apart: 16 -> 4, of which waited for: 4 -> 2; matrix products, arithmetic and copies ran while one was open for 0% -> 4% of each run, Pallas kernels for 0% -> 0%
where the time goes in v1:
time: 38.2 us; the launch traced here: 37.9 us
  blocking collectives  16.7 us (44%)
  Pallas kernels  6.66 us (17%)
  starting transfers between devices  5.7 us (15%)
  waiting for transfers between devices  4.58 us (12%)
  local copies, waits for them, and re-layouts  2.91 us (8%)
  other arithmetic  0.71 us (2%)
  between operations  0.67 us (2%)
    all_to_all x1, blocking collectives, two_planes(): gram = lax.all_to_all(gram, AXES, 0, 0, tiled=True)  16.7 us
    ppermute x1, waiting for transfers between devices, two_planes(): bulk = lax.ppermute(bulk, AXES, across)  3.04 us
    pallas_call x1, Pallas kernels, two_planes(): pl.pallas_call(krylov_kernel, out_shape=(shape((count, 1, 128), F32), sha...  2.99 us
    ppermute x1, starting transfers between devices, two_planes(): edge = lax.ppermute(edge, AXES, across)  2.94 us
    unnamed x7, local copies, waits for them, and re-layouts  2.39 us
    ppermute x1, starting transfers between devices, two_planes(): bulk = lax.ppermute(bulk, AXES, across)  2.02 us
    pallas_call x1, Pallas kernels, two_planes(): pl.pallas_call(pack_kernel, out_shape=(shape((6, rows, width), F32), shap...  1.86 us
    pallas_call x1, Pallas kernels, two_planes(): pl.pallas_call(functools.partial(finish_kernel, inverse_root), out_shape=...  1.8 us
  transfers between devices with their start and end apart: 4, of which 2 were waited for; matrix products, arithmetic and copies ran while one was open for 4% of the time, Pallas kernels for 0%

profile of v1, /device:TPU:0, one launch (start us, length us, event | category | flops | bytes accessed | tf_op | source)
XLA Modules:
  0.0 37.9 jit_solution(5673552140868660840)
XLA Ops:
  0.6 1.9 %shard_map.59 = (f32[6,8,256]{2,1,0:T(8,128)}, bf16[400,256]{1,0:T(8,128)(2,1)}, bf16[2,64,256]{2,1,0:T(8,128)(2,1)}, bf16[2,128,256]{2,1,0:T(8,128)(2,1)}) custom-call(f32[6,8,256]{2,1,0:T(8,128)} %bitcast.15, f32[6,8,256]{2,1,0:T(8,128)} %bitcast.17, f32[6,6,8,256]{3,2,1,0:T(8,128)} %bitcast.13, f32[8,256]{1,0:T(8,128)} %bitcast.19), custom_call_target="tpu_custom_call" | custom-call | tf_op jit(solution)/shard_map/pallas_call | solution.py:329
  2.5 2.9 %collective-permute-start.1 = (bf16[2,64,256]{2,1,0:T(8,128)(2,1)}, bf16[2,64,256]{2,1,0:T(8,128)(2,1)S(1)}, u32[]{:S(2)}, u32[]{:S(2)}) collective-permute-start(bf16[2,64,256]{2,1,0:T(8,128)(2,1)} %get-tuple-element.13), channel_id=1, source_target_pairs={{0,16},{1,17},{2,18},{3,19},{4,20},{5,21},{6,22},{7,23},{8,24},{9,... | collective-permute-start | bytes 196616 | tf_op jit(solution)/shard_map/ppermute | solution.py:341
  5.4 0.9 %constant_dynamic-update-slice_fusion.1 = bf16[2,192,256]{2,1,0:T(8,128)(2,1)S(1)} fusion(bf16[2,128,256]{2,1,0:T(8,128)(2,1)} %get-tuple-element.12), kind=kLoop, calls=%fused_computation.5 | loop fusion | bytes 262144
  6.3 1.5 %collective-permute-done.1 = bf16[2,64,256]{2,1,0:T(8,128)(2,1)S(1)} collective-permute-done((bf16[2,64,256]{2,1,0:T(8,128)(2,1)}, bf16[2,64,256]{2,1,0:T(8,128)(2,1)S(1)}, u32[]{:S(2)}, u32[]{:S(2)}) %collective-permute-start.1) | collective-permute-done | bytes 65568 | tf_op jit(solution)/shard_map/ppermute | solution.py:341
  7.9 0.0 copy-start.1
  7.9 0.1 collective-permute-start.3
  8.0 0.7 %collective-permute-start.2 = (bf16[192,256]{1,0:T(8,128)(2,1)S(1)}, bf16[192,256]{1,0:T(8,128)(2,1)S(1)}, u32[]{:S(2)}, u32[]{:S(2)}) collective-permute-start(bf16[192,256]{1,0:T(8,128)(2,1)S(1)} %get-tuple-element.23), channel_id=1, source_target_pairs={{1,2},{2,1},{3,4},{4,3},{5,6},{6,5},{7,8},{8,7},{9,10},{10,9},{11,... | collective-permute-start | bytes 294920 | tf_op jit(solution)/shard_map/ppermute | solution.py:346
  8.7 0.1 copy-done.1
  8.8 2.0 %collective-permute-start = (bf16[400,256]{1,0:T(8,128)(2,1)S(1)}, bf16[400,256]{1,0:T(8,128)(2,1)S(1)}, u32[]{:S(2)}, u32[]{:S(2)}) collective-permute-start(bf16[400,256]{1,0:T(8,128)(2,1)S(1)} %copy-done.1), channel_id=1, source_target_pairs={{0,16},{1,17},{2,18},{3,19},{4,20},{5,21},{6,22},{7,23},{8,24},{9,... | collective-permute-start | bytes 614408 | tf_op jit(solution)/shard_map/ppermute | solution.py:342
  10.8 0.0 collective-permute-done.3
  10.8 0.0 collective-permute-done.2
  10.9 0.7 %broadcast_select_fusion = (bf16[192,256]{1,0:T(8,128)(2,1)}, bf16[192,256]{1,0:T(8,128)(2,1)}) fusion(bf16[192,256]{1,0:T(8,128)(2,1)S(1)} %collective-permute-done.3, bf16[192,256]{1,0:T(8,128)(2,1)S(1)} %collective-permute-done.2, pred[]{:T(512)S(6)} %eq.5), kind=kLoop, calls=%fused_computation.2 | loop fusion | flops 98304 | bytes 393217 | tf_op jit(solution)/shard_map/jit(_where)/select_n | solution.py:348
  11.5 3.0 %collective-permute-done.bulk_ref = bf16[400,256]{1,0:T(8,128)(2,1)S(1)} collective-permute-done((bf16[400,256]{1,0:T(8,128)(2,1)S(1)}, bf16[400,256]{1,0:T(8,128)(2,1)S(1)}, u32[]{:S(2)}, u32[]{:S(2)}) %collective-permute-start) | collective-permute-done | bytes 204832 | tf_op jit(solution)/shard_map/ppermute | solution.py:342
  14.6 0.0 copy-start
  14.6 0.7 %copy-done = bf16[400,256]{1,0:T(8,128)(2,1)} copy-done((bf16[400,256]{1,0:T(8,128)(2,1)}, bf16[400,256]{1,0:T(8,128)(2,1)S(1)}, u32[]{:S(2)}) %copy-start) | copy-done | bytes 204824
  15.3 3.0 %shard_map.60 = (f32[32,1,128]{2,1,0:T(1,128)}, f32[18,8,256]{2,1,0:T(8,128)}) custom-call(f32[6,8,256]{2,1,0:T(8,128)} %bitcast.16, f32[6,8,256]{2,1,0:T(8,128)} %bitcast.18, f32[6,6,8,256]{3,2,1,0:T(8,128)} %bitcast.14, f32[8,256]{1,0:T(8,128)} %bitcast.20, f32[6,8,256]{2,1,0:T(8,128)} %get-tuple-element.10.t0_ref, bf16[400,256]{1,0:T(8,128)(2,1)} %copy-done, ...), custom_call_target="tpu_custom_call" | custom-call | tf_op jit(solution)/shard_map/pallas_call | solution.py:350
  18.3 16.7 %all_to_all.5.gram_ref = f32[32,1,128]{2,1,0:T(1,128)} all-to-all(f32[32,1,128]{2,1,0:T(1,128)} %get-tuple-element.14), channel_id=1, replica_groups=mesh['tor'=2,'pol'=16] {'tor','pol'}, dimensions={0} | all-to-all | bytes 32768 | tf_op jit(solution)/shard_map/all_to_all | solution.py:365
  35.0 1.8 %shard_map.61 = (f32[6,8,256]{2,1,0:T(8,128)}, f32[1,128]{1,0:T(1,128)}) custom-call(f32[32,1,128]{2,1,0:T(1,128)} %all_to_all.5.gram_ref, f32[18,8,256]{2,1,0:T(8,128)} %get-tuple-element.15.t_ref), custom_call_target="tpu_custom_call" | custom-call | tf_op jit(solution)/shard_map/pallas_call | solution.py:367
  36.8 0.0 copy-start.2
  36.8 0.7 %copy-done.2 = f32[1,128]{1,0:T(1,128)S(1)} copy-done((f32[1,128]{1,0:T(1,128)S(1)}, f32[1,128]{1,0:T(1,128)}, u32[]{:S(2)}) %copy-start.2) | copy-done | bytes 536
  37.4 0.5 %slice_bitcast_fusion = f32[3]{0:T(128)} fusion(f32[1,128]{1,0:T(1,128)S(1)} %copy-done.2), kind=kLoop, calls=%fused_computation.6 | loop fusion | bytes 24 | tf_op jit(solution)/shard_map/squeeze | solution.py:373
  (2 shorter events, 0.0 us)
Async XLA Ops:
  2.5 5.4 %collective-permute-start.1 = (bf16[2,64,256]{2,1,0:T(8,128)(2,1)}, bf16[2,64,256]{2,1,0:T(8,128)(2,1)S(1)}, u32[]{:S(2)}, u32[]{:S(2)}) collective-permute-start(bf16[2,64,256]{2,1,0:T(8,128)(2,1)} %get-tuple-element.13), channel_id=1, source_target_pairs={{0,16},{1,17},{2,18},{3,19},{4,20},{5,21},{6,22},{7,23},{8,24},{9,... | collective-permute-start | bytes 196616 | tf_op jit(solution)/shard_map/ppermute | solution.py:341
  7.9 0.9 %copy-start.1 = (bf16[400,256]{1,0:T(8,128)(2,1)S(1)}, bf16[400,256]{1,0:T(8,128)(2,1)}, u32[]{:S(2)}) copy-start(bf16[400,256]{1,0:T(8,128)(2,1)} %get-tuple-element.11) | copy-start | bytes 614404
  7.9 2.9 %collective-permute-start.3 = (bf16[192,256]{1,0:T(8,128)(2,1)S(1)}, bf16[192,256]{1,0:T(8,128)(2,1)S(1)}, u32[]{:S(2)}, u32[]{:S(2)}) collective-permute-start(bf16[192,256]{1,0:T(8,128)(2,1)S(1)} %get-tuple-element.22), channel_id=1, source_target_pairs={{0,1},{1,0},{2,3},{3,2},{4,5},{5,4},{6,7},{7,6},{8,9},{9,8},{10,11... | collective-permute-start | bytes 294920 | tf_op jit(solution)/shard_map/ppermute | solution.py:345
  8.0 2.8 %collective-permute-start.2 = (bf16[192,256]{1,0:T(8,128)(2,1)S(1)}, bf16[192,256]{1,0:T(8,128)(2,1)S(1)}, u32[]{:S(2)}, u32[]{:S(2)}) collective-permute-start(bf16[192,256]{1,0:T(8,128)(2,1)S(1)} %get-tuple-element.23), channel_id=1, source_target_pairs={{1,2},{2,1},{3,4},{4,3},{5,6},{6,5},{7,8},{8,7},{9,10},{10,9},{11,... | collective-permute-start | bytes 294920 | tf_op jit(solution)/shard_map/ppermute | solution.py:346
  8.8 5.8 %collective-permute-start = (bf16[400,256]{1,0:T(8,128)(2,1)S(1)}, bf16[400,256]{1,0:T(8,128)(2,1)S(1)}, u32[]{:S(2)}, u32[]{:S(2)}) collective-permute-start(bf16[400,256]{1,0:T(8,128)(2,1)S(1)} %copy-done.1), channel_id=1, source_target_pairs={{0,16},{1,17},{2,18},{3,19},{4,20},{5,21},{6,22},{7,23},{8,24},{9,... | collective-permute-start | bytes 614408 | tf_op jit(solution)/shard_map/ppermute | solution.py:342
  14.6 0.7 %copy-start = (bf16[400,256]{1,0:T(8,128)(2,1)}, bf16[400,256]{1,0:T(8,128)(2,1)S(1)}, u32[]{:S(2)}) copy-start(bf16[400,256]{1,0:T(8,128)(2,1)S(1)} %collective-permute-done.bulk_ref) | copy-start | bytes 614404
  36.8 0.7 %copy-start.2 = (f32[1,128]{1,0:T(1,128)S(1)}, f32[1,128]{1,0:T(1,128)}, u32[]{:S(2)}) copy-start(f32[1,128]{1,0:T(1,128)} %get-tuple-element.17) | copy-start | bytes 1540

commit v2 on v1

--- a/solution.py
+++ b/solution.py
@@ -139,13 +139,30 @@
     return factors, estimate_list
 
 
+in_vmem = functools.partial(pltpu.with_memory_space_constraint, memory_space=pltpu.VMEM)
+in_hbm = functools.partial(pltpu.with_memory_space_constraint, memory_space=pltpu.HBM)
+vmem_array = pltpu.VMEM
 P_ROWS, Q_ROWS = 128, 64
 
 
-def pack_kernel(plasma_ref, rhs_ref, blocks_ref, res_ref, t0_ref, bulk_ref, edge_ref, side_ref, scr_p, scr_q):
+def pack_kernel(
+    plasma_ref, rhs_ref, blocks_ref, res_ref,
+    t0_ref, bulk_ref, edge_ref, side_ref, own_ref, scr_p, scr_q, blocks_in, res_in, state_in, rhs_in, sems,
+):
+    copies = [
+        pltpu.make_async_copy(rhs_ref, rhs_in, sems.at[0]),
+        pltpu.make_async_copy(plasma_ref, state_in, sems.at[1]),
+        pltpu.make_async_copy(res_ref, res_in, sems.at[2]),
+    ] + [pltpu.make_async_copy(blocks_ref.at[a], blocks_in.at[a], sems.at[3 + a]) for a in range(6)]
+    for copy in copies:
+        copy.start()
+    for copy in copies[:3]:
+        copy.wait()
+    plasma_ref, rhs_ref, res_ref, blocks_ref = state_in, rhs_in, res_in, blocks_in
     vector = [rhs_ref[b] for b in range(6)]
     t0 = []
     for a in range(6):
+        copies[3 + a].wait()
         total = blocks_ref[a, 0] * vector[0]
         for b in range(1, 6):
             total = total + blocks_ref[a, b] * vector[b]
@@ -154,6 +171,8 @@
     state = [plasma_ref[a] for a in range(6)]
     deep = t0 + state
     wide = [blocks_ref[i // 6, i % 6] for i in range(36)] + [res_ref[...]]
+    for f, value in enumerate(wide + state + vector):
+        own_ref[f] = value
     fields = wide[:36] + deep + [wide[36], wide[36]]
     for g in range(25):
         pair = jnp.concatenate([fields[2 * g], fields[2 * g + 1]], axis=0)
@@ -172,13 +191,22 @@
         edge_ref[side] = scr_q[...].astype(BF16)
 
 
+def unpack_kernel(bulk_ref, other_ref):
+    for g in range(25):
+        pair = bulk_ref[pl.ds(16 * g, 16), :].astype(F32)
+        other_ref[2 * g] = pair[0:8]
+        other_ref[2 * g + 1] = pair[8:16]
+
+
 def krylov_kernel(
-    plasma_ref, rhs_ref, blocks_ref, res_ref, t0_ref, bulk_ref, above_ref, below_ref,
+    own_ref, t0_ref, other_ref, outer_ref, core_ref,
     gram_ref, t_ref, up, down, blk_p, blk_q, st_p, st_q, res_s,
 ):
-    width = rhs_ref.shape[-1]
-    up[...] = above_ref[...].astype(F32)
-    down[...] = below_ref[...].astype(F32)
+    width = own_ref.shape[-1]
+    even = lax.axis_index("pol") % 2 == 0
+    from_outer, from_core = outer_ref[...].astype(F32), core_ref[...].astype(F32)
+    up[...] = jnp.where(even, from_outer, from_core)
+    down[...] = jnp.where(even, from_core, from_outer)
     zeros = jnp.zeros((8, width), F32)
 
     def halo(ref, at, offset, rows):
@@ -188,20 +216,19 @@
         ref[at, 16 - rows : 16] = up[pl.ds(offset, rows), :]
 
     def other(field):
-        pair = bulk_ref[pl.ds(16 * (field // 2), 16), :].astype(F32)
-        return pair[0:8] if field % 2 == 0 else pair[8:16]
+        return other_ref[field]
 
     for i in range(36):
-        blk_p[i, 0:8] = blocks_ref[i // 6, i % 6]
+        blk_p[i, 0:8] = own_ref[i]
         halo(blk_p, i, 48 + 2 * i, 2)
         blk_q[i, 0:8] = other(i)
         halo(blk_q, i, P_ROWS + 24 + i, 1)
     for i in range(12):
-        st_p[i, 0:8] = t0_ref[i] if i < 6 else plasma_ref[i - 6]
+        st_p[i, 0:8] = t0_ref[i] if i < 6 else own_ref[31 + i]
         halo(st_p, i, 4 * i, 4)
         st_q[i, 0:8] = other(36 + i)
         halo(st_q, i, P_ROWS + 2 * i, 2)
-    res_s[0, 0:8] = res_ref[...]
+    res_s[0, 0:8] = own_ref[36]
     halo(res_s, 0, 120, 2)
     res_s[1, 0:8] = other(48)
     halo(res_s, 1, P_ROWS + 60, 1)
@@ -249,7 +276,7 @@
     plasma_q = [st_q[6 + i] for i in range(6)]
     half_p = [x[0:8] for x in plasma_p]
     half_q = [x[0:8] for x in plasma_q]
-    krylov = [[rhs_ref[i] for i in range(6)]]
+    krylov = [[own_ref[43 + i] for i in range(6)]]
     tang_p = [st_p[i] for i in range(6)]
     tang_q = [st_q[i] for i in range(6)]
     for i in range(6):
@@ -297,10 +324,8 @@
     wide = [jnp.broadcast_to(f, (8, width)) for f in factors]
     for i in range(6):
         update_ref[i] = wide[0] * t_ref[i] + wide[1] * t_ref[6 + i] + wide[2] * t_ref[12 + i]
-    out = jnp.zeros((1, 128), F32)
     for k, value in enumerate(estimate_list):
-        out = jnp.where(lanes == k, value * inverse_root, out)
-    estimates_ref[...] = out
+        estimates_ref[k] = jnp.sum(value * inverse_root)
 
 
 def two_planes(pol, plasma_state, right_side, resistivity, jacobi_blocks):
@@ -326,31 +351,41 @@
     blocks = jacobi_blocks.reshape(6, 6, rows, width)
     vmem = pl.BlockSpec(memory_space=pltpu.VMEM)
     shape = jax.ShapeDtypeStruct
-    t0, bulk, edge, side = pl.pallas_call(
+    t0, bulk, edge, side, own = pl.pallas_call(
         pack_kernel,
         out_shape=(
-            shape((6, rows, width), F32),
-            shape((400, width), BF16),
-            shape((2, Q_ROWS, width), BF16),
-            shape((2, P_ROWS, width), BF16),
+            vmem_array((6, rows, width), F32),
+            vmem_array((400, width), BF16),
+            vmem_array((2, Q_ROWS, width), BF16),
+            vmem_array((2, P_ROWS, width), BF16),
+            vmem_array((49, rows, width), F32),
         ),
-        in_specs=[vmem] * 4,
-        out_specs=(vmem,) * 4,
-        scratch_shapes=[pltpu.VMEM((P_ROWS, width), F32), pltpu.VMEM((Q_ROWS, width), F32)],
-    )(plasma, rhs, blocks, res)
+        in_specs=[pl.BlockSpec(memory_space=pltpu.HBM)] * 4,
+        out_specs=(vmem,) * 5,
+        scratch_shapes=[
+            pltpu.VMEM((P_ROWS, width), F32),
+            pltpu.VMEM((Q_ROWS, width), F32),
+            pltpu.VMEM((6, 6, rows, width), F32),
+            pltpu.VMEM((rows, width), F32),
+            pltpu.VMEM((6, rows, width), F32),
+            pltpu.VMEM((6, rows, width), F32),
+            pltpu.SemaphoreType.DMA((9,)),
+        ],
+    )(*map(in_hbm, (plasma, rhs, blocks, res)))
     edge = lax.ppermute(edge, AXES, across)
     bulk = lax.ppermute(bulk, AXES, across)
     even = lax.axis_index("pol") % 2 == 0
     both = jnp.concatenate([side, edge], axis=1)
     from_core = lax.ppermute(jnp.where(even, both[1], both[0]), AXES, core)
     from_outer = lax.ppermute(jnp.where(even, both[0], both[1]), AXES, outer)
-    above = jnp.where(even, from_outer, from_core)
-    below = jnp.where(even, from_core, from_outer)
+    other = pl.pallas_call(
+        unpack_kernel, out_shape=vmem_array((50, rows, width), F32), in_specs=[vmem], out_specs=vmem
+    )(in_vmem(bulk))
     slab = P_ROWS + Q_ROWS
     gram, tangents = pl.pallas_call(
         krylov_kernel,
-        out_shape=(shape((count, 1, 128), F32), shape((18, rows, width), F32)),
-        in_specs=[vmem] * 8,
+        out_shape=(vmem_array((count, 1, 128), F32), vmem_array((18, rows, width), F32)),
+        in_specs=[vmem] * 5,
         out_specs=(vmem,) * 2,
         scratch_shapes=[
             pltpu.VMEM((slab, width), F32),
@@ -361,16 +396,16 @@
             pltpu.VMEM((12, 16, width), F32),
             pltpu.VMEM((2, 16, width), F32),
         ],
-    )(plasma, rhs, blocks, res, t0, bulk, above, below)
+    )(*map(in_vmem, (own, t0, other, from_outer, from_core)))
     gram = lax.all_to_all(gram, AXES, 0, 0, tiled=True)
     inverse_root = float((6.0 * count * rows * width) ** -0.5)
     update, estimates = pl.pallas_call(
         functools.partial(finish_kernel, inverse_root),
-        out_shape=(shape((6, rows, width), F32), shape((1, 128), F32)),
+        out_shape=(shape((6, rows, width), F32), shape((ITERS,), F32)),
         in_specs=[vmem] * 2,
-        out_specs=(vmem,) * 2,
-    )(gram, tangents)
-    return update.reshape(plasma_state.shape), estimates[0, :ITERS]
+        out_specs=(vmem, pl.BlockSpec(memory_space=pltpu.SMEM)),
+    )(in_vmem(gram), in_vmem(tangents))
+    return update.reshape(plasma_state.shape), estimates
 
 
 def padded(cells, axis, dim, closed):

time: 38.2 us -> 29.8 us (0.78)
  Pallas kernels: 6.66 us -> 3.45 us
  local copies, waits for them, and re-layouts: 2.91 us -> 0.01 us
  starting transfers between devices: 5.7 us -> 3.82 us
  waiting for transfers between devices: 4.58 us -> 5.77 us
  blocking collectives: 16.7 us -> 15.8 us
  other arithmetic: 0.71 us -> 0.02 us
    unnamed x7 -> x1, local copies, waits for them, and re-layouts: 2.39 us -> 0.01 us
    pallas_call x2 -> x3, Pallas kernels: 4.86 us -> 2.56 us  [the longest x1 1.3 us: two_planes(): pl.pallas_call(krylov_kernel, out_shape=(vmem_array((count, 1, 128), F32)...]
    ppermute x1, starting transfers between devices: 2.02 us -> 0.08 us  [two_planes(): bulk = lax.ppermute(bulk, AXES, across)]
    pallas_call x1, Pallas kernels: 1.8 us -> 0.89 us  [two_planes(): pl.pallas_call(functools.partial(finish_kernel, inverse_root), out_shape=...]
    all_to_all x1, blocking collectives: 16.7 us -> 15.8 us  [two_planes(): gram = lax.all_to_all(gram, AXES, 0, 0, tiled=True)]
    ppermute x1, waiting for transfers between devices: 1.54 us -> 2.41 us  [two_planes(): edge = lax.ppermute(edge, AXES, across)]
    select_n x1 -> x0, other arithmetic: 0.69 us -> none  [two_planes(): below = jnp.where(even, from_core, from_outer)]
    squeeze x1 -> x0, local copies, waits for them, and re-layouts: 0.51 us -> none  [two_planes(): return (update.reshape(plasma_state.shape), estimates[0, :ITERS])]
  transfers between devices with their start and end apart: 4 -> 4, of which waited for: 2 -> 2; matrix products, arithmetic and copies ran while one was open for 4% -> 0% of each run, Pallas kernels for 0% -> 0%
where the time goes in v2:
time: 29.8 us; the launch traced here: 29.6 us
  blocking collectives  15.8 us (53%)
  waiting for transfers between devices  5.77 us (19%)
  starting transfers between devices  3.82 us (13%)
  Pallas kernels  3.45 us (12%)
  between operations  0.69 us (2%)
    all_to_all x1, blocking collectives, two_planes(): gram = lax.all_to_all(gram, AXES, 0, 0, tiled=True)  15.8 us
    ppermute x1, waiting for transfers between devices, two_planes(): bulk = lax.ppermute(bulk, AXES, across)  3.36 us
    ppermute x1, starting transfers between devices, two_planes(): edge = lax.ppermute(edge, AXES, across)  3 us
    ppermute x1, waiting for transfers between devices, two_planes(): edge = lax.ppermute(edge, AXES, across)  2.41 us
    pallas_call x1, Pallas kernels, two_planes(): pl.pallas_call(krylov_kernel, out_shape=(vmem_array((count, 1, 128), F32)...  1.3 us
    pallas_call x1, Pallas kernels, two_planes(): pl.pallas_call(pack_kernel, out_shape=(vmem_array((6, rows, width), F32),...  1.23 us
    pallas_call x1, Pallas kernels, two_planes(): pl.pallas_call(functools.partial(finish_kernel, inverse_root), out_shape=...  0.89 us
    ppermute x1, starting transfers between devices, two_planes(): from_outer = lax.ppermute(jnp.where(even, both[0], both[1]), AXES, outer)  0.67 us
  transfers between devices with their start and end apart: 4, of which 2 were waited for; matrix products, arithmetic and copies ran while one was open for 0% of the time, Pallas kernels for 0%

profile of v2, /device:TPU:0, one launch (start us, length us, event | category | flops | bytes accessed | tf_op | source)
XLA Modules:
  0.0 29.6 jit_solution(2018946222866868871)
XLA Ops:
  0.6 1.2 %shard_map.59 = (f32[6,8,256]{2,1,0:T(8,128)S(1)}, bf16[400,256]{1,0:T(8,128)(2,1)S(1)}, bf16[2,64,256]{2,1,0:T(8,128)(2,1)S(1)}, bf16[2,128,256]{2,1,0:T(8,128)(2,1)S(1)}, f32[49,8,256]{2,1,0:T(8,128)S(1)}) custom-call(f32[6,8,256]{2,1,0:T(8,128)} %bitcast.12, f32[6,8,256]{2,1,0:T(8,128)} %bitcast.13, f32[6,6,8,256]{3,2,1,0:T(8,128)} %bitcast.11, ...), custom_call_target="tpu_custom_call" | custom-call | tf_op jit(solution)/shard_map/pallas_call | solution.py:354
  1.9 3.0 %collective-permute-start.1 = (bf16[2,64,256]{2,1,0:T(8,128)(2,1)S(1)}, bf16[2,64,256]{2,1,0:T(8,128)(2,1)S(1)}, u32[]{:S(2)}, u32[]{:S(2)}) collective-permute-start(bf16[2,64,256]{2,1,0:T(8,128)(2,1)S(1)} %get-tuple-element.15), channel_id=1, source_target_pairs={{0,16},{1,17},{2,18},{3,19},{4,20},{5,21},{6,22},{7,23},{8,24},{9,... | collective-permute-start | bytes 196616 | tf_op jit(solution)/shard_map/ppermute | solution.py:375
  4.9 0.1 collective-permute-start
  5.0 2.4 %collective-permute-done.1 = bf16[2,64,256]{2,1,0:T(8,128)(2,1)S(1)} collective-permute-done((bf16[2,64,256]{2,1,0:T(8,128)(2,1)S(1)}, bf16[2,64,256]{2,1,0:T(8,128)(2,1)S(1)}, u32[]{:S(2)}, u32[]{:S(2)}) %collective-permute-start.1) | collective-permute-done | bytes 65568 | tf_op jit(solution)/shard_map/ppermute | solution.py:375
  7.4 0.1 collective-permute-start.3
  7.5 0.7 %collective-permute-start.2 = (bf16[192,256]{1,0:T(8,128)(2,1)S(1)}, bf16[192,256]{1,0:T(8,128)(2,1)S(1)}, u32[]{:S(2)}, u32[]{:S(2)}) collective-permute-start(bf16[192,256]{1,0:T(8,128)(2,1)S(1)} %get-tuple-element.23), channel_id=1, source_target_pairs={{1,2},{2,1},{3,4},{4,3},{5,6},{6,5},{7,8},{8,7},{9,10},{10,9},{11,... | collective-permute-start | bytes 294920 | tf_op jit(solution)/shard_map/ppermute | solution.py:380
  8.2 3.4 %collective-permute-done.bulk_ref = bf16[400,256]{1,0:T(8,128)(2,1)S(1)} collective-permute-done((bf16[400,256]{1,0:T(8,128)(2,1)S(1)}, bf16[400,256]{1,0:T(8,128)(2,1)S(1)}, u32[]{:S(2)}, u32[]{:S(2)}) %collective-permute-start) | collective-permute-done | bytes 204832 | tf_op jit(solution)/shard_map/ppermute | solution.py:376
  11.5 0.0 collective-permute-done.3.core_ref
  11.5 0.0 collective-permute-done.2.outer_ref
  11.6 1.3 %shard_map.61 = (f32[32,1,128]{2,1,0:T(1,128)S(1)}, f32[18,8,256]{2,1,0:T(8,128)S(1)}) custom-call(f32[49,8,256]{2,1,0:T(8,128)S(1)} %get-tuple-element.11.own_ref, f32[6,8,256]{2,1,0:T(8,128)S(1)} %get-tuple-element.12.t0_ref, f32[50,8,256]{2,1,0:T(8,128)S(1)} %shard_map.60.other_ref, bf16[192,256]{1,0:T(8,128)(2,1)S(1)} %collective-permute-done.2.outer_ref, ...), custom_call_target="tpu_custom_call" | custom-call | tf_op jit(solution)/shard_map/pallas_call | solution.py:385
  12.9 15.8 %all_to_all.5.gram_ref = f32[32,1,128]{2,1,0:T(1,128)S(1)} all-to-all(f32[32,1,128]{2,1,0:T(1,128)S(1)} %get-tuple-element.16), channel_id=1, replica_groups=mesh['tor'=2,'pol'=16] {'tor','pol'}, dimensions={0} | all-to-all | bytes 32768 | tf_op jit(solution)/shard_map/all_to_all | solution.py:400
  28.7 0.9 %shard_map.62 = (f32[6,8,256]{2,1,0:T(8,128)}, f32[3]{0:T(128)}) custom-call(f32[32,1,128]{2,1,0:T(1,128)S(1)} %all_to_all.5.gram_ref, f32[18,8,256]{2,1,0:T(8,128)S(1)} %get-tuple-element.17.t_ref), custom_call_target="tpu_custom_call" | custom-call | tf_op jit(solution)/shard_map/pallas_call | solution.py:402
  (4 shorter events, 0.1 us)
Async XLA Ops:
  1.9 5.5 %collective-permute-start.1 = (bf16[2,64,256]{2,1,0:T(8,128)(2,1)S(1)}, bf16[2,64,256]{2,1,0:T(8,128)(2,1)S(1)}, u32[]{:S(2)}, u32[]{:S(2)}) collective-permute-start(bf16[2,64,256]{2,1,0:T(8,128)(2,1)S(1)} %get-tuple-element.15), channel_id=1, source_target_pairs={{0,16},{1,17},{2,18},{3,19},{4,20},{5,21},{6,22},{7,23},{8,24},{9,... | collective-permute-start | bytes 196616 | tf_op jit(solution)/shard_map/ppermute | solution.py:375
  4.9 6.6 %collective-permute-start = (bf16[400,256]{1,0:T(8,128)(2,1)S(1)}, bf16[400,256]{1,0:T(8,128)(2,1)S(1)}, u32[]{:S(2)}, u32[]{:S(2)}) collective-permute-start(bf16[400,256]{1,0:T(8,128)(2,1)S(1)} %get-tuple-element.13), channel_id=1, source_target_pairs={{0,16},{1,17},{2,18},{3,19},{4,20},{5,21},{6,22},{7,23},{8,24},{9,... | collective-permute-start | bytes 614408 | tf_op jit(solution)/shard_map/ppermute | solution.py:376
  7.4 4.1 %collective-permute-start.3 = (bf16[192,256]{1,0:T(8,128)(2,1)S(1)}, bf16[192,256]{1,0:T(8,128)(2,1)S(1)}, u32[]{:S(2)}, u32[]{:S(2)}) collective-permute-start(bf16[192,256]{1,0:T(8,128)(2,1)S(1)} %get-tuple-element.22), channel_id=1, source_target_pairs={{0,1},{1,0},{2,3},{3,2},{4,5},{5,4},{6,7},{7,6},{8,9},{9,8},{10,11... | collective-permute-start | bytes 294920 | tf_op jit(solution)/shard_map/ppermute | solution.py:379
  7.5 4.1 %collective-permute-start.2 = (bf16[192,256]{1,0:T(8,128)(2,1)S(1)}, bf16[192,256]{1,0:T(8,128)(2,1)S(1)}, u32[]{:S(2)}, u32[]{:S(2)}) collective-permute-start(bf16[192,256]{1,0:T(8,128)(2,1)S(1)} %get-tuple-element.23), channel_id=1, source_target_pairs={{1,2},{2,1},{3,4},{4,3},{5,6},{6,5},{7,8},{8,7},{9,10},{10,9},{11,... | collective-permute-start | bytes 294920 | tf_op jit(solution)/shard_map/ppermute | solution.py:380

commit v3 on v2

--- a/solution.py
+++ b/solution.py
@@ -145,57 +145,83 @@
 P_ROWS, Q_ROWS = 128, 64
 
 
-def pack_kernel(
-    plasma_ref, rhs_ref, blocks_ref, res_ref,
-    t0_ref, bulk_ref, edge_ref, side_ref, own_ref, scr_p, scr_q, blocks_in, res_in, state_in, rhs_in, sems,
+def tile_rows(value, count, first):
+    return jnp.where(first, value[0:count], value[8 - count : 8])
+
+
+def fill_slab_q(scr, deep, wide, first):
+    scr[pl.ds(Q_ROWS - 8, 8), :] = jnp.zeros((8, deep[0].shape[1]), F32)
+    for f, value in enumerate(deep):
+        scr[pl.ds(2 * f, 2), :] = tile_rows(value, 2, first)
+    for f, value in enumerate(wide):
+        scr[pl.ds(24 + f, 1), :] = tile_rows(value, 1, first)
+    return scr[...].astype(BF16)
+
+
+def fill_slab_p(scr, deep, wide, first):
+    scr[pl.ds(P_ROWS - 8, 8), :] = jnp.zeros((8, deep[0].shape[1]), F32)
+    for f, value in enumerate(deep):
+        scr[pl.ds(4 * f, 4), :] = tile_rows(value, 4, first)
+    for f, value in enumerate(wide):
+        scr[pl.ds(48 + 2 * f, 2), :] = tile_rows(value, 2, first)
+    return scr[...].astype(BF16)
+
+
+def first_kernel(
+    plasma_hbm, rhs_hbm, blocks_hbm, res_hbm,
+    t0_ref, own_ref, edge_ref, scr, sems,
 ):
     copies = [
-        pltpu.make_async_copy(rhs_ref, rhs_in, sems.at[0]),
-        pltpu.make_async_copy(plasma_ref, state_in, sems.at[1]),
-        pltpu.make_async_copy(res_ref, res_in, sems.at[2]),
-    ] + [pltpu.make_async_copy(blocks_ref.at[a], blocks_in.at[a], sems.at[3 + a]) for a in range(6)]
+        pltpu.make_async_copy(rhs_hbm, own_ref.at[pl.ds(43, 6)], sems.at[0]),
+        pltpu.make_async_copy(plasma_hbm, own_ref.at[pl.ds(37, 6)], sems.at[1]),
+        pltpu.make_async_copy(res_hbm, own_ref.at[pl.ds(36, 1)], sems.at[2]),
+    ] + [pltpu.make_async_copy(blocks_hbm.at[a], own_ref.at[pl.ds(6 * a, 6)], sems.at[3 + a]) for a in range(6)]
     for copy in copies:
         copy.start()
+    even = lax.axis_index("pol") % 2 == 0
     for copy in copies[:3]:
         copy.wait()
-    plasma_ref, rhs_ref, res_ref, blocks_ref = state_in, rhs_in, res_in, blocks_in
-    vector = [rhs_ref[b] for b in range(6)]
+    vector = [own_ref[43 + b] for b in range(6)]
     t0 = []
     for a in range(6):
         copies[3 + a].wait()
-        total = blocks_ref[a, 0] * vector[0]
+        total = own_ref[6 * a] * vector[0]
         for b in range(1, 6):
-            total = total + blocks_ref[a, b] * vector[b]
+            total = total + own_ref[6 * a + b] * vector[b]
         t0_ref[a] = total
         t0.append(total)
-    state = [plasma_ref[a] for a in range(6)]
-    deep = t0 + state
-    wide = [blocks_ref[i // 6, i % 6] for i in range(36)] + [res_ref[...]]
-    for f, value in enumerate(wide + state + vector):
-        own_ref[f] = value
+    deep = t0 + [own_ref[37 + i] for i in range(6)]
+    wide = [own_ref[i] for i in range(37)]
+    edge_ref[...] = fill_slab_q(scr, deep, wide, even)
+
+
+def pack_kernel(t0_ref, own_ref, bulk_ref, side_ref, core_ref, scr):
+    even = lax.axis_index("pol") % 2 == 0
+    deep = [t0_ref[i] for i in range(6)] + [own_ref[37 + i] for i in range(6)]
+    wide = [own_ref[i] for i in range(37)]
     fields = wide[:36] + deep + [wide[36], wide[36]]
     for g in range(25):
         pair = jnp.concatenate([fields[2 * g], fields[2 * g + 1]], axis=0)
         bulk_ref[pl.ds(16 * g, 16), :] = pair.astype(BF16)
-    zeros = jnp.zeros((8, deep[0].shape[1]), F32)
-    for side in range(2):
-        scr_p[pl.ds(P_ROWS - 8, 8), :] = zeros
-        scr_q[pl.ds(Q_ROWS - 8, 8), :] = zeros
-        for f, value in enumerate(deep):
-            scr_p[pl.ds(4 * f, 4), :] = value[0:4] if side == 0 else value[4:8]
-            scr_q[pl.ds(2 * f, 2), :] = value[0:2] if side == 0 else value[6:8]
-        for f, value in enumerate(wide):
-            scr_p[pl.ds(48 + 2 * f, 2), :] = value[0:2] if side == 0 else value[6:8]
-            scr_q[pl.ds(24 + f, 1), :] = value[0:1] if side == 0 else value[7:8]
-        side_ref[side] = scr_p[...].astype(BF16)
-        edge_ref[side] = scr_q[...].astype(BF16)
-
-
-def unpack_kernel(bulk_ref, other_ref):
+    side_ref[...] = fill_slab_p(scr, deep, wide, even)
+    core_ref[...] = fill_slab_p(scr, deep, wide, jnp.logical_not(even))
+
+
+def join_kernel(side_ref, edge_ref, slab_ref):
+    slab_ref[pl.ds(0, P_ROWS), :] = side_ref[...]
+    slab_ref[pl.ds(P_ROWS, Q_ROWS), :] = edge_ref[...]
+
+
+def unpack_kernel(bulk_ref, core_ref, other_ref, slab_ref, scr):
+    odd = lax.axis_index("pol") % 2 == 1
     for g in range(25):
         pair = bulk_ref[pl.ds(16 * g, 16), :].astype(F32)
         other_ref[2 * g] = pair[0:8]
         other_ref[2 * g + 1] = pair[8:16]
+    deep = [other_ref[36 + i] for i in range(12)]
+    wide = [other_ref[i] for i in range(36)] + [other_ref[48]]
+    slab_ref[pl.ds(0, P_ROWS), :] = core_ref[...]
+    slab_ref[pl.ds(P_ROWS, Q_ROWS), :] = fill_slab_q(scr, deep, wide, odd)
 
 
 def krylov_kernel(
@@ -347,41 +373,51 @@
 
     plasma = plasma_state.reshape(6, rows, width)
     rhs = right_side.reshape(6, rows, width)
-    res = resistivity.reshape(rows, width)
+    res = resistivity.reshape(1, rows, width)
     blocks = jacobi_blocks.reshape(6, 6, rows, width)
+    slab = P_ROWS + Q_ROWS
     vmem = pl.BlockSpec(memory_space=pltpu.VMEM)
     shape = jax.ShapeDtypeStruct
-    t0, bulk, edge, side, own = pl.pallas_call(
+    t0, own, edge = pl.pallas_call(
+        first_kernel,
+        out_shape=(
+            vmem_array((6, rows, width), F32),
+            vmem_array((49, rows, width), F32),
+            vmem_array((Q_ROWS, width), BF16),
+        ),
+        in_specs=[pl.BlockSpec(memory_space=pltpu.HBM)] * 4,
+        out_specs=(vmem,) * 3,
+        scratch_shapes=[pltpu.VMEM((Q_ROWS, width), F32), pltpu.SemaphoreType.DMA((9,))],
+    )(*map(in_hbm, (plasma, rhs, blocks, res)))
+    edge = lax.ppermute(edge, AXES, across)
+    bulk, side, core_side = pl.pallas_call(
         pack_kernel,
         out_shape=(
-            vmem_array((6, rows, width), F32),
             vmem_array((400, width), BF16),
-            vmem_array((2, Q_ROWS, width), BF16),
-            vmem_array((2, P_ROWS, width), BF16),
-            vmem_array((49, rows, width), F32),
+            vmem_array((P_ROWS, width), BF16),
+            vmem_array((P_ROWS, width), BF16),
         ),
-        in_specs=[pl.BlockSpec(memory_space=pltpu.HBM)] * 4,
-        out_specs=(vmem,) * 5,
-        scratch_shapes=[
-            pltpu.VMEM((P_ROWS, width), F32),
-            pltpu.VMEM((Q_ROWS, width), F32),
-            pltpu.VMEM((6, 6, rows, width), F32),
-            pltpu.VMEM((rows, width), F32),
-            pltpu.VMEM((6, rows, width), F32),
-            pltpu.VMEM((6, rows, width), F32),
-            pltpu.SemaphoreType.DMA((9,)),
-        ],
-    )(*map(in_hbm, (plasma, rhs, blocks, res)))
-    edge = lax.ppermute(edge, AXES, across)
+        in_specs=[vmem] * 2,
+        out_specs=(vmem,) * 3,
+        scratch_shapes=[pltpu.VMEM((P_ROWS, width), F32)],
+    )(in_vmem(t0), in_vmem(own))
     bulk = lax.ppermute(bulk, AXES, across)
-    even = lax.axis_index("pol") % 2 == 0
-    both = jnp.concatenate([side, edge], axis=1)
-    from_core = lax.ppermute(jnp.where(even, both[1], both[0]), AXES, core)
-    from_outer = lax.ppermute(jnp.where(even, both[0], both[1]), AXES, outer)
-    other = pl.pallas_call(
-        unpack_kernel, out_shape=vmem_array((50, rows, width), F32), in_specs=[vmem], out_specs=vmem
-    )(in_vmem(bulk))
-    slab = P_ROWS + Q_ROWS
+    outer_slab = pl.pallas_call(
+        join_kernel,
+        out_shape=vmem_array((slab, width), BF16),
+        in_specs=[vmem] * 2,
+        out_specs=vmem,
+        cost_estimate=pl.CostEstimate(flops=100_000_000_000, bytes_accessed=1_000_000, transcendentals=0),
+    )(in_vmem(side), in_vmem(edge))
+    from_outer = lax.ppermute(outer_slab, AXES, outer)
+    other, core_slab = pl.pallas_call(
+        unpack_kernel,
+        out_shape=(vmem_array((50, rows, width), F32), vmem_array((slab, width), BF16)),
+        in_specs=[vmem] * 2,
+        out_specs=(vmem,) * 2,
+        scratch_shapes=[pltpu.VMEM((Q_ROWS, width), F32)],
+    )(in_vmem(bulk), in_vmem(core_side))
+    from_core = lax.ppermute(core_slab, AXES, core)
     gram, tangents = pl.pallas_call(
         krylov_kernel,
         out_shape=(vmem_array((count, 1, 128), F32), vmem_array((18, rows, width), F32)),

time: 29.8 us -> 28.7 us (0.963)
  blocking collectives: 15.8 us -> 13.3 us
  waiting for transfers between devices: 5.77 us -> 7.11 us
    all_to_all x1, blocking collectives: 15.8 us -> 13.3 us  [two_planes(): gram = lax.all_to_all(gram, AXES, 0, 0, tiled=True)]
    ppermute x2, waiting for transfers between devices: 0.01 us -> 1.28 us  [the longest x1 1.28 us: two_planes(): from_core = lax.ppermute(core_slab, AXES, core)]
    ppermute x1, waiting for transfers between devices: 3.36 us -> 4.14 us  [two_planes(): bulk = lax.ppermute(bulk, AXES, across)]
    ppermute x1, waiting for transfers between devices: 2.41 us -> 1.69 us  [two_planes(): edge = lax.ppermute(edge, AXES, across)]
    pallas_call x2 -> x4, Pallas kernels: 1.26 us -> 1.35 us  [the longest x1 1.12 us: two_planes(): pl.pallas_call(first_kernel, out_shape=(vmem_array((6, rows, width), F32)...]
  transfers between devices with their start and end apart: 4 -> 4, of which waited for: 2 -> 3; matrix products, arithmetic and copies ran while one was open for 0% -> 0% of each run, Pallas kernels for 0% -> 1%
where the time goes in v3:
time: 28.7 us; the launch traced here: 28.5 us
  blocking collectives  13.3 us (46%)
  waiting for transfers between devices  7.11 us (25%)
  starting transfers between devices  3.82 us (13%)
  Pallas kernels  3.51 us (12%)
  between operations  0.68 us (2%)
    all_to_all x1, blocking collectives, two_planes(): gram = lax.all_to_all(gram, AXES, 0, 0, tiled=True)  13.3 us
    ppermute x1, waiting for transfers between devices, two_planes(): bulk = lax.ppermute(bulk, AXES, across)  4.14 us
    ppermute x1, starting transfers between devices, two_planes(): edge = lax.ppermute(edge, AXES, across)  3 us
    ppermute x1, waiting for transfers between devices, two_planes(): edge = lax.ppermute(edge, AXES, across)  1.69 us
    ppermute x1, waiting for transfers between devices, two_planes(): from_core = lax.ppermute(core_slab, AXES, core)  1.28 us
    pallas_call x1, Pallas kernels, two_planes(): pl.pallas_call(krylov_kernel, out_shape=(vmem_array((count, 1, 128), F32)...  1.27 us
    pallas_call x1, Pallas kernels, two_planes(): pl.pallas_call(first_kernel, out_shape=(vmem_array((6, rows, width), F32)...  1.12 us
    pallas_call x1, Pallas kernels, two_planes(): pl.pallas_call(functools.partial(finish_kernel, inverse_root), out_shape=...  0.89 us
  transfers between devices with their start and end apart: 4, of which 3 were waited for; matrix products, arithmetic and copies ran while one was open for 0% of the time, Pallas kernels for 1%

profile of v3, /device:TPU:0, one launch (start us, length us, event | category | flops | bytes accessed | tf_op | source)
XLA Modules:
  0.0 28.5 jit_solution(1809590308129897914)
XLA Ops:
  0.6 1.1 %shard_map.59 = (f32[6,8,256]{2,1,0:T(8,128)S(1)}, f32[49,8,256]{2,1,0:T(8,128)S(1)}, bf16[64,256]{1,0:T(8,128)(2,1)S(1)}) custom-call(f32[6,8,256]{2,1,0:T(8,128)} %bitcast.7, f32[6,8,256]{2,1,0:T(8,128)} %bitcast.8, f32[6,6,8,256]{3,2,1,0:T(8,128)} %bitcast.6, f32[1,8,256]{2,1,0:T(8,128)} %res_hbm.1), custom_call_target="tpu_custom_call" | custom-call | tf_op jit(solution)/shard_map/pallas_call | solution.py:381
  1.8 3.0 %collective-permute-start.1 = (bf16[64,256]{1,0:T(8,128)(2,1)S(1)}, bf16[64,256]{1,0:T(8,128)(2,1)S(1)}, u32[]{:S(2)}, u32[]{:S(2)}) collective-permute-start(bf16[64,256]{1,0:T(8,128)(2,1)S(1)} %get-tuple-element.20), channel_id=1, source_target_pairs={{0,16},{1,17},{2,18},{3,19},{4,20},{5,21},{6,22},{7,23},{8,24},{9,... | collective-permute-start | bytes 98312 | tf_op jit(solution)/shard_map/ppermute | solution.py:392
  4.8 0.1 shard_map.60
  4.9 0.1 collective-permute-start
  5.0 1.7 %collective-permute-done.1.edge_ref = bf16[64,256]{1,0:T(8,128)(2,1)S(1)} collective-permute-done((bf16[64,256]{1,0:T(8,128)(2,1)S(1)}, bf16[64,256]{1,0:T(8,128)(2,1)S(1)}, u32[]{:S(2)}, u32[]{:S(2)}) %collective-permute-start.1) | collective-permute-done | bytes 32800 | tf_op jit(solution)/shard_map/ppermute | solution.py:392
  6.7 0.7 %collective-permute-start.2 = (bf16[192,256]{1,0:T(8,128)(2,1)S(1)}, bf16[192,256]{1,0:T(8,128)(2,1)S(1)}, u32[]{:S(2)}, u32[]{:S(2)}) collective-permute-start(bf16[192,256]{1,0:T(8,128)(2,1)S(1)} %shard_map.62), channel_id=1, source_target_pairs={{1,2},{2,1},{3,4},{4,3},{5,6},{6,5},{7,8},{8,7},{9,10},{10,9},{11,... | collective-permute-start | bytes 294920 | tf_op jit(solution)/shard_map/ppermute | solution.py:412
  7.3 4.1 %collective-permute-done.bulk_ref = bf16[400,256]{1,0:T(8,128)(2,1)S(1)} collective-permute-done((bf16[400,256]{1,0:T(8,128)(2,1)S(1)}, bf16[400,256]{1,0:T(8,128)(2,1)S(1)}, u32[]{:S(2)}, u32[]{:S(2)}) %collective-permute-start) | collective-permute-done | bytes 204832 | tf_op jit(solution)/shard_map/ppermute | solution.py:404
  11.5 0.1 shard_map.61
  11.6 0.1 collective-permute-start.3
  11.7 0.0 collective-permute-done.2.outer_ref
  11.7 1.3 %collective-permute-done.3.core_ref = bf16[192,256]{1,0:T(8,128)(2,1)S(1)} collective-permute-done((bf16[192,256]{1,0:T(8,128)(2,1)S(1)}, bf16[192,256]{1,0:T(8,128)(2,1)S(1)}, u32[]{:S(2)}, u32[]{:S(2)}) %collective-permute-start.3) | collective-permute-done | bytes 98336 | tf_op jit(solution)/shard_map/ppermute | solution.py:420
  13.0 1.3 %shard_map.63 = (f32[32,1,128]{2,1,0:T(1,128)S(1)}, f32[18,8,256]{2,1,0:T(8,128)S(1)}) custom-call(f32[49,8,256]{2,1,0:T(8,128)S(1)} %get-tuple-element.14.own_ref, f32[6,8,256]{2,1,0:T(8,128)S(1)} %get-tuple-element.15.t0_ref, f32[50,8,256]{2,1,0:T(8,128)S(1)} %get-tuple-element.18.other_ref, bf16[192,256]{1,0:T(8,128)(2,1)S(1)} %collective-permute-done.2.outer_ref, ...), custom_call_target="tpu_custom_call" | custom-call | tf_op jit(solution)/shard_map/pallas_call | solution.py:421
  14.2 13.3 %all_to_all.5.gram_ref = f32[32,1,128]{2,1,0:T(1,128)S(1)} all-to-all(f32[32,1,128]{2,1,0:T(1,128)S(1)} %get-tuple-element.22), channel_id=1, replica_groups=mesh['tor'=2,'pol'=16] {'tor','pol'}, dimensions={0} | all-to-all | bytes 32768 | tf_op jit(solution)/shard_map/all_to_all | solution.py:436
  27.6 0.9 %shard_map.64 = (f32[6,8,256]{2,1,0:T(8,128)}, f32[3]{0:T(128)}) custom-call(f32[32,1,128]{2,1,0:T(1,128)S(1)} %all_to_all.5.gram_ref, f32[18,8,256]{2,1,0:T(8,128)S(1)} %get-tuple-element.23.t_ref), custom_call_target="tpu_custom_call" | custom-call | tf_op jit(solution)/shard_map/pallas_call | solution.py:438
  (1 shorter events, 0.0 us)
Async XLA Ops:
  1.8 4.9 %collective-permute-start.1 = (bf16[64,256]{1,0:T(8,128)(2,1)S(1)}, bf16[64,256]{1,0:T(8,128)(2,1)S(1)}, u32[]{:S(2)}, u32[]{:S(2)}) collective-permute-start(bf16[64,256]{1,0:T(8,128)(2,1)S(1)} %get-tuple-element.20), channel_id=1, source_target_pairs={{0,16},{1,17},{2,18},{3,19},{4,20},{5,21},{6,22},{7,23},{8,24},{9,... | collective-permute-start | bytes 98312 | tf_op jit(solution)/shard_map/ppermute | solution.py:392
  4.9 6.6 %collective-permute-start = (bf16[400,256]{1,0:T(8,128)(2,1)S(1)}, bf16[400,256]{1,0:T(8,128)(2,1)S(1)}, u32[]{:S(2)}, u32[]{:S(2)}) collective-permute-start(bf16[400,256]{1,0:T(8,128)(2,1)S(1)} %get-tuple-element.16), channel_id=1, source_target_pairs={{0,16},{1,17},{2,18},{3,19},{4,20},{5,21},{6,22},{7,23},{8,24},{9,... | collective-permute-start | bytes 614408 | tf_op jit(solution)/shard_map/ppermute | solution.py:404
  6.7 5.0 %collective-permute-start.2 = (bf16[192,256]{1,0:T(8,128)(2,1)S(1)}, bf16[192,256]{1,0:T(8,128)(2,1)S(1)}, u32[]{:S(2)}, u32[]{:S(2)}) collective-permute-start(bf16[192,256]{1,0:T(8,128)(2,1)S(1)} %shard_map.62), channel_id=1, source_target_pairs={{1,2},{2,1},{3,4},{4,3},{5,6},{6,5},{7,8},{8,7},{9,10},{10,9},{11,... | collective-permute-start | bytes 294920 | tf_op jit(solution)/shard_map/ppermute | solution.py:412
  11.6 1.4 %collective-permute-start.3 = (bf16[192,256]{1,0:T(8,128)(2,1)S(1)}, bf16[192,256]{1,0:T(8,128)(2,1)S(1)}, u32[]{:S(2)}, u32[]{:S(2)}) collective-permute-start(bf16[192,256]{1,0:T(8,128)(2,1)S(1)} %get-tuple-element.21), channel_id=1, source_target_pairs={{0,1},{1,0},{2,3},{3,2},{4,5},{5,4},{6,7},{7,6},{8,9},{9,8},{10,11... | collective-permute-start | bytes 294920 | tf_op jit(solution)/shard_map/ppermute | solution.py:420

commit v4 on v3

--- a/solution.py
+++ b/solution.py
@@ -195,14 +195,19 @@
     edge_ref[...] = fill_slab_q(scr, deep, wide, even)
 
 
-def pack_kernel(t0_ref, own_ref, bulk_ref, side_ref, core_ref, scr):
-    even = lax.axis_index("pol") % 2 == 0
+def bulk_kernel(t0_ref, own_ref, after_ref, bulk_ref):
     deep = [t0_ref[i] for i in range(6)] + [own_ref[37 + i] for i in range(6)]
     wide = [own_ref[i] for i in range(37)]
     fields = wide[:36] + deep + [wide[36], wide[36]]
     for g in range(25):
         pair = jnp.concatenate([fields[2 * g], fields[2 * g + 1]], axis=0)
         bulk_ref[pl.ds(16 * g, 16), :] = pair.astype(BF16)
+
+
+def pack_kernel(t0_ref, own_ref, side_ref, core_ref, scr):
+    even = lax.axis_index("pol") % 2 == 0
+    deep = [t0_ref[i] for i in range(6)] + [own_ref[37 + i] for i in range(6)]
+    wide = [own_ref[i] for i in range(37)]
     side_ref[...] = fill_slab_p(scr, deep, wide, even)
     core_ref[...] = fill_slab_p(scr, deep, wide, jnp.logical_not(even))
 
@@ -212,7 +217,7 @@
     slab_ref[pl.ds(P_ROWS, Q_ROWS), :] = edge_ref[...]
 
 
-def unpack_kernel(bulk_ref, core_ref, other_ref, slab_ref, scr):
+def unpack_kernel(bulk_ref, other_ref, slab_ref, scr):
     odd = lax.axis_index("pol") % 2 == 1
     for g in range(25):
         pair = bulk_ref[pl.ds(16 * g, 16), :].astype(F32)
@@ -220,17 +225,17 @@
         other_ref[2 * g + 1] = pair[8:16]
     deep = [other_ref[36 + i] for i in range(12)]
     wide = [other_ref[i] for i in range(36)] + [other_ref[48]]
-    slab_ref[pl.ds(0, P_ROWS), :] = core_ref[...]
-    slab_ref[pl.ds(P_ROWS, Q_ROWS), :] = fill_slab_q(scr, deep, wide, odd)
+    slab_ref[...] = fill_slab_q(scr, deep, wide, odd)
 
 
 def krylov_kernel(
-    own_ref, t0_ref, other_ref, outer_ref, core_ref,
+    own_ref, t0_ref, other_ref, outer_ref, core_p_ref, core_q_ref,
     gram_ref, t_ref, up, down, blk_p, blk_q, st_p, st_q, res_s,
 ):
     width = own_ref.shape[-1]
     even = lax.axis_index("pol") % 2 == 0
-    from_outer, from_core = outer_ref[...].astype(F32), core_ref[...].astype(F32)
+    from_outer = outer_ref[...].astype(F32)
+    from_core = jnp.concatenate([core_p_ref[...], core_q_ref[...]], axis=0).astype(F32)
     up[...] = jnp.where(even, from_outer, from_core)
     down[...] = jnp.where(even, from_core, from_outer)
     zeros = jnp.zeros((8, width), F32)
@@ -390,17 +395,17 @@
         scratch_shapes=[pltpu.VMEM((Q_ROWS, width), F32), pltpu.SemaphoreType.DMA((9,))],
     )(*map(in_hbm, (plasma, rhs, blocks, res)))
     edge = lax.ppermute(edge, AXES, across)
-    bulk, side, core_side = pl.pallas_call(
+    side, core_side = pl.pallas_call(
         pack_kernel,
-        out_shape=(
-            vmem_array((400, width), BF16),
-            vmem_array((P_ROWS, width), BF16),
-            vmem_array((P_ROWS, width), BF16),
-        ),
+        out_shape=(vmem_array((P_ROWS, width), BF16), vmem_array((P_ROWS, width), BF16)),
         in_specs=[vmem] * 2,
-        out_specs=(vmem,) * 3,
+        out_specs=(vmem,) * 2,
         scratch_shapes=[pltpu.VMEM((P_ROWS, width), F32)],
     )(in_vmem(t0), in_vmem(own))
+    core_p = lax.ppermute(core_side, AXES, core)
+    bulk = pl.pallas_call(
+        bulk_kernel, out_shape=vmem_array((400, width), BF16), in_specs=[vmem] * 3, out_specs=vmem
+    )(in_vmem(t0), in_vmem(own), in_vmem(core_p))
     bulk = lax.ppermute(bulk, AXES, across)
     outer_slab = pl.pallas_call(
         join_kernel,
@@ -412,16 +417,16 @@
     from_outer = lax.ppermute(outer_slab, AXES, outer)
     other, core_slab = pl.pallas_call(
         unpack_kernel,
-        out_shape=(vmem_array((50, rows, width), F32), vmem_array((slab, width), BF16)),
-        in_specs=[vmem] * 2,
+        out_shape=(vmem_array((50, rows, width), F32), vmem_array((Q_ROWS, width), BF16)),
+        in_specs=[vmem],
         out_specs=(vmem,) * 2,
         scratch_shapes=[pltpu.VMEM((Q_ROWS, width), F32)],
-    )(in_vmem(bulk), in_vmem(core_side))
-    from_core = lax.ppermute(core_slab, AXES, core)
+    )(in_vmem(bulk))
+    core_q = lax.ppermute(core_slab, AXES, core)
     gram, tangents = pl.pallas_call(
         krylov_kernel,
         out_shape=(vmem_array((count, 1, 128), F32), vmem_array((18, rows, width), F32)),
-        in_specs=[vmem] * 5,
+        in_specs=[vmem] * 6,
         out_specs=(vmem,) * 2,
         scratch_shapes=[
             pltpu.VMEM((slab, width), F32),
@@ -432,7 +437,7 @@
             pltpu.VMEM((12, 16, width), F32),
             pltpu.VMEM((2, 16, width), F32),
         ],
-    )(*map(in_vmem, (own, t0, other, from_outer, from_core)))
+    )(*map(in_vmem, (own, t0, other, from_outer, core_p, core_q)))
     gram = lax.all_to_all(gram, AXES, 0, 0, tiled=True)
     inverse_root = float((6.0 * count * rows * width) ** -0.5)
     update, estimates = pl.pallas_call(

time: 28.7 us -> 28.5 us (level)
  starting transfers between devices: 3.82 us -> 5.05 us
  blocking collectives: 13.3 us -> 12.6 us
  waiting for transfers between devices: 7.11 us -> 6.48 us
    ppermute x1, starting transfers between devices: 0.08 us -> 1.24 us  [two_planes(): bulk = lax.ppermute(bulk, AXES, across)]
    ppermute x1, waiting for transfers between devices: 1.69 us -> 0.72 us  [two_planes(): edge = lax.ppermute(edge, AXES, across)]
    all_to_all x1, blocking collectives: 13.3 us -> 12.6 us  [two_planes(): gram = lax.all_to_all(gram, AXES, 0, 0, tiled=True)]
    ppermute x1 -> x2, starting transfers between devices: 0.07 us -> 0.59 us  [the longest x1 0.52 us: two_planes(): core_p = lax.ppermute(core_side, AXES, core)]
    ppermute x1, starting transfers between devices: 3 us -> 2.56 us  [two_planes(): edge = lax.ppermute(edge, AXES, across)]
    ppermute x1, waiting for transfers between devices: 4.14 us -> 4.57 us  [two_planes(): bulk = lax.ppermute(bulk, AXES, across)]
    ppermute x1 -> x2, waiting for transfers between devices: 1.28 us -> 1.19 us  [the longest x1 1.18 us: two_planes(): core_q = lax.ppermute(core_slab, AXES, core)]
  transfers between devices with their start and end apart: 4 -> 5, of which waited for: 3 -> 3; matrix products, arithmetic and copies ran while one was open for 0% -> 0% of each run, Pallas kernels for 1% -> 0%
where the time goes in v4:
time: 28.5 us; the launch traced here: 28.3 us
  blocking collectives  12.6 us (44%)
  waiting for transfers between devices  6.48 us (23%)
  starting transfers between devices  5.05 us (18%)
  Pallas kernels  3.49 us (12%)
  between operations  0.68 us (2%)
    all_to_all x1, blocking collectives, two_planes(): gram = lax.all_to_all(gram, AXES, 0, 0, tiled=True)  12.6 us
    ppermute x1, waiting for transfers between devices, two_planes(): bulk = lax.ppermute(bulk, AXES, across)  4.57 us
    ppermute x1, starting transfers between devices, two_planes(): edge = lax.ppermute(edge, AXES, across)  2.56 us
    pallas_call x1, Pallas kernels, two_planes(): pl.pallas_call(krylov_kernel, out_shape=(vmem_array((count, 1, 128), F32)...  1.25 us
    ppermute x1, starting transfers between devices, two_planes(): bulk = lax.ppermute(bulk, AXES, across)  1.24 us
    ppermute x1, waiting for transfers between devices, two_planes(): core_q = lax.ppermute(core_slab, AXES, core)  1.18 us
    pallas_call x1, Pallas kernels, two_planes(): pl.pallas_call(first_kernel, out_shape=(vmem_array((6, rows, width), F32)...  1.12 us
    pallas_call x1, Pallas kernels, two_planes(): pl.pallas_call(functools.partial(finish_kernel, inverse_root), out_shape=...  0.89 us
  transfers between devices with their start and end apart: 5, of which 3 were waited for; matrix products, arithmetic and copies ran while one was open for 0% of the time, Pallas kernels for 0%

profile of v4, /device:TPU:0, one launch (start us, length us, event | category | flops | bytes accessed | tf_op | source)
XLA Modules:
  0.0 28.3 jit_solution(3711858781598805474)
XLA Ops:
  0.6 1.1 %shard_map.59 = (f32[6,8,256]{2,1,0:T(8,128)S(1)}, f32[49,8,256]{2,1,0:T(8,128)S(1)}, bf16[64,256]{1,0:T(8,128)(2,1)S(1)}) custom-call(f32[6,8,256]{2,1,0:T(8,128)} %bitcast.7, f32[6,8,256]{2,1,0:T(8,128)} %bitcast.8, f32[6,6,8,256]{3,2,1,0:T(8,128)} %bitcast.6, f32[1,8,256]{2,1,0:T(8,128)} %res_hbm.1), custom_call_target="tpu_custom_call" | custom-call | tf_op jit(solution)/shard_map/pallas_call | solution.py:386
  1.8 0.1 shard_map.60
  1.9 0.5 %collective-permute-start = (bf16[128,256]{1,0:T(8,128)(2,1)S(1)}, bf16[128,256]{1,0:T(8,128)(2,1)S(1)}, u32[]{:S(2)}, u32[]{:S(2)}) collective-permute-start(bf16[128,256]{1,0:T(8,128)(2,1)S(1)} %get-tuple-element.15), channel_id=1, source_target_pairs={{0,1},{1,0},{2,3},{3,2},{4,5},{5,4},{6,7},{7,6},{8,9},{9,8},{10,11... | collective-permute-start | bytes 196616 | tf_op jit(solution)/shard_map/ppermute | solution.py:405
  2.4 2.6 %collective-permute-start.2 = (bf16[64,256]{1,0:T(8,128)(2,1)S(1)}, bf16[64,256]{1,0:T(8,128)(2,1)S(1)}, u32[]{:S(2)}, u32[]{:S(2)}) collective-permute-start(bf16[64,256]{1,0:T(8,128)(2,1)S(1)} %get-tuple-element.18), channel_id=1, source_target_pairs={{0,16},{1,17},{2,18},{3,19},{4,20},{5,21},{6,22},{7,23},{8,24},{9,... | collective-permute-start | bytes 98312 | tf_op jit(solution)/shard_map/ppermute | solution.py:397
  5.0 0.0 collective-permute-done.after_ref.core_p_ref
  5.0 1.2 %collective-permute-start.1 = (bf16[400,256]{1,0:T(8,128)(2,1)S(1)}, bf16[400,256]{1,0:T(8,128)(2,1)S(1)}, u32[]{:S(2)}, u32[]{:S(2)}) collective-permute-start(bf16[400,256]{1,0:T(8,128)(2,1)S(1)} %shard_map.61), channel_id=1, source_target_pairs={{0,16},{1,17},{2,18},{3,19},{4,20},{5,21},{6,22},{7,23},{8,24},{9,... | collective-permute-start | bytes 614408 | tf_op jit(solution)/shard_map/ppermute | solution.py:409
  6.2 0.7 %collective-permute-done.2.edge_ref = bf16[64,256]{1,0:T(8,128)(2,1)S(1)} collective-permute-done((bf16[64,256]{1,0:T(8,128)(2,1)S(1)}, bf16[64,256]{1,0:T(8,128)(2,1)S(1)}, u32[]{:S(2)}, u32[]{:S(2)}) %collective-permute-start.2) | collective-permute-done | bytes 32800 | tf_op jit(solution)/shard_map/ppermute | solution.py:397
  6.9 0.7 %collective-permute-start.3 = (bf16[192,256]{1,0:T(8,128)(2,1)S(1)}, bf16[192,256]{1,0:T(8,128)(2,1)S(1)}, u32[]{:S(2)}, u32[]{:S(2)}) collective-permute-start(bf16[192,256]{1,0:T(8,128)(2,1)S(1)} %shard_map.63), channel_id=1, source_target_pairs={{1,2},{2,1},{3,4},{4,3},{5,6},{6,5},{7,8},{8,7},{9,10},{10,9},{11,... | collective-permute-start | bytes 294920 | tf_op jit(solution)/shard_map/ppermute | solution.py:417
  7.6 4.6 %collective-permute-done.1.bulk_ref = bf16[400,256]{1,0:T(8,128)(2,1)S(1)} collective-permute-done((bf16[400,256]{1,0:T(8,128)(2,1)S(1)}, bf16[400,256]{1,0:T(8,128)(2,1)S(1)}, u32[]{:S(2)}, u32[]{:S(2)}) %collective-permute-start.1) | collective-permute-done | bytes 204832 | tf_op jit(solution)/shard_map/ppermute | solution.py:409
  12.2 0.1 shard_map.62
  12.3 0.1 collective-permute-start.4
  12.4 0.0 collective-permute-done.3.outer_ref
  12.4 1.2 %collective-permute-done.4.core_q_ref = bf16[64,256]{1,0:T(8,128)(2,1)S(1)} collective-permute-done((bf16[64,256]{1,0:T(8,128)(2,1)S(1)}, bf16[64,256]{1,0:T(8,128)(2,1)S(1)}, u32[]{:S(2)}, u32[]{:S(2)}) %collective-permute-start.4) | collective-permute-done | bytes 32800 | tf_op jit(solution)/shard_map/ppermute | solution.py:425
  13.6 1.2 %shard_map.64 = (f32[32,1,128]{2,1,0:T(1,128)S(1)}, f32[18,8,256]{2,1,0:T(8,128)S(1)}) custom-call(f32[49,8,256]{2,1,0:T(8,128)S(1)} %get-tuple-element.13.own_ref, f32[6,8,256]{2,1,0:T(8,128)S(1)} %get-tuple-element.14.t0_ref, f32[50,8,256]{2,1,0:T(8,128)S(1)} %get-tuple-element.16.other_ref, bf16[192,256]{1,0:T(8,128)(2,1)S(1)} %collective-permute-done.3.outer_ref, ...), custom_call_target="tpu_custom_call" | custom-call | tf_op jit(solution)/shard_map/pallas_call | solution.py:426
  14.8 12.6 %all_to_all.5.gram_ref = f32[32,1,128]{2,1,0:T(1,128)S(1)} all-to-all(f32[32,1,128]{2,1,0:T(1,128)S(1)} %get-tuple-element.20), channel_id=1, replica_groups=mesh['tor'=2,'pol'=16] {'tor','pol'}, dimensions={0} | all-to-all | bytes 32768 | tf_op jit(solution)/shard_map/all_to_all | solution.py:441
  27.4 0.9 %shard_map.65 = (f32[6,8,256]{2,1,0:T(8,128)}, f32[3]{0:T(128)}) custom-call(f32[32,1,128]{2,1,0:T(1,128)S(1)} %all_to_all.5.gram_ref, f32[18,8,256]{2,1,0:T(8,128)S(1)} %get-tuple-element.21.t_ref), custom_call_target="tpu_custom_call" | custom-call | tf_op jit(solution)/shard_map/pallas_call | solution.py:443
  (2 shorter events, 0.0 us)
Async XLA Ops:
  1.9 3.1 %collective-permute-start = (bf16[128,256]{1,0:T(8,128)(2,1)S(1)}, bf16[128,256]{1,0:T(8,128)(2,1)S(1)}, u32[]{:S(2)}, u32[]{:S(2)}) collective-permute-start(bf16[128,256]{1,0:T(8,128)(2,1)S(1)} %get-tuple-element.15), channel_id=1, source_target_pairs={{0,1},{1,0},{2,3},{3,2},{4,5},{5,4},{6,7},{7,6},{8,9},{9,8},{10,11... | collective-permute-start | bytes 196616 | tf_op jit(solution)/shard_map/ppermute | solution.py:405
  2.4 4.5 %collective-permute-start.2 = (bf16[64,256]{1,0:T(8,128)(2,1)S(1)}, bf16[64,256]{1,0:T(8,128)(2,1)S(1)}, u32[]{:S(2)}, u32[]{:S(2)}) collective-permute-start(bf16[64,256]{1,0:T(8,128)(2,1)S(1)} %get-tuple-element.18), channel_id=1, source_target_pairs={{0,16},{1,17},{2,18},{3,19},{4,20},{5,21},{6,22},{7,23},{8,24},{9,... | collective-permute-start | bytes 98312 | tf_op jit(solution)/shard_map/ppermute | solution.py:397
  5.0 7.2 %collective-permute-start.1 = (bf16[400,256]{1,0:T(8,128)(2,1)S(1)}, bf16[400,256]{1,0:T(8,128)(2,1)S(1)}, u32[]{:S(2)}, u32[]{:S(2)}) collective-permute-start(bf16[400,256]{1,0:T(8,128)(2,1)S(1)} %shard_map.61), channel_id=1, source_target_pairs={{0,16},{1,17},{2,18},{3,19},{4,20},{5,21},{6,22},{7,23},{8,24},{9,... | collective-permute-start | bytes 614408 | tf_op jit(solution)/shard_map/ppermute | solution.py:409
  6.9 5.4 %collective-permute-start.3 = (bf16[192,256]{1,0:T(8,128)(2,1)S(1)}, bf16[192,256]{1,0:T(8,128)(2,1)S(1)}, u32[]{:S(2)}, u32[]{:S(2)}) collective-permute-start(bf16[192,256]{1,0:T(8,128)(2,1)S(1)} %shard_map.63), channel_id=1, source_target_pairs={{1,2},{2,1},{3,4},{4,3},{5,6},{6,5},{7,8},{8,7},{9,10},{10,9},{11,... | collective-permute-start | bytes 294920 | tf_op jit(solution)/shard_map/ppermute | solution.py:417
  12.3 1.3 %collective-permute-start.4 = (bf16[64,256]{1,0:T(8,128)(2,1)S(1)}, bf16[64,256]{1,0:T(8,128)(2,1)S(1)}, u32[]{:S(2)}, u32[]{:S(2)}) collective-permute-start(bf16[64,256]{1,0:T(8,128)(2,1)S(1)} %get-tuple-element.19), channel_id=1, source_target_pairs={{0,1},{1,0},{2,3},{3,2},{4,5},{5,4},{6,7},{7,6},{8,9},{9,8},{10,11... | collective-permute-start | bytes 98312 | tf_op jit(solution)/shard_map/ppermute | solution.py:425

commit v5 on v4

--- a/solution.py
+++ b/solution.py
@@ -169,7 +169,7 @@
 
 def first_kernel(
     plasma_hbm, rhs_hbm, blocks_hbm, res_hbm,
-    t0_ref, own_ref, edge_ref, scr, sems,
+    t0_ref, own_ref, bulk_ref, edge_ref, inner_ref, scr, sems,
 ):
     copies = [
         pltpu.make_async_copy(rhs_hbm, own_ref.at[pl.ds(43, 6)], sems.at[0]),
@@ -192,16 +192,12 @@
         t0.append(total)
     deep = t0 + [own_ref[37 + i] for i in range(6)]
     wide = [own_ref[i] for i in range(37)]
-    edge_ref[...] = fill_slab_q(scr, deep, wide, even)
-
-
-def bulk_kernel(t0_ref, own_ref, after_ref, bulk_ref):
-    deep = [t0_ref[i] for i in range(6)] + [own_ref[37 + i] for i in range(6)]
-    wide = [own_ref[i] for i in range(37)]
     fields = wide[:36] + deep + [wide[36], wide[36]]
     for g in range(25):
         pair = jnp.concatenate([fields[2 * g], fields[2 * g + 1]], axis=0)
         bulk_ref[pl.ds(16 * g, 16), :] = pair.astype(BF16)
+    edge_ref[...] = fill_slab_q(scr, deep, wide, even)
+    inner_ref[...] = fill_slab_q(scr, deep, wide, jnp.logical_not(even))
 
 
 def pack_kernel(t0_ref, own_ref, side_ref, core_ref, scr):
@@ -212,30 +208,17 @@
     core_ref[...] = fill_slab_p(scr, deep, wide, jnp.logical_not(even))
 
 
-def join_kernel(side_ref, edge_ref, slab_ref):
-    slab_ref[pl.ds(0, P_ROWS), :] = side_ref[...]
-    slab_ref[pl.ds(P_ROWS, Q_ROWS), :] = edge_ref[...]
-
-
-def unpack_kernel(bulk_ref, other_ref, slab_ref, scr):
-    odd = lax.axis_index("pol") % 2 == 1
-    for g in range(25):
-        pair = bulk_ref[pl.ds(16 * g, 16), :].astype(F32)
-        other_ref[2 * g] = pair[0:8]
-        other_ref[2 * g + 1] = pair[8:16]
-    deep = [other_ref[36 + i] for i in range(12)]
-    wide = [other_ref[i] for i in range(36)] + [other_ref[48]]
-    slab_ref[...] = fill_slab_q(scr, deep, wide, odd)
-
-
 def krylov_kernel(
-    own_ref, t0_ref, other_ref, outer_ref, core_p_ref, core_q_ref,
+    own_ref, t0_ref, bulk_ref, outer_p_ref, outer_q_ref, core_p_ref, core_q_ref,
     gram_ref, t_ref, up, down, blk_p, blk_q, st_p, st_q, res_s,
 ):
     width = own_ref.shape[-1]
     even = lax.axis_index("pol") % 2 == 0
-    from_outer = outer_ref[...].astype(F32)
+    from_outer = jnp.concatenate([outer_p_ref[...], outer_q_ref[...]], axis=0).astype(F32)
     from_core = jnp.concatenate([core_p_ref[...], core_q_ref[...]], axis=0).astype(F32)
+    place = lax.axis_index("pol")
+    edge = jnp.logical_or(place == 0, place == lax.axis_size("pol") - 1)
+    from_outer = jnp.where(edge, 0.0, from_outer)
     up[...] = jnp.where(even, from_outer, from_core)
     down[...] = jnp.where(even, from_core, from_outer)
     zeros = jnp.zeros((8, width), F32)
@@ -247,7 +230,8 @@
         ref[at, 16 - rows : 16] = up[pl.ds(offset, rows), :]
 
     def other(field):
-        return other_ref[field]
+        pair = bulk_ref[pl.ds(16 * (field // 2), 16), :].astype(F32)
+        return pair[0:8] if field % 2 == 0 else pair[8:16]
 
     for i in range(36):
         blk_p[i, 0:8] = own_ref[i]
@@ -364,17 +348,17 @@
     count = 2 * pol
 
     def pairs(partner):
-        out = []
-        for t in range(2):
-            for p in range(pol):
-                other = partner(t, p)
-                if 0 <= other[1] < pol:
-                    out.append((t * pol + p, other[0] * pol + other[1]))
-        return out
+        return [(t * pol + p, q * pol + r) for t in range(2) for p in range(pol) for q, r in [partner(t, p)]]
+
+    def beyond(t, p, far):
+        r = p - 1 if p % 2 == 0 else p + 1
+        return (far, r) if 0 <= r < pol else (1 - t, p)
 
     across = pairs(lambda t, p: (1 - t, p))
     core = pairs(lambda t, p: (t, p ^ 1))
-    outer = pairs(lambda t, p: (t, p - 1 if p % 2 == 0 else p + 1))
+    outer = pairs(lambda t, p: beyond(t, p, t))
+    corner = pairs(lambda t, p: beyond(t, p, 1 - t))
+    across_core = pairs(lambda t, p: (1 - t, p ^ 1))
 
     plasma = plasma_state.reshape(6, rows, width)
     rhs = right_side.reshape(6, rows, width)
@@ -383,18 +367,21 @@
     slab = P_ROWS + Q_ROWS
     vmem = pl.BlockSpec(memory_space=pltpu.VMEM)
     shape = jax.ShapeDtypeStruct
-    t0, own, edge = pl.pallas_call(
+    t0, own, bulk, edge, inner = pl.pallas_call(
         first_kernel,
         out_shape=(
             vmem_array((6, rows, width), F32),
             vmem_array((49, rows, width), F32),
+            vmem_array((400, width), BF16),
+            vmem_array((Q_ROWS, width), BF16),
             vmem_array((Q_ROWS, width), BF16),
         ),
         in_specs=[pl.BlockSpec(memory_space=pltpu.HBM)] * 4,
-        out_specs=(vmem,) * 3,
+        out_specs=(vmem,) * 5,
         scratch_shapes=[pltpu.VMEM((Q_ROWS, width), F32), pltpu.SemaphoreType.DMA((9,))],
     )(*map(in_hbm, (plasma, rhs, blocks, res)))
-    edge = lax.ppermute(edge, AXES, across)
+    bulk = lax.ppermute(bulk, AXES, across)
+    outer_q = lax.ppermute(edge, AXES, corner)
     side, core_side = pl.pallas_call(
         pack_kernel,
         out_shape=(vmem_array((P_ROWS, width), BF16), vmem_array((P_ROWS, width), BF16)),
@@ -402,31 +389,13 @@
         out_specs=(vmem,) * 2,
         scratch_shapes=[pltpu.VMEM((P_ROWS, width), F32)],
     )(in_vmem(t0), in_vmem(own))
+    outer_p = lax.ppermute(side, AXES, outer)
+    core_q = lax.ppermute(inner, AXES, across_core)
     core_p = lax.ppermute(core_side, AXES, core)
-    bulk = pl.pallas_call(
-        bulk_kernel, out_shape=vmem_array((400, width), BF16), in_specs=[vmem] * 3, out_specs=vmem
-    )(in_vmem(t0), in_vmem(own), in_vmem(core_p))
-    bulk = lax.ppermute(bulk, AXES, across)
-    outer_slab = pl.pallas_call(
-        join_kernel,
-        out_shape=vmem_array((slab, width), BF16),
-        in_specs=[vmem] * 2,
-        out_specs=vmem,
-        cost_estimate=pl.CostEstimate(flops=100_000_000_000, bytes_accessed=1_000_000, transcendentals=0),
-    )(in_vmem(side), in_vmem(edge))
-    from_outer = lax.ppermute(outer_slab, AXES, outer)
-    other, core_slab = pl.pallas_call(
-        unpack_kernel,
-        out_shape=(vmem_array((50, rows, width), F32), vmem_array((Q_ROWS, width), BF16)),
-        in_specs=[vmem],
-        out_specs=(vmem,) * 2,
-        scratch_shapes=[pltpu.VMEM((Q_ROWS, width), F32)],
-    )(in_vmem(bulk))
-    core_q = lax.ppermute(core_slab, AXES, core)
     gram, tangents = pl.pallas_call(
         krylov_kernel,
         out_shape=(vmem_array((count, 1, 128), F32), vmem_array((18, rows, width), F32)),
-        in_specs=[vmem] * 6,
+        in_specs=[vmem] * 7,
         out_specs=(vmem,) * 2,
         scratch_shapes=[
             pltpu.VMEM((slab, width), F32),
@@ -437,7 +406,7 @@
             pltpu.VMEM((12, 16, width), F32),
             pltpu.VMEM((2, 16, width), F32),
         ],
-    )(*map(in_vmem, (own, t0, other, from_outer, core_p, core_q)))
+    )(*map(in_vmem, (own, t0, bulk, outer_p, outer_q, core_p, core_q)))
     gram = lax.all_to_all(gram, AXES, 0, 0, tiled=True)
     inverse_root = float((6.0 * count * rows * width) ** -0.5)
     update, estimates = pl.pallas_call(

time: 28.5 us -> 27.3 us (0.958)
  waiting for transfers between devices: 6.48 us -> 2.95 us
  starting transfers between devices: 5.05 us -> 7.4 us
    ppermute x1, waiting for transfers between devices: 4.57 us -> 0.01 us  [two_planes(): bulk = lax.ppermute(bulk, AXES, across)]
    ppermute x1, starting transfers between devices: 1.24 us -> 3 us  [two_planes(): bulk = lax.ppermute(bulk, AXES, across)]
    ppermute x1, starting transfers between devices: 0.52 us -> 1.62 us  [two_planes(): core_p = lax.ppermute(core_side, AXES, core)]
    ppermute x3, waiting for transfers between devices: 1.9 us -> 2.95 us  [the longest x1 1.93 us: two_planes(): outer_q = lax.ppermute(edge, AXES, corner)]
    ppermute x3, starting transfers between devices: 3.3 us -> 2.78 us  [the longest x1 2.17 us: two_planes(): core_q = lax.ppermute(inner, AXES, across_core)]
  transfers between devices with their start and end apart: 5 -> 5, of which waited for: 3 -> 2; matrix products, arithmetic and copies ran while one was open for 0% -> 0% of each run, Pallas kernels for 0% -> 0%
where the time goes in v5:
time: 27.3 us; the launch traced here: 27.1 us
  blocking collectives  12.7 us (47%)
  starting transfers between devices  7.4 us (27%)
  Pallas kernels  3.44 us (13%)
  waiting for transfers between devices  2.95 us (11%)
  between operations  0.66 us (2%)
    all_to_all x1, blocking collectives, two_planes(): gram = lax.all_to_all(gram, AXES, 0, 0, tiled=True)  12.7 us
    ppermute x1, starting transfers between devices, two_planes(): bulk = lax.ppermute(bulk, AXES, across)  3 us
    ppermute x1, starting transfers between devices, two_planes(): core_q = lax.ppermute(inner, AXES, across_core)  2.17 us
    ppermute x1, waiting for transfers between devices, two_planes(): outer_q = lax.ppermute(edge, AXES, corner)  1.93 us
    ppermute x1, starting transfers between devices, two_planes(): core_p = lax.ppermute(core_side, AXES, core)  1.62 us
    pallas_call x1, Pallas kernels, two_planes(): pl.pallas_call(krylov_kernel, out_shape=(vmem_array((count, 1, 128), F32)...  1.24 us
    pallas_call x1, Pallas kernels, two_planes(): pl.pallas_call(first_kernel, out_shape=(vmem_array((6, rows, width), F32)...  1.19 us
    ppermute x1, waiting for transfers between devices, two_planes(): core_q = lax.ppermute(inner, AXES, across_core)  1.01 us
  transfers between devices with their start and end apart: 5, of which 2 were waited for; matrix products, arithmetic and copies ran while one was open for 0% of the time, Pallas kernels for 0%

profile of v5, /device:TPU:0, one launch (start us, length us, event | category | flops | bytes accessed | tf_op | source)
XLA Modules:
  0.0 27.1 jit_solution(13689464028339227422)
XLA Ops:
  0.6 1.2 %shard_map.59 = (f32[6,8,256]{2,1,0:T(8,128)S(1)}, f32[49,8,256]{2,1,0:T(8,128)S(1)}, bf16[400,256]{1,0:T(8,128)(2,1)S(1)}, bf16[64,256]{1,0:T(8,128)(2,1)S(1)}, bf16[64,256]{1,0:T(8,128)(2,1)S(1)}) custom-call(f32[6,8,256]{2,1,0:T(8,128)} %bitcast.7, f32[6,8,256]{2,1,0:T(8,128)} %bitcast.8, f32[6,6,8,256]{3,2,1,0:T(8,128)} %bitcast.6, f32[1,8,256]{2,1,0:T(8,128)} %res_hbm.1), custom_call_target="tpu_custom_call" | custom-call | tf_op jit(solution)/shard_map/pallas_call | solution.py:370
  1.8 3.0 %collective-permute-start = (bf16[400,256]{1,0:T(8,128)(2,1)S(1)}, bf16[400,256]{1,0:T(8,128)(2,1)S(1)}, u32[]{:S(2)}, u32[]{:S(2)}) collective-permute-start(bf16[400,256]{1,0:T(8,128)(2,1)S(1)} %get-tuple-element.15), channel_id=1, source_target_pairs={{0,16},{1,17},{2,18},{3,19},{4,20},{5,21},{6,22},{7,23},{8,24},{9,... | collective-permute-start | bytes 614408 | tf_op jit(solution)/shard_map/ppermute | solution.py:383
  4.8 0.1 shard_map.60
  4.9 0.1 collective-permute-start.1
  5.0 1.6 %collective-permute-start.3 = (bf16[128,256]{1,0:T(8,128)(2,1)S(1)}, bf16[128,256]{1,0:T(8,128)(2,1)S(1)}, u32[]{:S(2)}, u32[]{:S(2)}) collective-permute-start(bf16[128,256]{1,0:T(8,128)(2,1)S(1)} %get-tuple-element.18), channel_id=1, source_target_pairs={{0,1},{1,0},{2,3},{3,2},{4,5},{5,4},{6,7},{7,6},{8,9},{9,8},{10,11... | collective-permute-start | bytes 196616 | tf_op jit(solution)/shard_map/ppermute | solution.py:394
  6.6 0.5 %collective-permute-start.2 = (bf16[64,256]{1,0:T(8,128)(2,1)S(1)}, bf16[64,256]{1,0:T(8,128)(2,1)S(1)}, u32[]{:S(2)}, u32[]{:S(2)}) collective-permute-start(bf16[64,256]{1,0:T(8,128)(2,1)S(1)} %get-tuple-element.17), channel_id=1, source_target_pairs={{0,16},{1,18},{2,17},{3,20},{4,19},{5,22},{6,21},{7,24},{8,23},{9,... | collective-permute-start | bytes 98312 | tf_op jit(solution)/shard_map/ppermute | solution.py:384
  7.2 2.2 %collective-permute-start.4 = (bf16[64,256]{1,0:T(8,128)(2,1)S(1)}, bf16[64,256]{1,0:T(8,128)(2,1)S(1)}, u32[]{:S(2)}, u32[]{:S(2)}) collective-permute-start(bf16[64,256]{1,0:T(8,128)(2,1)S(1)} %get-tuple-element.19), channel_id=1, source_target_pairs={{0,17},{1,16},{2,19},{3,18},{4,21},{5,20},{6,23},{7,22},{8,25},{9,... | collective-permute-start | bytes 98312 | tf_op jit(solution)/shard_map/ppermute | solution.py:393
  9.3 1.9 %collective-permute-done.2.outer_q_ref = bf16[64,256]{1,0:T(8,128)(2,1)S(1)} collective-permute-done((bf16[64,256]{1,0:T(8,128)(2,1)S(1)}, bf16[64,256]{1,0:T(8,128)(2,1)S(1)}, u32[]{:S(2)}, u32[]{:S(2)}) %collective-permute-start.2) | collective-permute-done | bytes 32800 | tf_op jit(solution)/shard_map/ppermute | solution.py:384
  11.3 1.0 %collective-permute-done.4.core_q_ref = bf16[64,256]{1,0:T(8,128)(2,1)S(1)} collective-permute-done((bf16[64,256]{1,0:T(8,128)(2,1)S(1)}, bf16[64,256]{1,0:T(8,128)(2,1)S(1)}, u32[]{:S(2)}, u32[]{:S(2)}) %collective-permute-start.4) | collective-permute-done | bytes 32800 | tf_op jit(solution)/shard_map/ppermute | solution.py:393
  12.3 0.0 collective-permute-done.1.outer_p_ref
  12.3 0.0 collective-permute-done.3.core_p_ref
  12.3 0.0 collective-permute-done.bulk_ref
  12.3 1.2 %shard_map.61 = (f32[32,1,128]{2,1,0:T(1,128)S(1)}, f32[18,8,256]{2,1,0:T(8,128)S(1)}) custom-call(f32[49,8,256]{2,1,0:T(8,128)S(1)} %get-tuple-element.13.own_ref, f32[6,8,256]{2,1,0:T(8,128)S(1)} %get-tuple-element.14.t0_ref, bf16[400,256]{1,0:T(8,128)(2,1)S(1)} %collective-permute-done.bulk_ref, bf16[128,256]{1,0:T(8,128)(2,1)S(1)} %collective-permute-done.1.outer_p_ref, ...), custom_call_target="tpu_custom_call" | custom-call | tf_op jit(solution)/shard_map/pallas_call | solution.py:395
  13.6 12.7 %all_to_all.5.gram_ref = f32[32,1,128]{2,1,0:T(1,128)S(1)} all-to-all(f32[32,1,128]{2,1,0:T(1,128)S(1)} %get-tuple-element.20), channel_id=1, replica_groups=mesh['tor'=2,'pol'=16] {'tor','pol'}, dimensions={0} | all-to-all | bytes 32768 | tf_op jit(solution)/shard_map/all_to_all | solution.py:410
  26.2 0.9 %shard_map.62 = (f32[6,8,256]{2,1,0:T(8,128)}, f32[3]{0:T(128)}) custom-call(f32[32,1,128]{2,1,0:T(1,128)S(1)} %all_to_all.5.gram_ref, f32[18,8,256]{2,1,0:T(8,128)S(1)} %get-tuple-element.21.t_ref), custom_call_target="tpu_custom_call" | custom-call | tf_op jit(solution)/shard_map/pallas_call | solution.py:412
Async XLA Ops:
  1.8 10.5 %collective-permute-start = (bf16[400,256]{1,0:T(8,128)(2,1)S(1)}, bf16[400,256]{1,0:T(8,128)(2,1)S(1)}, u32[]{:S(2)}, u32[]{:S(2)}) collective-permute-start(bf16[400,256]{1,0:T(8,128)(2,1)S(1)} %get-tuple-element.15), channel_id=1, source_target_pairs={{0,16},{1,17},{2,18},{3,19},{4,20},{5,21},{6,22},{7,23},{8,24},{9,... | collective-permute-start | bytes 614408 | tf_op jit(solution)/shard_map/ppermute | solution.py:383
  4.9 7.4 %collective-permute-start.1 = (bf16[128,256]{1,0:T(8,128)(2,1)S(1)}, bf16[128,256]{1,0:T(8,128)(2,1)S(1)}, u32[]{:S(2)}, u32[]{:S(2)}) collective-permute-start(bf16[128,256]{1,0:T(8,128)(2,1)S(1)} %get-tuple-element.16), channel_id=1, source_target_pairs={{0,16},{1,2},{2,1},{3,4},{4,3},{5,6},{6,5},{7,8},{8,7},{9,10},{10,... | collective-permute-start | bytes 196616 | tf_op jit(solution)/shard_map/ppermute | solution.py:392
  5.0 7.3 %collective-permute-start.3 = (bf16[128,256]{1,0:T(8,128)(2,1)S(1)}, bf16[128,256]{1,0:T(8,128)(2,1)S(1)}, u32[]{:S(2)}, u32[]{:S(2)}) collective-permute-start(bf16[128,256]{1,0:T(8,128)(2,1)S(1)} %get-tuple-element.18), channel_id=1, source_target_pairs={{0,1},{1,0},{2,3},{3,2},{4,5},{5,4},{6,7},{7,6},{8,9},{9,8},{10,11... | collective-permute-start | bytes 196616 | tf_op jit(solution)/shard_map/ppermute | solution.py:394
  6.6 4.6 %collective-permute-start.2 = (bf16[64,256]{1,0:T(8,128)(2,1)S(1)}, bf16[64,256]{1,0:T(8,128)(2,1)S(1)}, u32[]{:S(2)}, u32[]{:S(2)}) collective-permute-start(bf16[64,256]{1,0:T(8,128)(2,1)S(1)} %get-tuple-element.17), channel_id=1, source_target_pairs={{0,16},{1,18},{2,17},{3,20},{4,19},{5,22},{6,21},{7,24},{8,23},{9,... | collective-permute-start | bytes 98312 | tf_op jit(solution)/shard_map/ppermute | solution.py:384
  7.2 5.1 %collective-permute-start.4 = (bf16[64,256]{1,0:T(8,128)(2,1)S(1)}, bf16[64,256]{1,0:T(8,128)(2,1)S(1)}, u32[]{:S(2)}, u32[]{:S(2)}) collective-permute-start(bf16[64,256]{1,0:T(8,128)(2,1)S(1)} %get-tuple-element.19), channel_id=1, source_target_pairs={{0,17},{1,16},{2,19},{3,18},{4,21},{5,20},{6,23},{7,22},{8,25},{9,... | collective-permute-start | bytes 98312 | tf_op jit(solution)/shard_map/ppermute | solution.py:393

commit v6 on v5

--- a/solution.py
+++ b/solution.py
@@ -208,122 +208,226 @@
     core_ref[...] = fill_slab_p(scr, deep, wide, jnp.logical_not(even))
 
 
+def depth_next(x):
+    width = x.shape[1]
+    lanes = lax.broadcasted_iota(jnp.int32, x.shape, 1)
+    return jnp.where(lanes == width - 1, 0.0, pltpu.roll(x, width - 1, 1))
+
+
+def depth_prev(x):
+    lanes = lax.broadcasted_iota(jnp.int32, x.shape, 1)
+    return jnp.where(lanes == 0, 0.0, pltpu.roll(x, 1, 1))
+
+
+def sums_of(plasma):
+    magnetic, velocity = plasma[0:3], plasma[3:6]
+    return (
+        [0.25 * (v + b) for v, b in zip(velocity, magnetic)]
+        + [0.25 * (v - b) for v, b in zip(velocity, magnetic)]
+        + [0.5 * b for b in magnetic]
+    )
+
+
+def tangent_sums(state, tangent):
+    tang_mag, tang_vel = tangent[0:3], tangent[3:6]
+    half_pressure = state[6] * tang_mag[0] + state[7] * tang_mag[1] + state[8] * tang_mag[2]
+    return (
+        [w + b for w, b in zip(tang_vel, tang_mag)]
+        + [w - b for w, b in zip(tang_vel, tang_mag)]
+        + [half_pressure]
+    )
+
+
+def first_rows(values, rows):
+    return [x[0:rows] for x in values]
+
+
+def half_flux(state, sums, k):
+    magnetic, velocity = [], []
+    for i in range(3):
+        plus = sums[3 + k] * state[i] + state[3 + k] * sums[i]
+        minus = sums[k] * state[3 + i] + state[k] * sums[3 + i]
+        magnetic.append(plus - minus)
+        velocity.append(plus + minus + sums[6] if i == k else plus + minus)
+    return magnetic + velocity
+
+
+def row_next(x, rows):
+    if rows == 16:
+        return pltpu.roll(x, 15, 0)
+    own = x[0:8]
+    sublanes = lax.broadcasted_iota(jnp.int32, own.shape, 0)
+    return pltpu.roll(jnp.where(sublanes == 0, x[8:16], own), 7, 0)
+
+
+def row_prev(x, rows):
+    if rows == 16:
+        return pltpu.roll(x, 1, 0)
+    own = x[0:8]
+    sublanes = lax.broadcasted_iota(jnp.int32, own.shape, 0)
+    return pltpu.roll(jnp.where(sublanes == 7, x[8:16], own), 1, 0)
+
+
+def around(res):
+    return res, row_prev(res, 16), row_next(res, 16), depth_prev(res), depth_next(res)
+
+
+def in_plane(state, tangent, sums, diffusion, rows):
+    flux_rows = half_flux(state, sums, 1)
+    own = first_rows(tangent, rows)
+    flux_depth = half_flux(first_rows(state, rows), first_rows(sums, rows), 2)
+    out = []
+    for i in range(6):
+        here, above, below, west, east = diffusion if i < 3 else (viscosity,) * 5
+        if i < 3:
+            here, west, east = first_rows((here, west, east), rows)
+        total = (inverse_step + 4.0 * here) * own[i]
+        total = total + row_next(flux_rows[i] - above * tangent[i], rows)
+        total = total - row_prev(flux_rows[i] + below * tangent[i], rows)
+        total = total + depth_next(flux_depth[i] - west * own[i])
+        total = total - depth_prev(flux_depth[i] + east * own[i])
+        out.append(total)
+    return out
+
+
+def between_planes(image, tangent, after, before, res):
+    rows = image[0].shape[0]
+    (state_next, next_t, sums_next), (state_prev, prev_t, sums_prev) = [
+        [first_rows(values, rows) for values in plane] for plane in (after, before)
+    ]
+    flux_next = half_flux(state_next, sums_next, 0)
+    flux_prev = half_flux(state_prev, sums_prev, 0)
+    out = []
+    for i in range(6):
+        laplace = next_t[i] + prev_t[i] - 2.0 * tangent[i][0:rows]
+        total = image[i] + (flux_next[i] - flux_prev[i])
+        out.append(total - (res[0:rows] if i < 3 else viscosity) * laplace)
+    return out
+
+
+def precondition(ref, vector):
+    rows = vector[0].shape[0]
+    out = []
+    for a in range(6):
+        total = ref[6 * a, 0:rows] * vector[0]
+        for b in range(1, 6):
+            total = total + ref[6 * a + b, 0:rows] * vector[b]
+        out.append(total)
+    return out
+
+
+def put_halo(ref, at, below, above, offset, rows):
+    if rows < 4:
+        ref[at, 8:16] = jnp.zeros((8, ref.shape[-1]), F32)
+    ref[at, 8 : 8 + rows] = below[pl.ds(offset, rows), :]
+    ref[at, 16 - rows : 16] = above[pl.ds(offset, rows), :]
+
+
+def sort_slabs(outer_ref, core_ref, below, above):
+    place = lax.axis_index("pol")
+    even = place % 2 == 0
+    edge = jnp.logical_or(place == 0, place == lax.axis_size("pol") - 1)
+    from_outer = jnp.where(edge, 0.0, outer_ref[...].astype(F32))
+    from_core = core_ref[...].astype(F32)
+    above[...] = jnp.where(even, from_outer, from_core)
+    below[...] = jnp.where(even, from_core, from_outer)
+
+
+def own_plane_kernel(own_ref, t0_ref, outer_ref, core_ref, plane_ref, image_ref, below, above):
+    sort_slabs(outer_ref, core_ref, below, above)
+    for i in range(37):
+        plane_ref[i, 0:8] = own_ref[i]
+        put_halo(plane_ref, i, below, above, 48 + 2 * i, 2)
+    for i in range(6):
+        plane_ref[37 + i, 0:8] = own_ref[37 + i]
+        put_halo(plane_ref, 37 + i, below, above, 24 + 4 * i, 4)
+        plane_ref[43 + i, 0:8] = t0_ref[i]
+        put_halo(plane_ref, 43 + i, below, above, 4 * i, 4)
+    state = sums_of([plane_ref[37 + i] for i in range(6)])
+    for i, value in enumerate(state):
+        plane_ref[49 + i] = value
+    tangent = [plane_ref[43 + i] for i in range(6)]
+    sums = tangent_sums(state, tangent)
+    for i, value in enumerate(in_plane(state, tangent, sums, around(plane_ref[36]), 16)):
+        image_ref[i] = value
+
+
 def krylov_kernel(
-    own_ref, t0_ref, bulk_ref, outer_p_ref, outer_q_ref, core_p_ref, core_q_ref,
-    gram_ref, t_ref, up, down, blk_p, blk_q, st_p, st_q, res_s,
+    own_ref, plane_ref, image_ref, bulk_ref, outer_ref, core_ref,
+    gram_ref, t_ref, below, above, other_s,
 ):
-    width = own_ref.shape[-1]
-    even = lax.axis_index("pol") % 2 == 0
-    from_outer = jnp.concatenate([outer_p_ref[...], outer_q_ref[...]], axis=0).astype(F32)
-    from_core = jnp.concatenate([core_p_ref[...], core_q_ref[...]], axis=0).astype(F32)
-    place = lax.axis_index("pol")
-    edge = jnp.logical_or(place == 0, place == lax.axis_size("pol") - 1)
-    from_outer = jnp.where(edge, 0.0, from_outer)
-    up[...] = jnp.where(even, from_outer, from_core)
-    down[...] = jnp.where(even, from_core, from_outer)
-    zeros = jnp.zeros((8, width), F32)
-
-    def halo(ref, at, offset, rows):
-        if rows < 4:
-            ref[at, 8:16] = zeros
-        ref[at, 8 : 8 + rows] = down[pl.ds(offset, rows), :]
-        ref[at, 16 - rows : 16] = up[pl.ds(offset, rows), :]
+    sort_slabs(outer_ref, core_ref, below, above)
 
     def other(field):
         pair = bulk_ref[pl.ds(16 * (field // 2), 16), :].astype(F32)
         return pair[0:8] if field % 2 == 0 else pair[8:16]
 
-    for i in range(36):
-        blk_p[i, 0:8] = own_ref[i]
-        halo(blk_p, i, 48 + 2 * i, 2)
-        blk_q[i, 0:8] = other(i)
-        halo(blk_q, i, P_ROWS + 24 + i, 1)
-    for i in range(12):
-        st_p[i, 0:8] = t0_ref[i] if i < 6 else own_ref[31 + i]
-        halo(st_p, i, 4 * i, 4)
-        st_q[i, 0:8] = other(36 + i)
-        halo(st_q, i, P_ROWS + 2 * i, 2)
-    res_s[0, 0:8] = own_ref[36]
-    halo(res_s, 0, 120, 2)
-    res_s[1, 0:8] = other(48)
-    halo(res_s, 1, P_ROWS + 60, 1)
-
-    def lane(shape):
-        return lax.broadcasted_iota(jnp.int32, shape, 1)
-
-    def depth_next(x):
-        return jnp.where(lane(x.shape) == width - 1, 0.0, pltpu.roll(x, width - 1, 1))
-
-    def depth_prev(x):
-        return jnp.where(lane(x.shape) == 0, 0.0, pltpu.roll(x, 1, 1))
-
-    def jacobian(plasma, tangent, plasma_next, tangent_next, plasma_prev, tangent_prev, res, rows):
-        flux_next = linear_flux(plasma_next, tangent_next, 0)
-        flux_prev = linear_flux(plasma_prev, tangent_prev, 0)
-        flux_rows = linear_flux(plasma, tangent, 1)
-        own = [x[0:rows] for x in tangent]
-        flux_depth = linear_flux([x[0:rows] for x in plasma], own, 2)
-        out = []
-        for i in range(6):
-            total = inverse_step * own[i] + 0.5 * (flux_next[i][0:rows] - flux_prev[i][0:rows])
-            laplace = tangent_next[i][0:rows] + tangent_prev[i][0:rows] - 2.0 * own[i]
-            total = total + 0.5 * (
-                pltpu.roll(flux_rows[i], 15, 0)[0:rows] - pltpu.roll(flux_rows[i], 1, 0)[0:rows]
-            )
-            laplace = laplace + (
-                pltpu.roll(tangent[i], 15, 0)[0:rows] + pltpu.roll(tangent[i], 1, 0)[0:rows] - 2.0 * own[i]
-            )
-            total = total + 0.5 * (depth_next(flux_depth[i]) - depth_prev(flux_depth[i]))
-            laplace = laplace + (depth_next(own[i]) + depth_prev(own[i]) - 2.0 * own[i])
-            out.append(total - (res[0:rows] if i < 3 else viscosity) * laplace)
-        return out
-
-    def precondition(ref, vector, rows):
-        out = []
-        for a in range(6):
-            total = ref[6 * a, 0:rows] * vector[0]
-            for b in range(1, 6):
-                total = total + ref[6 * a + b, 0:rows] * vector[b]
-            out.append(total)
-        return out
-
-    plasma_p = [st_p[6 + i] for i in range(6)]
-    plasma_q = [st_q[6 + i] for i in range(6)]
-    half_p = [x[0:8] for x in plasma_p]
-    half_q = [x[0:8] for x in plasma_q]
+    for i in range(37):
+        other_s[i, 0:8] = other(i if i < 36 else 48)
+        put_halo(other_s, i, below, above, 24 + i, 1)
+    for i in range(6):
+        other_s[37 + i, 0:8] = other(42 + i)
+        put_halo(other_s, 37 + i, below, above, 12 + 2 * i, 2)
+        other_s[43 + i, 0:8] = other(36 + i)
+        put_halo(other_s, 43 + i, below, above, 2 * i, 2)
+
+    res_p, res_q = plane_ref[36], other_s[36]
+    diffusion_p, diffusion_q = around(res_p), around(res_q)
+    state_p = [plane_ref[49 + i] for i in range(9)]
+    state_q = sums_of([other_s[37 + i] for i in range(6)])
+    tang_p = [plane_ref[43 + i] for i in range(6)]
+    tang_q = [other_s[43 + i] for i in range(6)]
     krylov = [[own_ref[43 + i] for i in range(6)]]
-    tang_p = [st_p[i] for i in range(6)]
-    tang_q = [st_q[i] for i in range(6)]
-    for i in range(6):
-        t_ref[i] = t0_ref[i]
-
-    image_p = jacobian(plasma_p, tang_p, plasma_q, tang_q, plasma_q, tang_q, res_s[0], 16)
-    image_q = jacobian(plasma_q, tang_q, plasma_p, tang_p, plasma_p, tang_p, res_s[1], 16)
+    for i in range(6):
+        t_ref[i] = tang_p[i][0:8]
+
+    def shifted(tangents, shift, earlier):
+        return [t - shift * e[0 : t.shape[0]] for t, e in zip(tangents, earlier)]
+
+    plane_p = (state_p, tang_p, tangent_sums(state_p, tang_p))
+    plane_q = (state_q, tang_q, tangent_sums(state_q, tang_q))
+    image_p = [image_ref[i] for i in range(6)]
+    image_q = in_plane(*plane_q, diffusion_q, 16)
+    image_p = between_planes(image_p, tang_p, plane_q, plane_q, res_p)
+    image_q = between_planes(image_q, tang_q, plane_p, plane_p, res_q)
     krylov.append([image_p[i][0:8] - SHIFTS[0] * krylov[0][i] for i in range(6)])
-    next_p = [x - SHIFTS[0] * t for x, t in zip(precondition(blk_p, image_p, 16), tang_p)]
-    next_q = [x - SHIFTS[0] * t for x, t in zip(precondition(blk_q, image_q, 16), tang_q)]
+    next_p = shifted(precondition(plane_ref, image_p), SHIFTS[0], tang_p)
+    next_q = shifted(precondition(other_s, image_q), SHIFTS[0], tang_q)
     for i in range(6):
         t_ref[6 + i] = next_p[i][0:8]
 
-    image_p = jacobian(plasma_p, next_p, plasma_q, next_q, plasma_q, next_q, res_s[0], 16)
-    image_q = jacobian(plasma_q, next_q, half_p, [x[0:8] for x in next_p], half_p, [x[0:8] for x in next_p], res_s[1], 8)
+    plane_p = (state_p, next_p, tangent_sums(state_p, next_p))
+    plane_q = (state_q, next_q, tangent_sums(state_q, next_q))
+    image_p = in_plane(*plane_p, diffusion_p, 16)
+    image_q = in_plane(*plane_q, diffusion_q, 8)
+    image_p = between_planes(image_p, next_p, plane_q, plane_q, res_p)
+    image_q = between_planes(image_q, next_q, plane_p, plane_p, res_q)
     krylov.append([image_p[i][0:8] - SHIFTS[1] * krylov[1][i] for i in range(6)])
-    last_p = [x - SHIFTS[1] * t for x, t in zip(precondition(blk_p, image_p, 16), next_p)]
-    last_q = [x - SHIFTS[1] * t[0:8] for x, t in zip(precondition(blk_q, image_q, 8), next_q)]
+    last_p = shifted(precondition(plane_ref, image_p), SHIFTS[1], next_p)
+    last_q = shifted(precondition(other_s, image_q), SHIFTS[1], next_q)
     for i in range(6):
         t_ref[12 + i] = last_p[i][0:8]
 
-    image_p = jacobian(plasma_p, last_p, half_q, last_q, half_q, last_q, res_s[0], 8)
+    plane_p = (state_p, last_p, tangent_sums(state_p, last_p))
+    half_q = first_rows(state_q, 8)
+    plane_q = (half_q, last_q, tangent_sums(half_q, last_q))
+    image_p = in_plane(*plane_p, diffusion_p, 8)
+    image_p = between_planes(image_p, last_p, plane_q, plane_q, res_p)
     krylov.append([image_p[i] - SHIFTS[2] * krylov[2][i] for i in range(6)])
 
-    out = jnp.zeros((1, 128), F32)
-    lanes = lax.broadcasted_iota(jnp.int32, (1, 128), 1)
+    rows = lax.broadcasted_iota(jnp.int32, (16, 128), 0)
+    lanes = lax.broadcasted_iota(jnp.int32, (16, 128), 1)
+    table = jnp.zeros((16, 128), F32)
     for k, (i, j) in enumerate(PAIRS):
         total = krylov[i][0] * krylov[j][0]
         for f in range(1, 6):
             total = total + krylov[i][f] * krylov[j][f]
-        total = jnp.sum(jnp.sum(total, axis=0, keepdims=True), axis=1, keepdims=True)
-        out = jnp.where(lanes == k, total, out)
+        line = total[:, 0:128]
+        for start in range(128, total.shape[1], 128):
+            line = line + total[:, start : start + 128]
+        table = jnp.where(rows == k, jnp.sum(line, axis=0, keepdims=True), table)
+    sums = jnp.sum(table, axis=1, keepdims=True)
+    out = jnp.sum(jnp.where(rows == lanes, sums, 0.0), axis=0, keepdims=True)
     gram_ref[...] = jnp.broadcast_to(out[None], gram_ref.shape)
 
 
@@ -364,7 +468,6 @@
     rhs = right_side.reshape(6, rows, width)
     res = resistivity.reshape(1, rows, width)
     blocks = jacobi_blocks.reshape(6, 6, rows, width)
-    slab = P_ROWS + Q_ROWS
     vmem = pl.BlockSpec(memory_space=pltpu.VMEM)
     shape = jax.ShapeDtypeStruct
     t0, own, bulk, edge, inner = pl.pallas_call(
@@ -392,21 +495,21 @@
     outer_p = lax.ppermute(side, AXES, outer)
     core_q = lax.ppermute(inner, AXES, across_core)
     core_p = lax.ppermute(core_side, AXES, core)
+    plane, image = pl.pallas_call(
+        own_plane_kernel,
+        out_shape=(vmem_array((58, 16, width), F32), vmem_array((6, 16, width), F32)),
+        in_specs=[vmem] * 4,
+        out_specs=(vmem,) * 2,
+        scratch_shapes=[pltpu.VMEM((P_ROWS, width), F32)] * 2,
+        cost_estimate=pl.CostEstimate(flops=0, bytes_accessed=1_000_000, transcendentals=0),
+    )(*map(in_vmem, (own, t0, outer_p, core_p)))
     gram, tangents = pl.pallas_call(
         krylov_kernel,
         out_shape=(vmem_array((count, 1, 128), F32), vmem_array((18, rows, width), F32)),
-        in_specs=[vmem] * 7,
+        in_specs=[vmem] * 6,
         out_specs=(vmem,) * 2,
-        scratch_shapes=[
-            pltpu.VMEM((slab, width), F32),
-            pltpu.VMEM((slab, width), F32),
-            pltpu.VMEM((36, 16, width), F32),
-            pltpu.VMEM((36, 16, width), F32),
-            pltpu.VMEM((12, 16, width), F32),
-            pltpu.VMEM((12, 16, width), F32),
-            pltpu.VMEM((2, 16, width), F32),
-        ],
-    )(*map(in_vmem, (own, t0, bulk, outer_p, outer_q, core_p, core_q)))
+        scratch_shapes=[pltpu.VMEM((Q_ROWS, width), F32)] * 2 + [pltpu.VMEM((49, 16, width), F32)],
+    )(*map(in_vmem, (own, plane, image, bulk, outer_q, core_q)))
     gram = lax.all_to_all(gram, AXES, 0, 0, tiled=True)
     inverse_root = float((6.0 * count * rows * width) ** -0.5)
     update, estimates = pl.pallas_call(

time: 27.3 us -> 27 us (0.989)
  waiting for transfers between devices: 2.95 us -> 2.64 us
    ppermute x1, waiting for transfers between devices: 1.93 us -> 0.04 us  [two_planes(): outer_q = lax.ppermute(edge, AXES, corner)]
    ppermute x1, waiting for transfers between devices: 0.01 us -> 1.58 us  [two_planes(): outer_p = lax.ppermute(side, AXES, outer)]
    pallas_call x1, Pallas kernels: 1.24 us -> 0.93 us  [two_planes(): pl.pallas_call(krylov_kernel, out_shape=(vmem_array((count, 1, 128), F32)...]
    pallas_call x0 -> x1, Pallas kernels: none -> 0.3 us  [two_planes(): pl.pallas_call(own_plane_kernel, out_shape=(vmem_array((58, 16, width), F...]
  transfers between devices with their start and end apart: 5 -> 5, of which waited for: 2 -> 2; matrix products, arithmetic and copies ran while one was open for 0% -> 0% of each run, Pallas kernels for 0% -> 2%
where the time goes in v6:
time: 27 us; the launch traced here: 26.8 us
  blocking collectives  12.7 us (47%)
  starting transfers between devices  7.4 us (27%)
  Pallas kernels  3.43 us (13%)
  waiting for transfers between devices  2.64 us (10%)
  between operations  0.66 us (2%)
    all_to_all x1, blocking collectives, two_planes(): gram = lax.all_to_all(gram, AXES, 0, 0, tiled=True)  12.7 us
    ppermute x1, starting transfers between devices, two_planes(): bulk = lax.ppermute(bulk, AXES, across)  3 us
    ppermute x1, starting transfers between devices, two_planes(): core_q = lax.ppermute(inner, AXES, across_core)  2.17 us
    ppermute x1, starting transfers between devices, two_planes(): core_p = lax.ppermute(core_side, AXES, core)  1.62 us
    ppermute x1, waiting for transfers between devices, two_planes(): outer_p = lax.ppermute(side, AXES, outer)  1.58 us
    pallas_call x1, Pallas kernels, two_planes(): pl.pallas_call(first_kernel, out_shape=(vmem_array((6, rows, width), F32)...  1.19 us
    ppermute x1, waiting for transfers between devices, two_planes(): core_q = lax.ppermute(inner, AXES, across_core)  1.01 us
    pallas_call x1, Pallas kernels, two_planes(): pl.pallas_call(krylov_kernel, out_shape=(vmem_array((count, 1, 128), F32)...  0.93 us
  transfers between devices with their start and end apart: 5, of which 2 were waited for; matrix products, arithmetic and copies ran while one was open for 0% of the time, Pallas kernels for 2%

profile of v6, /device:TPU:0, one launch (start us, length us, event | category | flops | bytes accessed | tf_op | source)
XLA Modules:
  0.0 26.8 jit_solution(5199643513930278437)
XLA Ops:
  0.6 1.2 %shard_map.59 = (f32[6,8,256]{2,1,0:T(8,128)S(1)}, f32[49,8,256]{2,1,0:T(8,128)S(1)}, bf16[400,256]{1,0:T(8,128)(2,1)S(1)}, bf16[64,256]{1,0:T(8,128)(2,1)S(1)}, bf16[64,256]{1,0:T(8,128)(2,1)S(1)}) custom-call(f32[6,8,256]{2,1,0:T(8,128)} %bitcast.7, f32[6,8,256]{2,1,0:T(8,128)} %bitcast.8, f32[6,6,8,256]{3,2,1,0:T(8,128)} %bitcast.6, f32[1,8,256]{2,1,0:T(8,128)} %res_hbm.1), custom_call_target="tpu_custom_call" | custom-call | tf_op jit(solution)/shard_map/pallas_call | solution.py:473
  1.8 3.0 %collective-permute-start.2 = (bf16[400,256]{1,0:T(8,128)(2,1)S(1)}, bf16[400,256]{1,0:T(8,128)(2,1)S(1)}, u32[]{:S(2)}, u32[]{:S(2)}) collective-permute-start(bf16[400,256]{1,0:T(8,128)(2,1)S(1)} %get-tuple-element.21), channel_id=1, source_target_pairs={{0,16},{1,17},{2,18},{3,19},{4,20},{5,21},{6,22},{7,23},{8,24},{9,... | collective-permute-start | bytes 614408 | tf_op jit(solution)/shard_map/ppermute | solution.py:486
  4.8 0.1 shard_map.60
  4.9 0.1 collective-permute-start
  5.0 1.6 %collective-permute-start.1 = (bf16[128,256]{1,0:T(8,128)(2,1)S(1)}, bf16[128,256]{1,0:T(8,128)(2,1)S(1)}, u32[]{:S(2)}, u32[]{:S(2)}) collective-permute-start(bf16[128,256]{1,0:T(8,128)(2,1)S(1)} %get-tuple-element.18), channel_id=1, source_target_pairs={{0,1},{1,0},{2,3},{3,2},{4,5},{5,4},{6,7},{7,6},{8,9},{9,8},{10,11... | collective-permute-start | bytes 196616 | tf_op jit(solution)/shard_map/ppermute | solution.py:497
  6.6 0.5 %collective-permute-start.3 = (bf16[64,256]{1,0:T(8,128)(2,1)S(1)}, bf16[64,256]{1,0:T(8,128)(2,1)S(1)}, u32[]{:S(2)}, u32[]{:S(2)}) collective-permute-start(bf16[64,256]{1,0:T(8,128)(2,1)S(1)} %get-tuple-element.22), channel_id=1, source_target_pairs={{0,16},{1,18},{2,17},{3,20},{4,19},{5,22},{6,21},{7,24},{8,23},{9,... | collective-permute-start | bytes 98312 | tf_op jit(solution)/shard_map/ppermute | solution.py:487
  7.2 2.2 %collective-permute-start.4 = (bf16[64,256]{1,0:T(8,128)(2,1)S(1)}, bf16[64,256]{1,0:T(8,128)(2,1)S(1)}, u32[]{:S(2)}, u32[]{:S(2)}) collective-permute-start(bf16[64,256]{1,0:T(8,128)(2,1)S(1)} %get-tuple-element.23), channel_id=1, source_target_pairs={{0,17},{1,16},{2,19},{3,18},{4,21},{5,20},{6,23},{7,22},{8,25},{9,... | collective-permute-start | bytes 98312 | tf_op jit(solution)/shard_map/ppermute | solution.py:496
  9.3 1.6 %collective-permute-done.outer_ref = bf16[128,256]{1,0:T(8,128)(2,1)S(1)} collective-permute-done((bf16[128,256]{1,0:T(8,128)(2,1)S(1)}, bf16[128,256]{1,0:T(8,128)(2,1)S(1)}, u32[]{:S(2)}, u32[]{:S(2)}) %collective-permute-start) | collective-permute-done | bytes 65568 | tf_op jit(solution)/shard_map/ppermute | solution.py:495
  10.9 0.0 collective-permute-done.1.core_ref
  10.9 0.3 %shard_map.61 = (f32[58,16,256]{2,1,0:T(8,128)S(1)}, f32[6,16,256]{2,1,0:T(8,128)S(1)}) custom-call(f32[49,8,256]{2,1,0:T(8,128)S(1)} %get-tuple-element.15.own_ref, f32[6,8,256]{2,1,0:T(8,128)S(1)} %get-tuple-element.16.t0_ref, bf16[128,256]{1,0:T(8,128)(2,1)S(1)} %collective-permute-done.outer_ref, bf16[128,256]{1,0:T(8,128)(2,1)S(1)} %collective-permute-done.1.core_ref), custom_call_target="tpu_custom_call" | custom-call | bytes 1000000 | tf_op jit(solution)/shard_map/pallas_call | solution.py:498
  11.2 0.0 collective-permute-done.3.outer_ref
  11.3 1.0 %collective-permute-done.4.core_ref = bf16[64,256]{1,0:T(8,128)(2,1)S(1)} collective-permute-done((bf16[64,256]{1,0:T(8,128)(2,1)S(1)}, bf16[64,256]{1,0:T(8,128)(2,1)S(1)}, u32[]{:S(2)}, u32[]{:S(2)}) %collective-permute-start.4) | collective-permute-done | bytes 32800 | tf_op jit(solution)/shard_map/ppermute | solution.py:496
  12.3 0.0 collective-permute-done.2.bulk_ref
  12.3 0.9 %shard_map.62 = (f32[32,1,128]{2,1,0:T(1,128)S(1)}, f32[18,8,256]{2,1,0:T(8,128)S(1)}) custom-call(f32[49,8,256]{2,1,0:T(8,128)S(1)} %get-tuple-element.15.own_ref, f32[58,16,256]{2,1,0:T(8,128)S(1)} %get-tuple-element.19.plane_ref, f32[6,16,256]{2,1,0:T(8,128)S(1)} %get-tuple-element.20.image_ref, bf16[400,256]{1,0:T(8,128)(2,1)S(1)} %collective-permute-done.2.bulk_ref, ...), custom_call_target="tpu_custom_call" | custom-call | tf_op jit(solution)/shard_map/pallas_call | solution.py:506
  13.2 12.7 %all_to_all.5.gram_ref = f32[32,1,128]{2,1,0:T(1,128)S(1)} all-to-all(f32[32,1,128]{2,1,0:T(1,128)S(1)} %get-tuple-element.24), channel_id=1, replica_groups=mesh['tor'=2,'pol'=16] {'tor','pol'}, dimensions={0} | all-to-all | bytes 32768 | tf_op jit(solution)/shard_map/all_to_all | solution.py:513
  25.9 0.9 %shard_map.63 = (f32[6,8,256]{2,1,0:T(8,128)}, f32[3]{0:T(128)}) custom-call(f32[32,1,128]{2,1,0:T(1,128)S(1)} %all_to_all.5.gram_ref, f32[18,8,256]{2,1,0:T(8,128)S(1)} %get-tuple-element.25.t_ref), custom_call_target="tpu_custom_call" | custom-call | tf_op jit(solution)/shard_map/pallas_call | solution.py:515
Async XLA Ops:
  1.8 10.5 %collective-permute-start.2 = (bf16[400,256]{1,0:T(8,128)(2,1)S(1)}, bf16[400,256]{1,0:T(8,128)(2,1)S(1)}, u32[]{:S(2)}, u32[]{:S(2)}) collective-permute-start(bf16[400,256]{1,0:T(8,128)(2,1)S(1)} %get-tuple-element.21), channel_id=1, source_target_pairs={{0,16},{1,17},{2,18},{3,19},{4,20},{5,21},{6,22},{7,23},{8,24},{9,... | collective-permute-start | bytes 614408 | tf_op jit(solution)/shard_map/ppermute | solution.py:486
  4.9 6.0 %collective-permute-start = (bf16[128,256]{1,0:T(8,128)(2,1)S(1)}, bf16[128,256]{1,0:T(8,128)(2,1)S(1)}, u32[]{:S(2)}, u32[]{:S(2)}) collective-permute-start(bf16[128,256]{1,0:T(8,128)(2,1)S(1)} %get-tuple-element.17), channel_id=1, source_target_pairs={{0,16},{1,2},{2,1},{3,4},{4,3},{5,6},{6,5},{7,8},{8,7},{9,10},{10,... | collective-permute-start | bytes 196616 | tf_op jit(solution)/shard_map/ppermute | solution.py:495
  5.0 5.9 %collective-permute-start.1 = (bf16[128,256]{1,0:T(8,128)(2,1)S(1)}, bf16[128,256]{1,0:T(8,128)(2,1)S(1)}, u32[]{:S(2)}, u32[]{:S(2)}) collective-permute-start(bf16[128,256]{1,0:T(8,128)(2,1)S(1)} %get-tuple-element.18), channel_id=1, source_target_pairs={{0,1},{1,0},{2,3},{3,2},{4,5},{5,4},{6,7},{7,6},{8,9},{9,8},{10,11... | collective-permute-start | bytes 196616 | tf_op jit(solution)/shard_map/ppermute | solution.py:497
  6.6 4.6 %collective-permute-start.3 = (bf16[64,256]{1,0:T(8,128)(2,1)S(1)}, bf16[64,256]{1,0:T(8,128)(2,1)S(1)}, u32[]{:S(2)}, u32[]{:S(2)}) collective-permute-start(bf16[64,256]{1,0:T(8,128)(2,1)S(1)} %get-tuple-element.22), channel_id=1, source_target_pairs={{0,16},{1,18},{2,17},{3,20},{4,19},{5,22},{6,21},{7,24},{8,23},{9,... | collective-permute-start | bytes 98312 | tf_op jit(solution)/shard_map/ppermute | solution.py:487
  7.2 5.1 %collective-permute-start.4 = (bf16[64,256]{1,0:T(8,128)(2,1)S(1)}, bf16[64,256]{1,0:T(8,128)(2,1)S(1)}, u32[]{:S(2)}, u32[]{:S(2)}) collective-permute-start(bf16[64,256]{1,0:T(8,128)(2,1)S(1)} %get-tuple-element.23), channel_id=1, source_target_pairs={{0,17},{1,16},{2,19},{3,18},{4,21},{5,20},{6,23},{7,22},{8,25},{9,... | collective-permute-start | bytes 98312 | tf_op jit(solution)/shard_map/ppermute | solution.py:496

commit v7 on v6

--- a/solution.py
+++ b/solution.py
@@ -169,7 +169,7 @@
 
 def first_kernel(
     plasma_hbm, rhs_hbm, blocks_hbm, res_hbm,
-    t0_ref, own_ref, bulk_ref, edge_ref, inner_ref, scr, sems,
+    t0_ref, own_ref, bulk_ref, sems,
 ):
     copies = [
         pltpu.make_async_copy(rhs_hbm, own_ref.at[pl.ds(43, 6)], sems.at[0]),
@@ -178,7 +178,6 @@
     ] + [pltpu.make_async_copy(blocks_hbm.at[a], own_ref.at[pl.ds(6 * a, 6)], sems.at[3 + a]) for a in range(6)]
     for copy in copies:
         copy.start()
-    even = lax.axis_index("pol") % 2 == 0
     for copy in copies[:3]:
         copy.wait()
     vector = [own_ref[43 + b] for b in range(6)]
@@ -196,16 +195,16 @@
     for g in range(25):
         pair = jnp.concatenate([fields[2 * g], fields[2 * g + 1]], axis=0)
         bulk_ref[pl.ds(16 * g, 16), :] = pair.astype(BF16)
-    edge_ref[...] = fill_slab_q(scr, deep, wide, even)
-    inner_ref[...] = fill_slab_q(scr, deep, wide, jnp.logical_not(even))
-
-
-def pack_kernel(t0_ref, own_ref, side_ref, core_ref, scr):
+
+
+def pack_kernel(t0_ref, own_ref, side_ref, core_ref, edge_ref, inner_ref, scr, scr_q):
     even = lax.axis_index("pol") % 2 == 0
     deep = [t0_ref[i] for i in range(6)] + [own_ref[37 + i] for i in range(6)]
     wide = [own_ref[i] for i in range(37)]
     side_ref[...] = fill_slab_p(scr, deep, wide, even)
     core_ref[...] = fill_slab_p(scr, deep, wide, jnp.logical_not(even))
+    edge_ref[...] = fill_slab_q(scr_q, deep, wide, even)
+    inner_ref[...] = fill_slab_q(scr_q, deep, wide, jnp.logical_not(even))
 
 
 def depth_next(x):
@@ -470,31 +469,30 @@
     blocks = jacobi_blocks.reshape(6, 6, rows, width)
     vmem = pl.BlockSpec(memory_space=pltpu.VMEM)
     shape = jax.ShapeDtypeStruct
-    t0, own, bulk, edge, inner = pl.pallas_call(
+    t0, own, bulk = pl.pallas_call(
         first_kernel,
         out_shape=(
             vmem_array((6, rows, width), F32),
             vmem_array((49, rows, width), F32),
             vmem_array((400, width), BF16),
-            vmem_array((Q_ROWS, width), BF16),
-            vmem_array((Q_ROWS, width), BF16),
         ),
         in_specs=[pl.BlockSpec(memory_space=pltpu.HBM)] * 4,
-        out_specs=(vmem,) * 5,
-        scratch_shapes=[pltpu.VMEM((Q_ROWS, width), F32), pltpu.SemaphoreType.DMA((9,))],
+        out_specs=(vmem,) * 3,
+        scratch_shapes=[pltpu.SemaphoreType.DMA((9,))],
     )(*map(in_hbm, (plasma, rhs, blocks, res)))
     bulk = lax.ppermute(bulk, AXES, across)
-    outer_q = lax.ppermute(edge, AXES, corner)
-    side, core_side = pl.pallas_call(
+    slabs = (P_ROWS, P_ROWS, Q_ROWS, Q_ROWS)
+    side, core_side, edge, inner = pl.pallas_call(
         pack_kernel,
-        out_shape=(vmem_array((P_ROWS, width), BF16), vmem_array((P_ROWS, width), BF16)),
+        out_shape=tuple(vmem_array((size, width), BF16) for size in slabs),
         in_specs=[vmem] * 2,
-        out_specs=(vmem,) * 2,
-        scratch_shapes=[pltpu.VMEM((P_ROWS, width), F32)],
+        out_specs=(vmem,) * 4,
+        scratch_shapes=[pltpu.VMEM((P_ROWS, width), F32), pltpu.VMEM((Q_ROWS, width), F32)],
     )(in_vmem(t0), in_vmem(own))
     outer_p = lax.ppermute(side, AXES, outer)
+    core_p = lax.ppermute(core_side, AXES, core)
+    outer_q = lax.ppermute(edge, AXES, corner)
     core_q = lax.ppermute(inner, AXES, across_core)
-    core_p = lax.ppermute(core_side, AXES, core)
     plane, image = pl.pallas_call(
         own_plane_kernel,
         out_shape=(vmem_array((58, 16, width), F32), vmem_array((6, 16, width), F32)),

time: 27 us -> 26.9 us (level)
  waiting for transfers between devices: 2.64 us -> 2.07 us
  blocking collectives: 12.7 us -> 13.1 us
    ppermute x1, waiting for transfers between devices: 1.01 us -> 0.56 us  [two_planes(): core_q = lax.ppermute(inner, AXES, across_core)]
    all_to_all x1, blocking collectives: 12.7 us -> 13.1 us  [two_planes(): gram = lax.all_to_all(gram, AXES, 0, 0, tiled=True)]
where the time goes in v7:
time: 26.9 us; the launch traced here: 26.7 us
  blocking collectives  13.1 us (49%)
  starting transfers between devices  7.4 us (28%)
  Pallas kernels  3.43 us (13%)
  waiting for transfers between devices  2.07 us (8%)
  between operations  0.66 us (2%)
    all_to_all x1, blocking collectives, two_planes(): gram = lax.all_to_all(gram, AXES, 0, 0, tiled=True)  13.1 us
    ppermute x1, starting transfers between devices, two_planes(): bulk = lax.ppermute(bulk, AXES, across)  3 us
    ppermute x1, starting transfers between devices, two_planes(): core_q = lax.ppermute(inner, AXES, across_core)  2.17 us
    ppermute x1, starting transfers between devices, two_planes(): core_p = lax.ppermute(core_side, AXES, core)  1.62 us
    ppermute x1, waiting for transfers between devices, two_planes(): outer_p = lax.ppermute(side, AXES, outer)  1.47 us
    pallas_call x1, Pallas kernels, two_planes(): pl.pallas_call(first_kernel, out_shape=(vmem_array((6, rows, width), F32)...  1.08 us
    pallas_call x1, Pallas kernels, two_planes(): pl.pallas_call(krylov_kernel, out_shape=(vmem_array((count, 1, 128), F32)...  0.93 us
    pallas_call x1, Pallas kernels, two_planes(): pl.pallas_call(functools.partial(finish_kernel, inverse_root), out_shape=...  0.89 us
  transfers between devices with their start and end apart: 5, of which 2 were waited for; matrix products, arithmetic and copies ran while one was open for 0% of the time, Pallas kernels for 2%

profile of v7, /device:TPU:0, one launch (start us, length us, event | category | flops | bytes accessed | tf_op | source)
XLA Modules:
  0.0 26.7 jit_solution(12157255332047039530)
XLA Ops:
  0.6 1.1 %shard_map.59 = (f32[6,8,256]{2,1,0:T(8,128)S(1)}, f32[49,8,256]{2,1,0:T(8,128)S(1)}, bf16[400,256]{1,0:T(8,128)(2,1)S(1)}) custom-call(f32[6,8,256]{2,1,0:T(8,128)} %bitcast.7, f32[6,8,256]{2,1,0:T(8,128)} %bitcast.8, f32[6,6,8,256]{3,2,1,0:T(8,128)} %bitcast.6, f32[1,8,256]{2,1,0:T(8,128)} %res_hbm.1), custom_call_target="tpu_custom_call" | custom-call | tf_op jit(solution)/shard_map/pallas_call | solution.py:472
  1.7 3.0 %collective-permute-start.2 = (bf16[400,256]{1,0:T(8,128)(2,1)S(1)}, bf16[400,256]{1,0:T(8,128)(2,1)S(1)}, u32[]{:S(2)}, u32[]{:S(2)}) collective-permute-start(bf16[400,256]{1,0:T(8,128)(2,1)S(1)} %get-tuple-element.21), channel_id=1, source_target_pairs={{0,16},{1,17},{2,18},{3,19},{4,20},{5,21},{6,22},{7,23},{8,24},{9,... | collective-permute-start | bytes 614408 | tf_op jit(solution)/shard_map/ppermute | solution.py:483
  4.7 0.2 shard_map.60
  4.9 0.1 collective-permute-start
  5.0 1.6 %collective-permute-start.1 = (bf16[128,256]{1,0:T(8,128)(2,1)S(1)}, bf16[128,256]{1,0:T(8,128)(2,1)S(1)}, u32[]{:S(2)}, u32[]{:S(2)}) collective-permute-start(bf16[128,256]{1,0:T(8,128)(2,1)S(1)} %get-tuple-element.18), channel_id=1, source_target_pairs={{0,1},{1,0},{2,3},{3,2},{4,5},{5,4},{6,7},{7,6},{8,9},{9,8},{10,11... | collective-permute-start | bytes 196616 | tf_op jit(solution)/shard_map/ppermute | solution.py:493
  6.6 0.5 %collective-permute-start.3 = (bf16[64,256]{1,0:T(8,128)(2,1)S(1)}, bf16[64,256]{1,0:T(8,128)(2,1)S(1)}, u32[]{:S(2)}, u32[]{:S(2)}) collective-permute-start(bf16[64,256]{1,0:T(8,128)(2,1)S(1)} %get-tuple-element.22), channel_id=1, source_target_pairs={{0,16},{1,18},{2,17},{3,20},{4,19},{5,22},{6,21},{7,24},{8,23},{9,... | collective-permute-start | bytes 98312 | tf_op jit(solution)/shard_map/ppermute | solution.py:494
  7.2 2.2 %collective-permute-start.4 = (bf16[64,256]{1,0:T(8,128)(2,1)S(1)}, bf16[64,256]{1,0:T(8,128)(2,1)S(1)}, u32[]{:S(2)}, u32[]{:S(2)}) collective-permute-start(bf16[64,256]{1,0:T(8,128)(2,1)S(1)} %get-tuple-element.23), channel_id=1, source_target_pairs={{0,17},{1,16},{2,19},{3,18},{4,21},{5,20},{6,23},{7,22},{8,25},{9,... | collective-permute-start | bytes 98312 | tf_op jit(solution)/shard_map/ppermute | solution.py:495
  9.3 1.5 %collective-permute-done.outer_ref = bf16[128,256]{1,0:T(8,128)(2,1)S(1)} collective-permute-done((bf16[128,256]{1,0:T(8,128)(2,1)S(1)}, bf16[128,256]{1,0:T(8,128)(2,1)S(1)}, u32[]{:S(2)}, u32[]{:S(2)}) %collective-permute-start) | collective-permute-done | bytes 65568 | tf_op jit(solution)/shard_map/ppermute | solution.py:492
  10.8 0.0 collective-permute-done.1.core_ref
  10.8 0.3 %shard_map.61 = (f32[58,16,256]{2,1,0:T(8,128)S(1)}, f32[6,16,256]{2,1,0:T(8,128)S(1)}) custom-call(f32[49,8,256]{2,1,0:T(8,128)S(1)} %get-tuple-element.15.own_ref, f32[6,8,256]{2,1,0:T(8,128)S(1)} %get-tuple-element.16.t0_ref, bf16[128,256]{1,0:T(8,128)(2,1)S(1)} %collective-permute-done.outer_ref, bf16[128,256]{1,0:T(8,128)(2,1)S(1)} %collective-permute-done.1.core_ref), custom_call_target="tpu_custom_call" | custom-call | bytes 1000000 | tf_op jit(solution)/shard_map/pallas_call | solution.py:496
  11.1 0.0 collective-permute-done.3.outer_ref
  11.2 0.6 %collective-permute-done.4.core_ref = bf16[64,256]{1,0:T(8,128)(2,1)S(1)} collective-permute-done((bf16[64,256]{1,0:T(8,128)(2,1)S(1)}, bf16[64,256]{1,0:T(8,128)(2,1)S(1)}, u32[]{:S(2)}, u32[]{:S(2)}) %collective-permute-start.4) | collective-permute-done | bytes 32800 | tf_op jit(solution)/shard_map/ppermute | solution.py:495
  11.7 0.0 collective-permute-done.2.bulk_ref
  11.7 0.9 %shard_map.62 = (f32[32,1,128]{2,1,0:T(1,128)S(1)}, f32[18,8,256]{2,1,0:T(8,128)S(1)}) custom-call(f32[49,8,256]{2,1,0:T(8,128)S(1)} %get-tuple-element.15.own_ref, f32[58,16,256]{2,1,0:T(8,128)S(1)} %get-tuple-element.19.plane_ref, f32[6,16,256]{2,1,0:T(8,128)S(1)} %get-tuple-element.20.image_ref, bf16[400,256]{1,0:T(8,128)(2,1)S(1)} %collective-permute-done.2.bulk_ref, ...), custom_call_target="tpu_custom_call" | custom-call | tf_op jit(solution)/shard_map/pallas_call | solution.py:504
  12.7 13.1 %all_to_all.5.gram_ref = f32[32,1,128]{2,1,0:T(1,128)S(1)} all-to-all(f32[32,1,128]{2,1,0:T(1,128)S(1)} %get-tuple-element.24), channel_id=1, replica_groups=mesh['tor'=2,'pol'=16] {'tor','pol'}, dimensions={0} | all-to-all | bytes 32768 | tf_op jit(solution)/shard_map/all_to_all | solution.py:511
  25.8 0.9 %shard_map.63 = (f32[6,8,256]{2,1,0:T(8,128)}, f32[3]{0:T(128)}) custom-call(f32[32,1,128]{2,1,0:T(1,128)S(1)} %all_to_all.5.gram_ref, f32[18,8,256]{2,1,0:T(8,128)S(1)} %get-tuple-element.25.t_ref), custom_call_target="tpu_custom_call" | custom-call | tf_op jit(solution)/shard_map/pallas_call | solution.py:513
Async XLA Ops:
  1.7 10.0 %collective-permute-start.2 = (bf16[400,256]{1,0:T(8,128)(2,1)S(1)}, bf16[400,256]{1,0:T(8,128)(2,1)S(1)}, u32[]{:S(2)}, u32[]{:S(2)}) collective-permute-start(bf16[400,256]{1,0:T(8,128)(2,1)S(1)} %get-tuple-element.21), channel_id=1, source_target_pairs={{0,16},{1,17},{2,18},{3,19},{4,20},{5,21},{6,22},{7,23},{8,24},{9,... | collective-permute-start | bytes 614408 | tf_op jit(solution)/shard_map/ppermute | solution.py:483
  4.9 5.9 %collective-permute-start = (bf16[128,256]{1,0:T(8,128)(2,1)S(1)}, bf16[128,256]{1,0:T(8,128)(2,1)S(1)}, u32[]{:S(2)}, u32[]{:S(2)}) collective-permute-start(bf16[128,256]{1,0:T(8,128)(2,1)S(1)} %get-tuple-element.17), channel_id=1, source_target_pairs={{0,16},{1,2},{2,1},{3,4},{4,3},{5,6},{6,5},{7,8},{8,7},{9,10},{10,... | collective-permute-start | bytes 196616 | tf_op jit(solution)/shard_map/ppermute | solution.py:492
  5.0 5.8 %collective-permute-start.1 = (bf16[128,256]{1,0:T(8,128)(2,1)S(1)}, bf16[128,256]{1,0:T(8,128)(2,1)S(1)}, u32[]{:S(2)}, u32[]{:S(2)}) collective-permute-start(bf16[128,256]{1,0:T(8,128)(2,1)S(1)} %get-tuple-element.18), channel_id=1, source_target_pairs={{0,1},{1,0},{2,3},{3,2},{4,5},{5,4},{6,7},{7,6},{8,9},{9,8},{10,11... | collective-permute-start | bytes 196616 | tf_op jit(solution)/shard_map/ppermute | solution.py:493
  6.6 4.5 %collective-permute-start.3 = (bf16[64,256]{1,0:T(8,128)(2,1)S(1)}, bf16[64,256]{1,0:T(8,128)(2,1)S(1)}, u32[]{:S(2)}, u32[]{:S(2)}) collective-permute-start(bf16[64,256]{1,0:T(8,128)(2,1)S(1)} %get-tuple-element.22), channel_id=1, source_target_pairs={{0,16},{1,18},{2,17},{3,20},{4,19},{5,22},{6,21},{7,24},{8,23},{9,... | collective-permute-start | bytes 98312 | tf_op jit(solution)/shard_map/ppermute | solution.py:494
  7.2 4.6 %collective-permute-start.4 = (bf16[64,256]{1,0:T(8,128)(2,1)S(1)}, bf16[64,256]{1,0:T(8,128)(2,1)S(1)}, u32[]{:S(2)}, u32[]{:S(2)}) collective-permute-start(bf16[64,256]{1,0:T(8,128)(2,1)S(1)} %get-tuple-element.23), channel_id=1, source_target_pairs={{0,17},{1,16},{2,19},{3,18},{4,21},{5,20},{6,23},{7,22},{8,25},{9,... | collective-permute-start | bytes 98312 | tf_op jit(solution)/shard_map/ppermute | solution.py:495

commit v8 on v7

--- a/solution.py
+++ b/solution.py
@@ -143,6 +143,7 @@
 in_hbm = functools.partial(pltpu.with_memory_space_constraint, memory_space=pltpu.HBM)
 vmem_array = pltpu.VMEM
 P_ROWS, Q_ROWS = 128, 64
+M_ROWS = 272
 
 
 def tile_rows(value, count, first):
@@ -169,7 +170,7 @@
 
 def first_kernel(
     plasma_hbm, rhs_hbm, blocks_hbm, res_hbm,
-    t0_ref, own_ref, bulk_ref, sems,
+    t0_ref, own_ref, ends_ref, scr, sems,
 ):
     copies = [
         pltpu.make_async_copy(rhs_hbm, own_ref.at[pl.ds(43, 6)], sems.at[0]),
@@ -191,20 +192,23 @@
         t0.append(total)
     deep = t0 + [own_ref[37 + i] for i in range(6)]
     wide = [own_ref[i] for i in range(37)]
-    fields = wide[:36] + deep + [wide[36], wide[36]]
-    for g in range(25):
-        pair = jnp.concatenate([fields[2 * g], fields[2 * g + 1]], axis=0)
-        bulk_ref[pl.ds(16 * g, 16), :] = pair.astype(BF16)
-
-
-def pack_kernel(t0_ref, own_ref, side_ref, core_ref, edge_ref, inner_ref, scr, scr_q):
+    even = lax.axis_index("pol") % 2 == 0
+    ends_ref[pl.ds(0, Q_ROWS), :] = fill_slab_q(scr, deep, wide, even)
+    ends_ref[pl.ds(Q_ROWS, Q_ROWS), :] = fill_slab_q(scr, deep, wide, jnp.logical_not(even))
+
+
+def pack_kernel(t0_ref, own_ref, middle_ref, side_ref, core_ref, scr, scr_m):
     even = lax.axis_index("pol") % 2 == 0
     deep = [t0_ref[i] for i in range(6)] + [own_ref[37 + i] for i in range(6)]
     wide = [own_ref[i] for i in range(37)]
     side_ref[...] = fill_slab_p(scr, deep, wide, even)
     core_ref[...] = fill_slab_p(scr, deep, wide, jnp.logical_not(even))
-    edge_ref[...] = fill_slab_q(scr_q, deep, wide, even)
-    inner_ref[...] = fill_slab_q(scr_q, deep, wide, jnp.logical_not(even))
+    scr_m[pl.ds(M_ROWS - 8, 8), :] = jnp.zeros((8, scr_m.shape[1]), F32)
+    for f, value in enumerate(deep):
+        scr_m[pl.ds(4 * f, 4), :] = value[2:6]
+    for f, value in enumerate(wide):
+        scr_m[pl.ds(48 + 6 * f, 6), :] = value[1:7]
+    middle_ref[...] = scr_m[...].astype(BF16)
 
 
 def depth_next(x):
@@ -351,24 +355,35 @@
         image_ref[i] = value
 
 
+def other_plane_kernel(middle_ref, ends_ref, other_ref, scr_e, scr_m):
+    even = lax.axis_index("pol") % 2 == 0
+    outer, inner = ends_ref[pl.ds(0, Q_ROWS), :].astype(F32), ends_ref[pl.ds(Q_ROWS, Q_ROWS), :].astype(F32)
+    scr_e[pl.ds(0, Q_ROWS), :] = jnp.where(even, outer, inner)
+    scr_e[pl.ds(Q_ROWS, Q_ROWS), :] = jnp.where(even, inner, outer)
+    scr_m[...] = middle_ref[...].astype(F32)
+    for f in range(12):
+        at = 43 + f if f < 6 else 31 + f
+        other_ref[at, 0:2] = scr_e[pl.ds(2 * f, 2), :]
+        other_ref[at, 2:6] = scr_m[pl.ds(4 * f, 4), :]
+        other_ref[at, 6:8] = scr_e[pl.ds(Q_ROWS + 2 * f, 2), :]
+    for i in range(37):
+        other_ref[i, 0:1] = scr_e[pl.ds(24 + i, 1), :]
+        other_ref[i, 1:7] = scr_m[pl.ds(48 + 6 * i, 6), :]
+        other_ref[i, 7:8] = scr_e[pl.ds(Q_ROWS + 24 + i, 1), :]
+
+
 def krylov_kernel(
-    own_ref, plane_ref, image_ref, bulk_ref, outer_ref, core_ref,
+    own_ref, plane_ref, image_ref, other_ref, outer_ref, core_ref,
     gram_ref, t_ref, below, above, other_s,
 ):
     sort_slabs(outer_ref, core_ref, below, above)
 
-    def other(field):
-        pair = bulk_ref[pl.ds(16 * (field // 2), 16), :].astype(F32)
-        return pair[0:8] if field % 2 == 0 else pair[8:16]
-
-    for i in range(37):
-        other_s[i, 0:8] = other(i if i < 36 else 48)
-        put_halo(other_s, i, below, above, 24 + i, 1)
-    for i in range(6):
-        other_s[37 + i, 0:8] = other(42 + i)
-        put_halo(other_s, 37 + i, below, above, 12 + 2 * i, 2)
-        other_s[43 + i, 0:8] = other(36 + i)
-        put_halo(other_s, 43 + i, below, above, 2 * i, 2)
+    for i in range(49):
+        other_s[i, 0:8] = other_ref[i]
+        if i < 37:
+            put_halo(other_s, i, below, above, 24 + i, 1)
+        else:
+            put_halo(other_s, i, below, above, 2 * (i - 31) if i < 43 else 2 * (i - 43), 2)
 
     res_p, res_q = plane_ref[36], other_s[36]
     diffusion_p, diffusion_q = around(res_p), around(res_q)
@@ -461,7 +476,6 @@
     core = pairs(lambda t, p: (t, p ^ 1))
     outer = pairs(lambda t, p: beyond(t, p, t))
     corner = pairs(lambda t, p: beyond(t, p, 1 - t))
-    across_core = pairs(lambda t, p: (1 - t, p ^ 1))
 
     plasma = plasma_state.reshape(6, rows, width)
     rhs = right_side.reshape(6, rows, width)
@@ -469,37 +483,47 @@
     blocks = jacobi_blocks.reshape(6, 6, rows, width)
     vmem = pl.BlockSpec(memory_space=pltpu.VMEM)
     shape = jax.ShapeDtypeStruct
-    t0, own, bulk = pl.pallas_call(
+    t0, own, ends = pl.pallas_call(
         first_kernel,
         out_shape=(
             vmem_array((6, rows, width), F32),
             vmem_array((49, rows, width), F32),
-            vmem_array((400, width), BF16),
+            vmem_array((2 * Q_ROWS, width), BF16),
         ),
         in_specs=[pl.BlockSpec(memory_space=pltpu.HBM)] * 4,
         out_specs=(vmem,) * 3,
-        scratch_shapes=[pltpu.SemaphoreType.DMA((9,))],
+        scratch_shapes=[pltpu.VMEM((Q_ROWS, width), F32), pltpu.SemaphoreType.DMA((9,))],
     )(*map(in_hbm, (plasma, rhs, blocks, res)))
-    bulk = lax.ppermute(bulk, AXES, across)
-    slabs = (P_ROWS, P_ROWS, Q_ROWS, Q_ROWS)
-    side, core_side, edge, inner = pl.pallas_call(
+    edge = ends[:Q_ROWS]
+    ends = lax.ppermute(ends, AXES, across)
+    slabs = (M_ROWS, P_ROWS, P_ROWS)
+    middle, side, core_side = pl.pallas_call(
         pack_kernel,
         out_shape=tuple(vmem_array((size, width), BF16) for size in slabs),
         in_specs=[vmem] * 2,
-        out_specs=(vmem,) * 4,
-        scratch_shapes=[pltpu.VMEM((P_ROWS, width), F32), pltpu.VMEM((Q_ROWS, width), F32)],
+        out_specs=(vmem,) * 3,
+        scratch_shapes=[pltpu.VMEM((P_ROWS, width), F32), pltpu.VMEM((M_ROWS, width), F32)],
     )(in_vmem(t0), in_vmem(own))
+    middle = lax.ppermute(middle, AXES, across)
     outer_p = lax.ppermute(side, AXES, outer)
     core_p = lax.ppermute(core_side, AXES, core)
     outer_q = lax.ppermute(edge, AXES, corner)
-    core_q = lax.ppermute(inner, AXES, across_core)
+    core_q = lax.ppermute(ends[Q_ROWS:], AXES, core)
+    other = pl.pallas_call(
+        other_plane_kernel,
+        out_shape=vmem_array((49, rows, width), F32),
+        in_specs=[vmem] * 2,
+        out_specs=vmem,
+        scratch_shapes=[pltpu.VMEM((2 * Q_ROWS, width), F32), pltpu.VMEM((M_ROWS, width), F32)],
+        cost_estimate=pl.CostEstimate(flops=0, bytes_accessed=1_000_000, transcendentals=0),
+    )(in_vmem(middle), in_vmem(ends))
     plane, image = pl.pallas_call(
         own_plane_kernel,
         out_shape=(vmem_array((58, 16, width), F32), vmem_array((6, 16, width), F32)),
         in_specs=[vmem] * 4,
         out_specs=(vmem,) * 2,
         scratch_shapes=[pltpu.VMEM((P_ROWS, width), F32)] * 2,
-        cost_estimate=pl.CostEstimate(flops=0, bytes_accessed=1_000_000, transcendentals=0),
+        cost_estimate=pl.CostEstimate(flops=1000000000, bytes_accessed=1_000_000, transcendentals=0),
     )(*map(in_vmem, (own, t0, outer_p, core_p)))
     gram, tangents = pl.pallas_call(
         krylov_kernel,
@@ -507,7 +531,7 @@
         in_specs=[vmem] * 6,
         out_specs=(vmem,) * 2,
         scratch_shapes=[pltpu.VMEM((Q_ROWS, width), F32)] * 2 + [pltpu.VMEM((49, 16, width), F32)],
-    )(*map(in_vmem, (own, plane, image, bulk, outer_q, core_q)))
+    )(*map(in_vmem, (own, plane, image, other, outer_q, core_q)))
     gram = lax.all_to_all(gram, AXES, 0, 0, tiled=True)
     inverse_root = float((6.0 * count * rows * width) ** -0.5)
     update, estimates = pl.pallas_call(

time: 26.9 us -> 26.6 us (0.989)
  blocking collectives: 13.1 us -> 11.2 us
  waiting for transfers between devices: 2.07 us -> 3.1 us
  starting transfers between devices: 7.4 us -> 7.8 us
    ppermute x2 -> x3, waiting for transfers between devices: 0.57 us -> 2.9 us  [the longest x1 2.89 us: two_planes(): middle = lax.ppermute(middle, AXES, across)]
    all_to_all x1, blocking collectives: 13.1 us -> 11.2 us  [two_planes(): gram = lax.all_to_all(gram, AXES, 0, 0, tiled=True)]
    ppermute x1, waiting for transfers between devices: 1.47 us -> 0.01 us  [two_planes(): outer_p = lax.ppermute(side, AXES, outer)]
    ppermute x1, starting transfers between devices: 0.53 us -> 1.48 us  [two_planes(): outer_q = lax.ppermute(edge, AXES, corner)]
    ppermute x2 -> x3, starting transfers between devices: 5.17 us -> 4.62 us  [the longest x1 3 us: two_planes(): ends = lax.ppermute(ends, AXES, across)]
  transfers between devices with their start and end apart: 5 -> 6, of which waited for: 2 -> 2; matrix products, arithmetic and copies ran while one was open for 0% -> 0% of each run, Pallas kernels for 2% -> 2%
where the time goes in v8:
time: 26.6 us; the launch traced here: 26.4 us
  blocking collectives  11.2 us (42%)
  starting transfers between devices  7.8 us (29%)
  Pallas kernels  3.6 us (14%)
  waiting for transfers between devices  3.1 us (12%)
  between operations  0.67 us (3%)
    all_to_all x1, blocking collectives, two_planes(): gram = lax.all_to_all(gram, AXES, 0, 0, tiled=True)  11.2 us
    ppermute x1, starting transfers between devices, two_planes(): ends = lax.ppermute(ends, AXES, across)  3 us
    ppermute x1, waiting for transfers between devices, two_planes(): middle = lax.ppermute(middle, AXES, across)  2.89 us
    ppermute x1, starting transfers between devices, two_planes(): core_p = lax.ppermute(core_side, AXES, core)  1.62 us
    ppermute x1, starting transfers between devices, two_planes(): outer_q = lax.ppermute(edge, AXES, corner)  1.48 us
    pallas_call x1, Pallas kernels, two_planes(): pl.pallas_call(first_kernel, out_shape=(vmem_array((6, rows, width), F32)...  1.19 us
    ppermute x1, starting transfers between devices, two_planes(): core_q = lax.ppermute(ends[Q_ROWS:], AXES, core)  1.07 us
    pallas_call x1, Pallas kernels, two_planes(): pl.pallas_call(krylov_kernel, out_shape=(vmem_array((count, 1, 128), F32)...  0.92 us
  transfers between devices with their start and end apart: 6, of which 2 were waited for; matrix products, arithmetic and copies ran while one was open for 0% of the time, Pallas kernels for 2%

profile of v8, /device:TPU:0, one launch (start us, length us, event | category | flops | bytes accessed | tf_op | source)
XLA Modules:
  0.0 26.4 jit_solution(5579022315036972874)
XLA Ops:
  0.6 1.2 %shard_map.59 = (f32[6,8,256]{2,1,0:T(8,128)S(1)}, f32[49,8,256]{2,1,0:T(8,128)S(1)}, bf16[128,256]{1,0:T(8,128)(2,1)S(1)}) custom-call(f32[6,8,256]{2,1,0:T(8,128)} %bitcast.7, f32[6,8,256]{2,1,0:T(8,128)} %bitcast.8, f32[6,6,8,256]{3,2,1,0:T(8,128)} %bitcast.6, f32[1,8,256]{2,1,0:T(8,128)} %res_hbm.1), custom_call_target="tpu_custom_call" | custom-call | tf_op jit(solution)/shard_map/pallas_call | solution.py:486
  1.8 3.0 %collective-permute-start.3 = (bf16[128,256]{1,0:T(8,128)(2,1)S(1)}, bf16[128,256]{1,0:T(8,128)(2,1)S(1)}, u32[]{:S(2)}, u32[]{:S(2)}) collective-permute-start(bf16[128,256]{1,0:T(8,128)(2,1)S(1)} %get-tuple-element.21), channel_id=1, source_target_pairs={{0,16},{1,17},{2,18},{3,19},{4,20},{5,21},{6,22},{7,23},{8,24},{9,... | collective-permute-start | bytes 196616 | tf_op jit(solution)/shard_map/ppermute | solution.py:498
  4.8 0.2 shard_map.60
  5.0 0.1 collective-permute-start
  5.1 1.6 %collective-permute-start.1 = (bf16[128,256]{1,0:T(8,128)(2,1)S(1)}, bf16[128,256]{1,0:T(8,128)(2,1)S(1)}, u32[]{:S(2)}, u32[]{:S(2)}) collective-permute-start(bf16[128,256]{1,0:T(8,128)(2,1)S(1)} %get-tuple-element.17), channel_id=1, source_target_pairs={{0,1},{1,0},{2,3},{3,2},{4,5},{5,4},{6,7},{7,6},{8,9},{9,8},{10,11... | collective-permute-start | bytes 196616 | tf_op jit(solution)/shard_map/ppermute | solution.py:509
  6.7 0.5 %collective-permute-start.2 = (bf16[272,256]{1,0:T(8,128)(2,1)S(1)}, bf16[272,256]{1,0:T(8,128)(2,1)S(1)}, u32[]{:S(2)}, u32[]{:S(2)}) collective-permute-start(bf16[272,256]{1,0:T(8,128)(2,1)S(1)} %get-tuple-element.20), channel_id=1, source_target_pairs={{0,16},{1,17},{2,18},{3,19},{4,20},{5,21},{6,22},{7,23},{8,24},{9,... | collective-permute-start | bytes 417800 | tf_op jit(solution)/shard_map/ppermute | solution.py:507
  7.2 1.5 %collective-permute-start.4 = (bf16[64,256]{1,0:T(8,128)(2,1)S(1)}, bf16[64,256]{1,0:T(8,128)(2,1)S(1)}, u32[]{:S(2)}, u32[]{:S(2)}) collective-permute-start(bf16[64,256]{1,0:T(8,128)(2,1)S(1)} %slice.6), channel_id=1, source_target_pairs={{0,16},{1,18},{2,17},{3,20},{4,19},{5,22},{6,21},{7,24},{8,23},{9,... | collective-permute-start | bytes 98312 | tf_op jit(solution)/shard_map/ppermute | solution.py:510
  8.7 0.0 collective-permute-done.3.ends_ref
  8.7 1.1 %collective-permute-start.5 = (bf16[64,256]{1,0:T(8,128)(2,1)S(1)}, bf16[64,256]{1,0:T(8,128)(2,1)S(1)}, u32[]{:S(2)}, u32[]{:S(2)}) collective-permute-start(bf16[64,256]{1,0:T(8,128)(2,1)S(1)} %slice.8), channel_id=1, source_target_pairs={{0,1},{1,0},{2,3},{3,2},{4,5},{5,4},{6,7},{7,6},{8,9},{9,8},{10,11... | collective-permute-start | bytes 98312 | tf_op jit(solution)/shard_map/ppermute | solution.py:511
  9.8 0.0 collective-permute-done.outer_ref
  9.8 0.0 collective-permute-done.1.core_ref
  9.8 0.3 %shard_map.61 = (f32[58,16,256]{2,1,0:T(8,128)S(1)}, f32[6,16,256]{2,1,0:T(8,128)S(1)}) custom-call(f32[49,8,256]{2,1,0:T(8,128)S(1)} %get-tuple-element.14.own_ref, f32[6,8,256]{2,1,0:T(8,128)S(1)} %get-tuple-element.15.t0_ref, bf16[128,256]{1,0:T(8,128)(2,1)S(1)} %collective-permute-done.outer_ref, bf16[128,256]{1,0:T(8,128)(2,1)S(1)} %collective-permute-done.1.core_ref), custom_call_target="tpu_custom_call" | custom-call | flops 1000000000 | bytes 1000000 | tf_op jit(solution)/shard_map/pallas_call | solution.py:520
  10.1 2.9 %collective-permute-done.2.middle_ref = bf16[272,256]{1,0:T(8,128)(2,1)S(1)} collective-permute-done((bf16[272,256]{1,0:T(8,128)(2,1)S(1)}, bf16[272,256]{1,0:T(8,128)(2,1)S(1)}, u32[]{:S(2)}, u32[]{:S(2)}) %collective-permute-start.2) | collective-permute-done | bytes 139296 | tf_op jit(solution)/shard_map/ppermute | solution.py:507
  13.0 0.1 shard_map.62.other_ref
  13.2 0.2 collective-permute-done.4.outer_ref
  13.4 0.0 collective-permute-done.5.core_ref
  13.4 0.9 %shard_map.63 = (f32[32,1,128]{2,1,0:T(1,128)S(1)}, f32[18,8,256]{2,1,0:T(8,128)S(1)}) custom-call(f32[49,8,256]{2,1,0:T(8,128)S(1)} %get-tuple-element.14.own_ref, f32[58,16,256]{2,1,0:T(8,128)S(1)} %get-tuple-element.18.plane_ref, f32[6,16,256]{2,1,0:T(8,128)S(1)} %get-tuple-element.19.image_ref, f32[49,8,256]{2,1,0:T(8,128)S(1)} %shard_map.62.other_ref, ...), custom_call_target="tpu_custom_call" | custom-call | tf_op jit(solution)/shard_map/pallas_call | solution.py:528
  14.3 11.2 %all_to_all.5.gram_ref = f32[32,1,128]{2,1,0:T(1,128)S(1)} all-to-all(f32[32,1,128]{2,1,0:T(1,128)S(1)} %get-tuple-element.22), channel_id=1, replica_groups=mesh['tor'=2,'pol'=16] {'tor','pol'}, dimensions={0} | all-to-all | bytes 32768 | tf_op jit(solution)/shard_map/all_to_all | solution.py:535
  25.5 0.9 %shard_map.64 = (f32[6,8,256]{2,1,0:T(8,128)}, f32[3]{0:T(128)}) custom-call(f32[32,1,128]{2,1,0:T(1,128)S(1)} %all_to_all.5.gram_ref, f32[18,8,256]{2,1,0:T(8,128)S(1)} %get-tuple-element.23.t_ref), custom_call_target="tpu_custom_call" | custom-call | tf_op jit(solution)/shard_map/pallas_call | solution.py:537
  (2 shorter events, 0.0 us)
Async XLA Ops:
  1.8 6.9 %collective-permute-start.3 = (bf16[128,256]{1,0:T(8,128)(2,1)S(1)}, bf16[128,256]{1,0:T(8,128)(2,1)S(1)}, u32[]{:S(2)}, u32[]{:S(2)}) collective-permute-start(bf16[128,256]{1,0:T(8,128)(2,1)S(1)} %get-tuple-element.21), channel_id=1, source_target_pairs={{0,16},{1,17},{2,18},{3,19},{4,20},{5,21},{6,22},{7,23},{8,24},{9,... | collective-permute-start | bytes 196616 | tf_op jit(solution)/shard_map/ppermute | solution.py:498
  5.0 4.8 %collective-permute-start = (bf16[128,256]{1,0:T(8,128)(2,1)S(1)}, bf16[128,256]{1,0:T(8,128)(2,1)S(1)}, u32[]{:S(2)}, u32[]{:S(2)}) collective-permute-start(bf16[128,256]{1,0:T(8,128)(2,1)S(1)} %get-tuple-element.16), channel_id=1, source_target_pairs={{0,16},{1,2},{2,1},{3,4},{4,3},{5,6},{6,5},{7,8},{8,7},{9,10},{10,... | collective-permute-start | bytes 196616 | tf_op jit(solution)/shard_map/ppermute | solution.py:508
  5.1 4.7 %collective-permute-start.1 = (bf16[128,256]{1,0:T(8,128)(2,1)S(1)}, bf16[128,256]{1,0:T(8,128)(2,1)S(1)}, u32[]{:S(2)}, u32[]{:S(2)}) collective-permute-start(bf16[128,256]{1,0:T(8,128)(2,1)S(1)} %get-tuple-element.17), channel_id=1, source_target_pairs={{0,1},{1,0},{2,3},{3,2},{4,5},{5,4},{6,7},{7,6},{8,9},{9,8},{10,11... | collective-permute-start | bytes 196616 | tf_op jit(solution)/shard_map/ppermute | solution.py:509
  6.7 6.3 %collective-permute-start.2 = (bf16[272,256]{1,0:T(8,128)(2,1)S(1)}, bf16[272,256]{1,0:T(8,128)(2,1)S(1)}, u32[]{:S(2)}, u32[]{:S(2)}) collective-permute-start(bf16[272,256]{1,0:T(8,128)(2,1)S(1)} %get-tuple-element.20), channel_id=1, source_target_pairs={{0,16},{1,17},{2,18},{3,19},{4,20},{5,21},{6,22},{7,23},{8,24},{9,... | collective-permute-start | bytes 417800 | tf_op jit(solution)/shard_map/ppermute | solution.py:507
  7.2 6.1 %collective-permute-start.4 = (bf16[64,256]{1,0:T(8,128)(2,1)S(1)}, bf16[64,256]{1,0:T(8,128)(2,1)S(1)}, u32[]{:S(2)}, u32[]{:S(2)}) collective-permute-start(bf16[64,256]{1,0:T(8,128)(2,1)S(1)} %slice.6), channel_id=1, source_target_pairs={{0,16},{1,18},{2,17},{3,20},{4,19},{5,22},{6,21},{7,24},{8,23},{9,... | collective-permute-start | bytes 98312 | tf_op jit(solution)/shard_map/ppermute | solution.py:510
  8.7 4.6 %collective-permute-start.5 = (bf16[64,256]{1,0:T(8,128)(2,1)S(1)}, bf16[64,256]{1,0:T(8,128)(2,1)S(1)}, u32[]{:S(2)}, u32[]{:S(2)}) collective-permute-start(bf16[64,256]{1,0:T(8,128)(2,1)S(1)} %slice.8), channel_id=1, source_target_pairs={{0,1},{1,0},{2,3},{3,2},{4,5},{5,4},{6,7},{7,6},{8,9},{9,8},{10,11... | collective-permute-start | bytes 98312 | tf_op jit(solution)/shard_map/ppermute | solution.py:511

commit v9 on v8

--- a/solution.py
+++ b/solution.py
@@ -197,18 +197,23 @@
     ends_ref[pl.ds(Q_ROWS, Q_ROWS), :] = fill_slab_q(scr, deep, wide, jnp.logical_not(even))
 
 
-def pack_kernel(t0_ref, own_ref, middle_ref, side_ref, core_ref, scr, scr_m):
-    even = lax.axis_index("pol") % 2 == 0
+def middle_kernel(t0_ref, own_ref, middle_ref, scr_m):
     deep = [t0_ref[i] for i in range(6)] + [own_ref[37 + i] for i in range(6)]
     wide = [own_ref[i] for i in range(37)]
-    side_ref[...] = fill_slab_p(scr, deep, wide, even)
-    core_ref[...] = fill_slab_p(scr, deep, wide, jnp.logical_not(even))
     scr_m[pl.ds(M_ROWS - 8, 8), :] = jnp.zeros((8, scr_m.shape[1]), F32)
     for f, value in enumerate(deep):
         scr_m[pl.ds(4 * f, 4), :] = value[2:6]
     for f, value in enumerate(wide):
         scr_m[pl.ds(48 + 6 * f, 6), :] = value[1:7]
     middle_ref[...] = scr_m[...].astype(BF16)
+
+
+def pack_kernel(t0_ref, own_ref, side_ref, core_ref, scr):
+    even = lax.axis_index("pol") % 2 == 0
+    deep = [t0_ref[i] for i in range(6)] + [own_ref[37 + i] for i in range(6)]
+    wide = [own_ref[i] for i in range(37)]
+    side_ref[...] = fill_slab_p(scr, deep, wide, even)
+    core_ref[...] = fill_slab_p(scr, deep, wide, jnp.logical_not(even))
 
 
 def depth_next(x):
@@ -446,8 +451,10 @@
 
 
 def finish_kernel(inverse_root, gram_ref, t_ref, update_ref, estimates_ref):
-    gathered = gram_ref[...]
-    sums = jnp.sum(gathered, axis=0)
+    parts = [gram_ref[i] for i in range(gram_ref.shape[0])]
+    while len(parts) > 1:
+        parts = [a + b for a, b in zip(parts[0::2], parts[1::2])] + parts[len(parts) // 2 * 2 :]
+    sums = parts[0]
     lanes = lax.broadcasted_iota(jnp.int32, sums.shape, 1)
     gram = {}
     for k, pair in enumerate(PAIRS):
@@ -496,13 +503,19 @@
     )(*map(in_hbm, (plasma, rhs, blocks, res)))
     edge = ends[:Q_ROWS]
     ends = lax.ppermute(ends, AXES, across)
-    slabs = (M_ROWS, P_ROWS, P_ROWS)
-    middle, side, core_side = pl.pallas_call(
+    middle = pl.pallas_call(
+        middle_kernel,
+        out_shape=vmem_array((M_ROWS, width), BF16),
+        in_specs=[vmem] * 2,
+        out_specs=vmem,
+        scratch_shapes=[pltpu.VMEM((M_ROWS, width), F32)],
+    )(in_vmem(t0), in_vmem(own))
+    side, core_side = pl.pallas_call(
         pack_kernel,
-        out_shape=tuple(vmem_array((size, width), BF16) for size in slabs),
+        out_shape=(vmem_array((P_ROWS, width), BF16),) * 2,
         in_specs=[vmem] * 2,
-        out_specs=(vmem,) * 3,
-        scratch_shapes=[pltpu.VMEM((P_ROWS, width), F32), pltpu.VMEM((M_ROWS, width), F32)],
+        out_specs=(vmem,) * 2,
+        scratch_shapes=[pltpu.VMEM((P_ROWS, width), F32)],
     )(in_vmem(t0), in_vmem(own))
     middle = lax.ppermute(middle, AXES, across)
     outer_p = lax.ppermute(side, AXES, outer)

time: 26.6 us -> 26.4 us (level)
  no operation moved by 1% of the time
where the time goes in v9:
time: 26.4 us; the launch traced here: 26.2 us
  blocking collectives  11 us (42%)
  starting transfers between devices  7.87 us (30%)
  Pallas kernels  3.58 us (14%)
  waiting for transfers between devices  3.07 us (12%)
  between operations  0.67 us (3%)
    all_to_all x1, blocking collectives, two_planes(): gram = lax.all_to_all(gram, AXES, 0, 0, tiled=True)  11 us
    ppermute x1, starting transfers between devices, two_planes(): ends = lax.ppermute(ends, AXES, across)  3 us
    ppermute x1, waiting for transfers between devices, two_planes(): middle = lax.ppermute(middle, AXES, across)  2.86 us
    ppermute x1, starting transfers between devices, two_planes(): core_p = lax.ppermute(core_side, AXES, core)  1.62 us
    ppermute x1, starting transfers between devices, two_planes(): outer_q = lax.ppermute(edge, AXES, corner)  1.48 us
    pallas_call x1, Pallas kernels, two_planes(): pl.pallas_call(first_kernel, out_shape=(vmem_array((6, rows, width), F32)...  1.19 us
    ppermute x1, starting transfers between devices, two_planes(): core_q = lax.ppermute(ends[Q_ROWS:], AXES, core)  1.07 us
    pallas_call x1, Pallas kernels, two_planes(): pl.pallas_call(krylov_kernel, out_shape=(vmem_array((count, 1, 128), F32)...  0.92 us
  transfers between devices with their start and end apart: 6, of which 2 were waited for; matrix products, arithmetic and copies ran while one was open for 0% of the time, Pallas kernels for 2%

profile of v9, /device:TPU:0, one launch (start us, length us, event | category | flops | bytes accessed | tf_op | source)
XLA Modules:
  0.0 26.2 jit_solution(10863410199235229100)
XLA Ops:
  0.6 1.2 %shard_map.59 = (f32[6,8,256]{2,1,0:T(8,128)S(1)}, f32[49,8,256]{2,1,0:T(8,128)S(1)}, bf16[128,256]{1,0:T(8,128)(2,1)S(1)}) custom-call(f32[6,8,256]{2,1,0:T(8,128)} %bitcast.7, f32[6,8,256]{2,1,0:T(8,128)} %bitcast.8, f32[6,6,8,256]{3,2,1,0:T(8,128)} %bitcast.6, f32[1,8,256]{2,1,0:T(8,128)} %res_hbm.1), custom_call_target="tpu_custom_call" | custom-call | tf_op jit(solution)/shard_map/pallas_call | solution.py:493
  1.8 3.0 %collective-permute-start.3 = (bf16[128,256]{1,0:T(8,128)(2,1)S(1)}, bf16[128,256]{1,0:T(8,128)(2,1)S(1)}, u32[]{:S(2)}, u32[]{:S(2)}) collective-permute-start(bf16[128,256]{1,0:T(8,128)(2,1)S(1)} %get-tuple-element.19), channel_id=1, source_target_pairs={{0,16},{1,17},{2,18},{3,19},{4,20},{5,21},{6,22},{7,23},{8,24},{9,... | collective-permute-start | bytes 196616 | tf_op jit(solution)/shard_map/ppermute | solution.py:505
  4.8 0.1 shard_map.60
  4.9 0.1 collective-permute-start
  5.0 1.6 %collective-permute-start.1 = (bf16[128,256]{1,0:T(8,128)(2,1)S(1)}, bf16[128,256]{1,0:T(8,128)(2,1)S(1)}, u32[]{:S(2)}, u32[]{:S(2)}) collective-permute-start(bf16[128,256]{1,0:T(8,128)(2,1)S(1)} %get-tuple-element.16), channel_id=1, source_target_pairs={{0,1},{1,0},{2,3},{3,2},{4,5},{5,4},{6,7},{7,6},{8,9},{9,8},{10,11... | collective-permute-start | bytes 196616 | tf_op jit(solution)/shard_map/ppermute | solution.py:522
  6.6 0.1 shard_map.62
  6.7 0.6 %collective-permute-start.2 = (bf16[272,256]{1,0:T(8,128)(2,1)S(1)}, bf16[272,256]{1,0:T(8,128)(2,1)S(1)}, u32[]{:S(2)}, u32[]{:S(2)}) collective-permute-start(bf16[272,256]{1,0:T(8,128)(2,1)S(1)} %shard_map.62), channel_id=1, source_target_pairs={{0,16},{1,17},{2,18},{3,19},{4,20},{5,21},{6,22},{7,23},{8,24},{9,... | collective-permute-start | bytes 417800 | tf_op jit(solution)/shard_map/ppermute | solution.py:520
  7.3 1.5 %collective-permute-start.4 = (bf16[64,256]{1,0:T(8,128)(2,1)S(1)}, bf16[64,256]{1,0:T(8,128)(2,1)S(1)}, u32[]{:S(2)}, u32[]{:S(2)}) collective-permute-start(bf16[64,256]{1,0:T(8,128)(2,1)S(1)} %slice.6), channel_id=1, source_target_pairs={{0,16},{1,18},{2,17},{3,20},{4,19},{5,22},{6,21},{7,24},{8,23},{9,... | collective-permute-start | bytes 98312 | tf_op jit(solution)/shard_map/ppermute | solution.py:523
  8.8 0.0 collective-permute-done.3.ends_ref
  8.8 1.1 %collective-permute-start.5 = (bf16[64,256]{1,0:T(8,128)(2,1)S(1)}, bf16[64,256]{1,0:T(8,128)(2,1)S(1)}, u32[]{:S(2)}, u32[]{:S(2)}) collective-permute-start(bf16[64,256]{1,0:T(8,128)(2,1)S(1)} %slice.8), channel_id=1, source_target_pairs={{0,1},{1,0},{2,3},{3,2},{4,5},{5,4},{6,7},{7,6},{8,9},{9,8},{10,11... | collective-permute-start | bytes 98312 | tf_op jit(solution)/shard_map/ppermute | solution.py:524
  9.9 0.0 collective-permute-done.outer_ref
  9.9 0.0 collective-permute-done.1.core_ref
  9.9 0.3 %shard_map.61 = (f32[58,16,256]{2,1,0:T(8,128)S(1)}, f32[6,16,256]{2,1,0:T(8,128)S(1)}) custom-call(f32[49,8,256]{2,1,0:T(8,128)S(1)} %get-tuple-element.13.own_ref, f32[6,8,256]{2,1,0:T(8,128)S(1)} %get-tuple-element.14.t0_ref, bf16[128,256]{1,0:T(8,128)(2,1)S(1)} %collective-permute-done.outer_ref, bf16[128,256]{1,0:T(8,128)(2,1)S(1)} %collective-permute-done.1.core_ref), custom_call_target="tpu_custom_call" | custom-call | flops 1000000000 | bytes 1000000 | tf_op jit(solution)/shard_map/pallas_call | solution.py:533
  10.2 2.9 %collective-permute-done.2.middle_ref = bf16[272,256]{1,0:T(8,128)(2,1)S(1)} collective-permute-done((bf16[272,256]{1,0:T(8,128)(2,1)S(1)}, bf16[272,256]{1,0:T(8,128)(2,1)S(1)}, u32[]{:S(2)}, u32[]{:S(2)}) %collective-permute-start.2) | collective-permute-done | bytes 139296 | tf_op jit(solution)/shard_map/ppermute | solution.py:520
  13.0 0.1 shard_map.63.other_ref
  13.2 0.2 collective-permute-done.4.outer_ref
  13.4 0.0 collective-permute-done.5.core_ref
  13.4 0.9 %shard_map.64 = (f32[32,1,128]{2,1,0:T(1,128)S(1)}, f32[18,8,256]{2,1,0:T(8,128)S(1)}) custom-call(f32[49,8,256]{2,1,0:T(8,128)S(1)} %get-tuple-element.13.own_ref, f32[58,16,256]{2,1,0:T(8,128)S(1)} %get-tuple-element.17.plane_ref, f32[6,16,256]{2,1,0:T(8,128)S(1)} %get-tuple-element.18.image_ref, f32[49,8,256]{2,1,0:T(8,128)S(1)} %shard_map.63.other_ref, ...), custom_call_target="tpu_custom_call" | custom-call | tf_op jit(solution)/shard_map/pallas_call | solution.py:541
  14.3 11.0 %all_to_all.5.gram_ref = f32[32,1,128]{2,1,0:T(1,128)S(1)} all-to-all(f32[32,1,128]{2,1,0:T(1,128)S(1)} %get-tuple-element.20), channel_id=1, replica_groups=mesh['tor'=2,'pol'=16] {'tor','pol'}, dimensions={0} | all-to-all | bytes 32768 | tf_op jit(solution)/shard_map/all_to_all | solution.py:548
  25.3 0.9 %shard_map.65 = (f32[6,8,256]{2,1,0:T(8,128)}, f32[3]{0:T(128)}) custom-call(f32[32,1,128]{2,1,0:T(1,128)S(1)} %all_to_all.5.gram_ref, f32[18,8,256]{2,1,0:T(8,128)S(1)} %get-tuple-element.21.t_ref), custom_call_target="tpu_custom_call" | custom-call | tf_op jit(solution)/shard_map/pallas_call | solution.py:550
  (2 shorter events, 0.0 us)
Async XLA Ops:
  1.8 7.0 %collective-permute-start.3 = (bf16[128,256]{1,0:T(8,128)(2,1)S(1)}, bf16[128,256]{1,0:T(8,128)(2,1)S(1)}, u32[]{:S(2)}, u32[]{:S(2)}) collective-permute-start(bf16[128,256]{1,0:T(8,128)(2,1)S(1)} %get-tuple-element.19), channel_id=1, source_target_pairs={{0,16},{1,17},{2,18},{3,19},{4,20},{5,21},{6,22},{7,23},{8,24},{9,... | collective-permute-start | bytes 196616 | tf_op jit(solution)/shard_map/ppermute | solution.py:505
  4.9 4.9 %collective-permute-start = (bf16[128,256]{1,0:T(8,128)(2,1)S(1)}, bf16[128,256]{1,0:T(8,128)(2,1)S(1)}, u32[]{:S(2)}, u32[]{:S(2)}) collective-permute-start(bf16[128,256]{1,0:T(8,128)(2,1)S(1)} %get-tuple-element.15), channel_id=1, source_target_pairs={{0,16},{1,2},{2,1},{3,4},{4,3},{5,6},{6,5},{7,8},{8,7},{9,10},{10,... | collective-permute-start | bytes 196616 | tf_op jit(solution)/shard_map/ppermute | solution.py:521
  5.0 4.9 %collective-permute-start.1 = (bf16[128,256]{1,0:T(8,128)(2,1)S(1)}, bf16[128,256]{1,0:T(8,128)(2,1)S(1)}, u32[]{:S(2)}, u32[]{:S(2)}) collective-permute-start(bf16[128,256]{1,0:T(8,128)(2,1)S(1)} %get-tuple-element.16), channel_id=1, source_target_pairs={{0,1},{1,0},{2,3},{3,2},{4,5},{5,4},{6,7},{7,6},{8,9},{9,8},{10,11... | collective-permute-start | bytes 196616 | tf_op jit(solution)/shard_map/ppermute | solution.py:522
  6.7 6.3 %collective-permute-start.2 = (bf16[272,256]{1,0:T(8,128)(2,1)S(1)}, bf16[272,256]{1,0:T(8,128)(2,1)S(1)}, u32[]{:S(2)}, u32[]{:S(2)}) collective-permute-start(bf16[272,256]{1,0:T(8,128)(2,1)S(1)} %shard_map.62), channel_id=1, source_target_pairs={{0,16},{1,17},{2,18},{3,19},{4,20},{5,21},{6,22},{7,23},{8,24},{9,... | collective-permute-start | bytes 417800 | tf_op jit(solution)/shard_map/ppermute | solution.py:520
  7.3 6.1 %collective-permute-start.4 = (bf16[64,256]{1,0:T(8,128)(2,1)S(1)}, bf16[64,256]{1,0:T(8,128)(2,1)S(1)}, u32[]{:S(2)}, u32[]{:S(2)}) collective-permute-start(bf16[64,256]{1,0:T(8,128)(2,1)S(1)} %slice.6), channel_id=1, source_target_pairs={{0,16},{1,18},{2,17},{3,20},{4,19},{5,22},{6,21},{7,24},{8,23},{9,... | collective-permute-start | bytes 98312 | tf_op jit(solution)/shard_map/ppermute | solution.py:523
  8.8 4.6 %collective-permute-start.5 = (bf16[64,256]{1,0:T(8,128)(2,1)S(1)}, bf16[64,256]{1,0:T(8,128)(2,1)S(1)}, u32[]{:S(2)}, u32[]{:S(2)}) collective-permute-start(bf16[64,256]{1,0:T(8,128)(2,1)S(1)} %slice.8), channel_id=1, source_target_pairs={{0,1},{1,0},{2,3},{3,2},{4,5},{5,4},{6,7},{7,6},{8,9},{9,8},{10,11... | collective-permute-start | bytes 98312 | tf_op jit(solution)/shard_map/ppermute | solution.py:524

commit v10 on v9

--- a/solution.py
+++ b/solution.py
@@ -179,22 +179,32 @@
     ] + [pltpu.make_async_copy(blocks_hbm.at[a], own_ref.at[pl.ds(6 * a, 6)], sems.at[3 + a]) for a in range(6)]
     for copy in copies:
         copy.start()
+    even = lax.axis_index("pol") % 2 == 0
+    sides = ((scr.at[0], even), (scr.at[1], jnp.logical_not(even)))
+
+    def put(offset, count, value):
+        for slab, first in sides:
+            slab[pl.ds(offset, count), :] = tile_rows(value, count, first)
+
     for copy in copies[:3]:
         copy.wait()
+    for slab, _ in sides:
+        slab[pl.ds(Q_ROWS - 8, 8), :] = jnp.zeros((8, scr.shape[-1]), F32)
+    for i in range(6):
+        put(12 + 2 * i, 2, own_ref[37 + i])
+    put(60, 1, own_ref[36])
     vector = [own_ref[43 + b] for b in range(6)]
-    t0 = []
     for a in range(6):
         copies[3 + a].wait()
         total = own_ref[6 * a] * vector[0]
         for b in range(1, 6):
             total = total + own_ref[6 * a + b] * vector[b]
         t0_ref[a] = total
-        t0.append(total)
-    deep = t0 + [own_ref[37 + i] for i in range(6)]
-    wide = [own_ref[i] for i in range(37)]
-    even = lax.axis_index("pol") % 2 == 0
-    ends_ref[pl.ds(0, Q_ROWS), :] = fill_slab_q(scr, deep, wide, even)
-    ends_ref[pl.ds(Q_ROWS, Q_ROWS), :] = fill_slab_q(scr, deep, wide, jnp.logical_not(even))
+        put(2 * a, 2, total)
+        for b in range(6):
+            put(24 + 6 * a + b, 1, own_ref[6 * a + b])
+    ends_ref[pl.ds(0, Q_ROWS), :] = scr[0].astype(BF16)
+    ends_ref[pl.ds(Q_ROWS, Q_ROWS), :] = scr[1].astype(BF16)
 
 
 def middle_kernel(t0_ref, own_ref, middle_ref, scr_m):
@@ -499,7 +509,7 @@
         ),
         in_specs=[pl.BlockSpec(memory_space=pltpu.HBM)] * 4,
         out_specs=(vmem,) * 3,
-        scratch_shapes=[pltpu.VMEM((Q_ROWS, width), F32), pltpu.SemaphoreType.DMA((9,))],
+        scratch_shapes=[pltpu.VMEM((2, Q_ROWS, width), F32), pltpu.SemaphoreType.DMA((9,))],
     )(*map(in_hbm, (plasma, rhs, blocks, res)))
     edge = ends[:Q_ROWS]
     ends = lax.ppermute(ends, AXES, across)

time: 26.4 us -> 26.3 us (level)
  no operation moved by 1% of the time
where the time goes in v10:
time: 26.3 us; the launch traced here: 26.1 us
  blocking collectives  11 us (42%)
  starting transfers between devices  7.87 us (30%)
  Pallas kernels  3.49 us (13%)
  waiting for transfers between devices  3.07 us (12%)
  between operations  0.67 us (3%)
    all_to_all x1, blocking collectives, two_planes(): gram = lax.all_to_all(gram, AXES, 0, 0, tiled=True)  11 us
    ppermute x1, starting transfers between devices, two_planes(): ends = lax.ppermute(ends, AXES, across)  3 us
    ppermute x1, waiting for transfers between devices, two_planes(): middle = lax.ppermute(middle, AXES, across)  2.86 us
    ppermute x1, starting transfers between devices, two_planes(): core_p = lax.ppermute(core_side, AXES, core)  1.62 us
    ppermute x1, starting transfers between devices, two_planes(): outer_q = lax.ppermute(edge, AXES, corner)  1.48 us
    pallas_call x1, Pallas kernels, two_planes(): pl.pallas_call(first_kernel, out_shape=(vmem_array((6, rows, width), F32)...  1.09 us
    ppermute x1, starting transfers between devices, two_planes(): core_q = lax.ppermute(ends[Q_ROWS:], AXES, core)  1.07 us
    pallas_call x1, Pallas kernels, two_planes(): pl.pallas_call(krylov_kernel, out_shape=(vmem_array((count, 1, 128), F32)...  0.92 us
  transfers between devices with their start and end apart: 6, of which 2 were waited for; matrix products, arithmetic and copies ran while one was open for 0% of the time, Pallas kernels for 2%

profile of v10, /device:TPU:0, one launch (start us, length us, event | category | flops | bytes accessed | tf_op | source)
XLA Modules:
  0.0 26.1 jit_solution(8597761809328350854)
XLA Ops:
  0.6 1.1 %shard_map.59 = (f32[6,8,256]{2,1,0:T(8,128)S(1)}, f32[49,8,256]{2,1,0:T(8,128)S(1)}, bf16[128,256]{1,0:T(8,128)(2,1)S(1)}) custom-call(f32[6,8,256]{2,1,0:T(8,128)} %bitcast.7, f32[6,8,256]{2,1,0:T(8,128)} %bitcast.8, f32[6,6,8,256]{3,2,1,0:T(8,128)} %bitcast.6, f32[1,8,256]{2,1,0:T(8,128)} %res_hbm.1), custom_call_target="tpu_custom_call" | custom-call | tf_op jit(solution)/shard_map/pallas_call | solution.py:503
  1.7 3.0 %collective-permute-start.3 = (bf16[128,256]{1,0:T(8,128)(2,1)S(1)}, bf16[128,256]{1,0:T(8,128)(2,1)S(1)}, u32[]{:S(2)}, u32[]{:S(2)}) collective-permute-start(bf16[128,256]{1,0:T(8,128)(2,1)S(1)} %get-tuple-element.19), channel_id=1, source_target_pairs={{0,16},{1,17},{2,18},{3,19},{4,20},{5,21},{6,22},{7,23},{8,24},{9,... | collective-permute-start | bytes 196616 | tf_op jit(solution)/shard_map/ppermute | solution.py:515
  4.7 0.1 shard_map.60
  4.8 0.1 collective-permute-start
  4.9 1.6 %collective-permute-start.1 = (bf16[128,256]{1,0:T(8,128)(2,1)S(1)}, bf16[128,256]{1,0:T(8,128)(2,1)S(1)}, u32[]{:S(2)}, u32[]{:S(2)}) collective-permute-start(bf16[128,256]{1,0:T(8,128)(2,1)S(1)} %get-tuple-element.16), channel_id=1, source_target_pairs={{0,1},{1,0},{2,3},{3,2},{4,5},{5,4},{6,7},{7,6},{8,9},{9,8},{10,11... | collective-permute-start | bytes 196616 | tf_op jit(solution)/shard_map/ppermute | solution.py:532
  6.5 0.1 shard_map.62
  6.6 0.6 %collective-permute-start.2 = (bf16[272,256]{1,0:T(8,128)(2,1)S(1)}, bf16[272,256]{1,0:T(8,128)(2,1)S(1)}, u32[]{:S(2)}, u32[]{:S(2)}) collective-permute-start(bf16[272,256]{1,0:T(8,128)(2,1)S(1)} %shard_map.62), channel_id=1, source_target_pairs={{0,16},{1,17},{2,18},{3,19},{4,20},{5,21},{6,22},{7,23},{8,24},{9,... | collective-permute-start | bytes 417800 | tf_op jit(solution)/shard_map/ppermute | solution.py:530
  7.2 1.5 %collective-permute-start.4 = (bf16[64,256]{1,0:T(8,128)(2,1)S(1)}, bf16[64,256]{1,0:T(8,128)(2,1)S(1)}, u32[]{:S(2)}, u32[]{:S(2)}) collective-permute-start(bf16[64,256]{1,0:T(8,128)(2,1)S(1)} %slice.6), channel_id=1, source_target_pairs={{0,16},{1,18},{2,17},{3,20},{4,19},{5,22},{6,21},{7,24},{8,23},{9,... | collective-permute-start | bytes 98312 | tf_op jit(solution)/shard_map/ppermute | solution.py:533
  8.7 0.0 collective-permute-done.3.ends_ref
  8.7 1.1 %collective-permute-start.5 = (bf16[64,256]{1,0:T(8,128)(2,1)S(1)}, bf16[64,256]{1,0:T(8,128)(2,1)S(1)}, u32[]{:S(2)}, u32[]{:S(2)}) collective-permute-start(bf16[64,256]{1,0:T(8,128)(2,1)S(1)} %slice.8), channel_id=1, source_target_pairs={{0,1},{1,0},{2,3},{3,2},{4,5},{5,4},{6,7},{7,6},{8,9},{9,8},{10,11... | collective-permute-start | bytes 98312 | tf_op jit(solution)/shard_map/ppermute | solution.py:534
  9.8 0.0 collective-permute-done.outer_ref
  9.8 0.0 collective-permute-done.1.core_ref
  9.8 0.3 %shard_map.61 = (f32[58,16,256]{2,1,0:T(8,128)S(1)}, f32[6,16,256]{2,1,0:T(8,128)S(1)}) custom-call(f32[49,8,256]{2,1,0:T(8,128)S(1)} %get-tuple-element.13.own_ref, f32[6,8,256]{2,1,0:T(8,128)S(1)} %get-tuple-element.14.t0_ref, bf16[128,256]{1,0:T(8,128)(2,1)S(1)} %collective-permute-done.outer_ref, bf16[128,256]{1,0:T(8,128)(2,1)S(1)} %collective-permute-done.1.core_ref), custom_call_target="tpu_custom_call" | custom-call | flops 1000000000 | bytes 1000000 | tf_op jit(solution)/shard_map/pallas_call | solution.py:543
  10.1 2.9 %collective-permute-done.2.middle_ref = bf16[272,256]{1,0:T(8,128)(2,1)S(1)} collective-permute-done((bf16[272,256]{1,0:T(8,128)(2,1)S(1)}, bf16[272,256]{1,0:T(8,128)(2,1)S(1)}, u32[]{:S(2)}, u32[]{:S(2)}) %collective-permute-start.2) | collective-permute-done | bytes 139296 | tf_op jit(solution)/shard_map/ppermute | solution.py:530
  12.9 0.1 shard_map.63.other_ref
  13.1 0.2 collective-permute-done.4.outer_ref
  13.3 0.0 collective-permute-done.5.core_ref
  13.3 0.9 %shard_map.64 = (f32[32,1,128]{2,1,0:T(1,128)S(1)}, f32[18,8,256]{2,1,0:T(8,128)S(1)}) custom-call(f32[49,8,256]{2,1,0:T(8,128)S(1)} %get-tuple-element.13.own_ref, f32[58,16,256]{2,1,0:T(8,128)S(1)} %get-tuple-element.17.plane_ref, f32[6,16,256]{2,1,0:T(8,128)S(1)} %get-tuple-element.18.image_ref, f32[49,8,256]{2,1,0:T(8,128)S(1)} %shard_map.63.other_ref, ...), custom_call_target="tpu_custom_call" | custom-call | tf_op jit(solution)/shard_map/pallas_call | solution.py:551
  14.2 11.0 %all_to_all.5.gram_ref = f32[32,1,128]{2,1,0:T(1,128)S(1)} all-to-all(f32[32,1,128]{2,1,0:T(1,128)S(1)} %get-tuple-element.20), channel_id=1, replica_groups=mesh['tor'=2,'pol'=16] {'tor','pol'}, dimensions={0} | all-to-all | bytes 32768 | tf_op jit(solution)/shard_map/all_to_all | solution.py:558
  25.2 0.9 %shard_map.65 = (f32[6,8,256]{2,1,0:T(8,128)}, f32[3]{0:T(128)}) custom-call(f32[32,1,128]{2,1,0:T(1,128)S(1)} %all_to_all.5.gram_ref, f32[18,8,256]{2,1,0:T(8,128)S(1)} %get-tuple-element.21.t_ref), custom_call_target="tpu_custom_call" | custom-call | tf_op jit(solution)/shard_map/pallas_call | solution.py:560
  (2 shorter events, 0.0 us)
Async XLA Ops:
  1.7 7.0 %collective-permute-start.3 = (bf16[128,256]{1,0:T(8,128)(2,1)S(1)}, bf16[128,256]{1,0:T(8,128)(2,1)S(1)}, u32[]{:S(2)}, u32[]{:S(2)}) collective-permute-start(bf16[128,256]{1,0:T(8,128)(2,1)S(1)} %get-tuple-element.19), channel_id=1, source_target_pairs={{0,16},{1,17},{2,18},{3,19},{4,20},{5,21},{6,22},{7,23},{8,24},{9,... | collective-permute-start | bytes 196616 | tf_op jit(solution)/shard_map/ppermute | solution.py:515
  4.8 4.9 %collective-permute-start = (bf16[128,256]{1,0:T(8,128)(2,1)S(1)}, bf16[128,256]{1,0:T(8,128)(2,1)S(1)}, u32[]{:S(2)}, u32[]{:S(2)}) collective-permute-start(bf16[128,256]{1,0:T(8,128)(2,1)S(1)} %get-tuple-element.15), channel_id=1, source_target_pairs={{0,16},{1,2},{2,1},{3,4},{4,3},{5,6},{6,5},{7,8},{8,7},{9,10},{10,... | collective-permute-start | bytes 196616 | tf_op jit(solution)/shard_map/ppermute | solution.py:531
  4.9 4.9 %collective-permute-start.1 = (bf16[128,256]{1,0:T(8,128)(2,1)S(1)}, bf16[128,256]{1,0:T(8,128)(2,1)S(1)}, u32[]{:S(2)}, u32[]{:S(2)}) collective-permute-start(bf16[128,256]{1,0:T(8,128)(2,1)S(1)} %get-tuple-element.16), channel_id=1, source_target_pairs={{0,1},{1,0},{2,3},{3,2},{4,5},{5,4},{6,7},{7,6},{8,9},{9,8},{10,11... | collective-permute-start | bytes 196616 | tf_op jit(solution)/shard_map/ppermute | solution.py:532
  6.6 6.3 %collective-permute-start.2 = (bf16[272,256]{1,0:T(8,128)(2,1)S(1)}, bf16[272,256]{1,0:T(8,128)(2,1)S(1)}, u32[]{:S(2)}, u32[]{:S(2)}) collective-permute-start(bf16[272,256]{1,0:T(8,128)(2,1)S(1)} %shard_map.62), channel_id=1, source_target_pairs={{0,16},{1,17},{2,18},{3,19},{4,20},{5,21},{6,22},{7,23},{8,24},{9,... | collective-permute-start | bytes 417800 | tf_op jit(solution)/shard_map/ppermute | solution.py:530
  7.2 6.1 %collective-permute-start.4 = (bf16[64,256]{1,0:T(8,128)(2,1)S(1)}, bf16[64,256]{1,0:T(8,128)(2,1)S(1)}, u32[]{:S(2)}, u32[]{:S(2)}) collective-permute-start(bf16[64,256]{1,0:T(8,128)(2,1)S(1)} %slice.6), channel_id=1, source_target_pairs={{0,16},{1,18},{2,17},{3,20},{4,19},{5,22},{6,21},{7,24},{8,23},{9,... | collective-permute-start | bytes 98312 | tf_op jit(solution)/shard_map/ppermute | solution.py:533
  8.7 4.6 %collective-permute-start.5 = (bf16[64,256]{1,0:T(8,128)(2,1)S(1)}, bf16[64,256]{1,0:T(8,128)(2,1)S(1)}, u32[]{:S(2)}, u32[]{:S(2)}) collective-permute-start(bf16[64,256]{1,0:T(8,128)(2,1)S(1)} %slice.8), channel_id=1, source_target_pairs={{0,1},{1,0},{2,3},{3,2},{4,5},{5,4},{6,7},{7,6},{8,9},{9,8},{10,11... | collective-permute-start | bytes 98312 | tf_op jit(solution)/shard_map/ppermute | solution.py:534
